TPU v7x, 128 devices: a whole 4x4x4 slice. The times are simulated.
128 devices in a mesh: rows: 128 (over y, z, x, core).
Axes of the slice: x: 4, y: 4, z: 4, core: 2. Of those that a mesh axis runs over, the one named last changes fastest.
Arguments:
- parent_old: float32 [3, 512, 8192], P(None, 'rows'), may hold values from -3 to 3
- parent_now: float32 [3, 512, 8192], P(None, 'rows'), may hold values from -3 to 3
- child_old: float32 [4, 3, 1024, 4096], P(None, None, 'rows'), may hold values from -3 to 3
- child_now: float32 [4, 3, 1024, 4096], P(None, None, 'rows'), may hold values from -3 to 3
- parent_depth: float32 [512, 8192], P('rows'), may hold values from 0.5 to 2
- child_depth: float32 [4, 1024, 4096], P(None, 'rows'), may hold values from 0.5 to 2
- child_rows: int32 [4], replicated, may hold values from 0 to 384, as said below
- child_cols: int32 [4], replicated, may hold values from 1 to 7679, as said below
- parent_cot_mid: float32 [3, 512, 8192], P(None, 'rows'), may hold values from -6 to 6
- parent_cot_end: float32 [3, 512, 8192], P(None, 'rows'), may hold values from -6 to 6
- child_cot_mid: float32 [4, 3, 1024, 4096], P(None, None, 'rows'), may hold values from -6 to 6
- child_cot_end: float32 [4, 3, 1024, 4096], P(None, None, 'rows'), may hold values from -6 to 6
Outputs:
- parent_end: float32 [3, 512, 8192], P(None, 'rows')
- child_end: float32 [4, 3, 1024, 4096], P(None, None, 'rows')
- parent_grad_old: float32 [3, 512, 8192], P(None, 'rows')
- parent_grad_now: float32 [3, 512, 8192], P(None, 'rows')
- child_grad_old: float32 [4, 3, 1024, 4096], P(None, None, 'rows')
- child_grad_now: float32 [4, 3, 1024, 4096], P(None, None, 'rows')
Inputs may be any that keep to these rules, and one draw needn't show every extreme that they name: Coastal grid k covers the ocean rows child_rows[k] to child_rows[k] + 127, all inside the ocean grid. Coastal grid k covers the ocean columns child_cols[k] to child_cols[k] + 511, which lie, with one more column on each side, in columns k * 2048 to (k + 1) * 2048 - 1.
All inputs are finite; a program needn't handle non-finite values.
Results may differ from a plain program's by a relative error of at most 0.0001.
Values sent between devices are 32-bit elements; how exact they have to be, the bound alone decides.
A program may use at most 128 MiB of HBM per device.

v0:
```python
import jax
import jax.numpy as jnp
from jax import lax
from jax.sharding import PartitionSpec as P

P_ROWS = 4
C_ROWS = 8
C_COLS = 4096
NCHILD = 4
RATIO = 8
STEPS = 2
FOOT_COLS = 512


TIME_STEP = 0.15
GRAVITY = 1.0
FRICTION = 0.05


def extended(shard, sides, width):
    for axis, dim in sides:
        size, length = (lax.axis_size(axis), shard.shape[dim])
        up = [(i, (i + 1) % size) for i in range(size - 1)]
        down = [(j, i) for i, j in up]
        last = lax.slice_in_dim(shard, length - width, length, axis=dim)
        first = lax.slice_in_dim(shard, 0, width, axis=dim)
        before = lax.ppermute(last, axis, up)
        after = lax.ppermute(first, axis, down)
        shard = jnp.concatenate([before, shard, after], axis=dim)
    return shard


def east_west(field):
    return 0.5 * (field[..., 1:-1, 2:] - field[..., 1:-1, :-2])


def north_south(field):
    return 0.5 * (field[..., 2:, 1:-1] - field[..., :-2, 1:-1])


def tendency(padded, bathymetry):
    surface = padded[..., 0, :, :]
    east_flow = padded[..., 1, :, :]
    north_flow = padded[..., 2, :, :]
    east_mid = east_flow[..., 1:-1, 1:-1]
    north_mid = north_flow[..., 1:-1, 1:-1]
    surface_rate = (
        -bathymetry * (east_west(east_flow) + north_south(north_flow))
        - east_west(surface * east_flow)
        - north_south(surface * north_flow)
    )
    east_rate = (
        -(east_mid * east_west(east_flow) + north_mid * north_south(east_flow))
        - GRAVITY * east_west(surface)
        - FRICTION * east_mid
    )
    north_rate = (
        -(east_mid * east_west(north_flow) + north_mid * north_south(north_flow))
        - GRAVITY * north_south(surface)
        - FRICTION * north_mid
    )
    return jnp.stack([surface_rate, east_rate, north_rate], axis=-3)


def strip_rims(block):
    return extended(block, (("rows", 1),), 1)


def pad_parent(parent_now):
    framed = strip_rims(parent_now)
    return jnp.pad(framed, ((0, 0), (0, 0), (1, 1)))


def parent_edges(parent_now, child_cols):
    columns = []
    for nested in range(NCHILD):
        left_edge = lax.dynamic_slice_in_dim(parent_now, child_cols[nested] - 1, 1, 2)[..., 0]
        right_edge = lax.dynamic_slice_in_dim(parent_now, child_cols[nested] + FOOT_COLS, 1, 2)[
            ..., 0
        ]
        columns.append(jnp.stack([left_edge, right_edge], axis=1))
    return jnp.stack(columns)


def child_frame(parent_now, child_now, child_rows, child_cols):
    edge_cells = lax.all_gather(parent_edges(parent_now, child_cols), "rows", axis=3, tiled=True)
    first_row = lax.axis_index("rows") * (C_ROWS // RATIO)
    picked = []
    for nested in range(NCHILD):
        picked.append(
            lax.dynamic_slice_in_dim(
                edge_cells[nested], child_rows[nested] + first_row, C_ROWS // RATIO, 2
            )
        )
    ghosts = jnp.repeat(jnp.stack(picked), RATIO, axis=3)
    ghosts = jnp.pad(ghosts, ((0, 0), (0, 0), (0, 0), (1, 1)))
    merged = child_now.reshape(NCHILD * 3, C_ROWS, C_COLS)
    framed = strip_rims(merged).reshape(NCHILD, 3, C_ROWS + 2, C_COLS)
    return jnp.concatenate([ghosts[:, :, 0, :, None], framed, ghosts[:, :, 1, :, None]], axis=3)


def footprint_rows(child_rows):
    parent_row = lax.axis_index("rows") * P_ROWS + jnp.arange(P_ROWS)
    foot_row = parent_row[None, :] - child_rows[:, None]
    covered = (foot_row >= 0) & (foot_row < lax.axis_size("rows") * (C_ROWS // RATIO))
    return (foot_row, covered)


def restrict(parent_next, child_next, child_rows, child_cols):
    coarse_means = child_next.reshape(NCHILD, 3, C_ROWS // RATIO, RATIO, FOOT_COLS, RATIO).mean(
        axis=(3, 5)
    )
    foot_row, covered = footprint_rows(child_rows)
    shard_rows = lax.all_gather(coarse_means, "rows", axis=2, tiled=True)
    row_count = shard_rows.shape[2]
    chosen = (foot_row[:, :, None] == jnp.arange(row_count)[None, None, :]).astype(jnp.float32)
    placed = jnp.einsum("krj,kcjw->kcrw", chosen, shard_rows, precision=lax.Precision.HIGHEST)
    for nested in range(NCHILD):
        band_cells = lax.dynamic_slice_in_dim(parent_next, child_cols[nested], FOOT_COLS, 2)
        band_cells = jnp.where(covered[nested][None, :, None], placed[nested], band_cells)
        parent_next = lax.dynamic_update_slice_in_dim(
            parent_next, band_cells, child_cols[nested], 2
        )
    return parent_next


def forward_step(states, parent_depth, child_depth, child_rows, child_cols):
    parent_old, parent_now, child_old, child_now = states
    parent_framed = pad_parent(parent_now)
    child_framed = child_frame(parent_now, child_now, child_rows, child_cols)
    parent_next = parent_old + 2.0 * TIME_STEP * tendency(parent_framed, parent_depth)
    child_next = child_old + 2.0 * TIME_STEP * tendency(child_framed, child_depth)
    parent_next = restrict(parent_next, child_next, child_rows, child_cols)
    return ((parent_now, parent_next, child_now, child_next), (parent_framed, child_framed))


def rims_back(frame_cot):
    lead_shape = frame_cot.shape[:-2]
    width = frame_cot.shape[-1] - 2
    outer = jnp.stack([frame_cot[..., 0, 1:-1], frame_cot[..., -1, 1:-1]], axis=-2)
    received = strip_rims(outer.reshape(-1, 2, width)).reshape(lead_shape + (4, width))
    inner = frame_cot[..., 1:-1, 1:-1]
    inner = inner.at[..., 0, :].add(received[..., 0, :])
    return inner.at[..., -1, :].add(received[..., 3, :])


def adjoint_step(frame_pair, cots, parent_depth, child_depth, child_rows, child_cols):
    parent_framed, child_framed = frame_pair
    parent_cot_now, parent_cot_next, child_cot_now, child_cot_next = cots
    foot_row, covered = footprint_rows(child_rows)
    bands = []
    for nested in range(NCHILD):
        band_cells = lax.dynamic_slice_in_dim(parent_cot_next, child_cols[nested], FOOT_COLS, 2)
        bands.append(band_cells)
        cleared = jnp.where(covered[nested][None, :, None], 0.0, band_cells)
        parent_cot_next = lax.dynamic_update_slice_in_dim(
            parent_cot_next, cleared, child_cols[nested], 2
        )
    band_cot = jnp.stack(bands)
    whole_bands = lax.all_gather(band_cot, "rows", axis=2, tiled=True)
    first_row = lax.axis_index("rows") * (C_ROWS // RATIO)
    mean_cot = jnp.stack(
        [
            lax.dynamic_slice_in_dim(
                whole_bands[nested], child_rows[nested] + first_row, C_ROWS // RATIO, 1
            )
            for nested in range(NCHILD)
        ]
    )
    spread = jnp.repeat(jnp.repeat(mean_cot, RATIO, axis=2), RATIO, axis=3)
    child_total = child_cot_next + spread * (1.0 / (RATIO * RATIO))
    scale_factor = 2.0 * TIME_STEP
    child_pullback = jax.vjp(lambda framed: tendency(framed, child_depth), child_framed)[1]
    child_frame_cot = child_pullback(scale_factor * child_total)[0]
    child_now_cot = child_cot_now + rims_back(child_frame_cot)
    edge_cot = jnp.stack([child_frame_cot[..., 1:-1, 0], child_frame_cot[..., 1:-1, -1]], axis=2)
    edge_coarse = edge_cot.reshape(NCHILD, 3, 2, C_ROWS // RATIO, RATIO).sum(axis=4)
    child_start = lax.axis_index("rows") * (C_ROWS // RATIO)
    source_rows = child_rows[:, None] + child_start + jnp.arange(C_ROWS // RATIO)[None, :]
    parent_row = jnp.arange(lax.axis_size("rows") * P_ROWS)
    chosen = (parent_row[None, :, None] == source_rows[:, None, :]).astype(jnp.float32)
    edge_back = lax.psum_scatter(
        jnp.einsum("kij,kcsj->ikcs", chosen, edge_coarse, precision=lax.Precision.HIGHEST),
        "rows",
        scatter_dimension=0,
        tiled=True,
    )
    parent_pullback = jax.vjp(lambda framed: tendency(framed, parent_depth), parent_framed)[1]
    parent_frame_cot = parent_pullback(scale_factor * parent_cot_next)[0]
    parent_now_cot = parent_cot_now + rims_back(parent_frame_cot)
    for nested in range(NCHILD):
        west_cells = lax.dynamic_slice_in_dim(parent_now_cot, child_cols[nested] - 1, 1, 2)
        west_cells = west_cells + jnp.transpose(edge_back[:, nested, :, 0])[..., None]
        parent_now_cot = lax.dynamic_update_slice_in_dim(
            parent_now_cot, west_cells, child_cols[nested] - 1, 2
        )
        east_cells = lax.dynamic_slice_in_dim(parent_now_cot, child_cols[nested] + FOOT_COLS, 1, 2)
        east_cells = east_cells + jnp.transpose(edge_back[:, nested, :, 1])[..., None]
        parent_now_cot = lax.dynamic_update_slice_in_dim(
            parent_now_cot, east_cells, child_cols[nested] + FOOT_COLS, 2
        )
    return (parent_cot_next, parent_now_cot, child_total, child_now_cot)


def shards(
    parent_old,
    parent_now,
    child_old,
    child_now,
    parent_depth,
    child_depth,
    child_rows,
    child_cols,
    parent_cot_mid,
    parent_cot_end,
    child_cot_mid,
    child_cot_end,
):
    states = (parent_old, parent_now, child_old, child_now)
    history = []
    frames = []
    for step_index in range(STEPS):
        history.append(states)
        states, frame_pair = forward_step(states, parent_depth, child_depth, child_rows, child_cols)
        frames.append(frame_pair)
    cots = (parent_cot_mid, parent_cot_end, child_cot_mid, child_cot_end)
    for step_index in reversed(range(STEPS)):
        frame_pair = frames[step_index]
        cots = adjoint_step(frame_pair, cots, parent_depth, child_depth, child_rows, child_cols)
    return (states[1], states[3], cots[0], cots[1], cots[2], cots[3])


def solution(mesh):
    return jax.shard_map(
        shards,
        mesh=mesh,
        in_specs=(
            P(None, "rows", None),
            P(None, "rows", None),
            P(None, None, "rows", None),
            P(None, None, "rows", None),
            P("rows", None),
            P(None, "rows", None),
            P(),
            P(),
            P(None, "rows", None),
            P(None, "rows", None),
            P(None, None, "rows", None),
            P(None, None, "rows", None),
        ),
        out_specs=(
            P(None, "rows", None),
            P(None, None, "rows", None),
            P(None, "rows", None),
            P(None, "rows", None),
            P(None, None, "rows", None),
            P(None, None, "rows", None),
        ),
        check_vma=False,
    )
```

profile of v0, /device:TPU:0, one launch (start us, length us, event | category | flops | bytes accessed | tf_op | source)
XLA Modules:
  0.0 743.4 jit_solution(14121882828060721766)
XLA Ops:
  9.1 2.0 fusion.210
  11.0 1.9 collective-permute-start
  14.2 3.0 fusion.205
  17.2 4.9 collective-permute-start.2
  43.6 45.2 %all_gather.18 = f32[4,3,2,512]{0,2,1,3:T(2,128)S(1)} all-gather(f32[4,3,2,4]{0,2,1,3:T(2,128)S(1)} %copy.247), channel_id=1, replica_groups=mesh['rows'=128] {'rows'}, dimensions={3}, use_global_device_ids=true | all-gather | bytes 49536 | tf_op jit(solution)/shard_map/all_gather | solution.py:86
  88.7 6.7 fusion.206
  108.1 3.7 concatenate.60
  117.6 3.7 reduce_sum.43
  121.3 2.8 reduce_sum.52
  124.8 2.7 fusion.89
  128.3 2.3 collective-permute-start.6
  134.5 2.2 pad_maximum_fusion.1
  136.7 52.6 %all-gather.11.cloned.1.call-done = f32[4,3,65536]{2,0,1:T(4,128)} async-done(((f32[4,3,512]{2,0,1:T(4,128)}), f32[4,3,65536]{2,0,1:T(4,128)}) %all-gather.11.cloned.1.call-update) | async-done | bytes 3145744 | tf_op jit(solution)/shard_map/all_gather | solution.py:114
  189.3 5.3 reshape.452
  194.5 3.0 fusion.8
  198.4 1.9 dynamic_update_slice.96
  218.2 1.9 fusion.209
  220.1 2.8 collective-permute-start.4
  224.2 39.7 %all_gather.20 = f32[4,3,2,512]{0,2,1,3:T(2,128)S(1)} all-gather(f32[4,3,2,4]{0,2,1,3:T(2,128)S(1)} %copy.260), channel_id=1, replica_groups=mesh['rows'=128] {'rows'}, dimensions={3}, use_global_device_ids=true | all-gather | bytes 49536 | tf_op jit(solution)/shard_map/all_gather | solution.py:86
  263.9 5.4 fusion.204
  270.0 4.8 concatenate.65
  274.7 2.4 slice_bitcast_fusion.2
  277.3 2.6 fusion.27
  286.6 2.5 collective-permute-start.8
  292.6 2.8 scatter-add.26
  297.3 2.8 scatter-add.29
  300.1 2.0 add.655
  302.1 27.1 %fusion.202 = (f32[1,3,512,512]{3,0,2,1:T(1,128)S(1)}, f32[1,3,512,512]{3,0,2,1:T(1,128)S(1)}, f32[1,3,512,512]{3,0,2,1:T(1,128)S(1)}, f32[1,3,512,512]{3,0,2,1:T(1,128)S(1)}) fusion(f32[4,3,512,512]{3,0,2,1:T(4,128)} %all-gather.7.cloned.1.call-done), kind=kLoop, calls=%fused_computation.474 | loop fusion | bytes 25165824 | tf_op jit(solution)/shard_map/slice | solution.py:165
  329.3 2.1 broadcast_in_dim.209
  331.4 3.9 mul.663
  343.8 3.4 add_bitcast_fusion.5
  350.0 73.7 %all-reduce.104 = f32[512,4,3,2]{1,3,2,0:T(2,128)} all-reduce(f32[512,4,3,2]{1,3,2,0:T(2,128)} %multiply_bitcast_fusion.1), channel_id=4, replica_groups=mesh['rows'=128] {'rows'}, use_global_device_ids=true, to_apply=%region_5.6.clone | all-reduce | flops 12288 | bytes 98304
  423.7 1.9 dynamic-slice_reduce_fusion.8
  454.5 1.9 dynamic_update_slice.117
  459.3 1.9 dynamic_update_slice.118
  465.4 3.4 fusion.72
  468.7 2.4 pad_add_fusion.15
  474.1 4.4 collective-permute-start.12
  481.5 2.8 fusion.183
  488.0 3.1 collective-permute-start.10
  496.6 2.8 scatter-add.30
  500.6 2.8 scatter-add.31
  503.5 2.1 add.669
  507.3 4.8 scatter-add.34
  513.8 4.8 scatter-add.35
  518.6 20.2 %all-gather.9.cloned.1.call-done = f32[4,3,512,512]{3,0,2,1:T(4,128)} async-done(((f32[4,3,4,512]{3,0,2,1:T(4,128)}), f32[4,3,512,512]{3,0,2,1:T(4,128)}) %all-gather.9.cloned.1.call-update) | async-done | bytes 12582928 | tf_op jit(solution)/shard_map/all_gather | solution.py:160
  538.8 27.1 %fusion.201 = (f32[1,3,512,512]{3,0,2,1:T(1,128)S(1)}, f32[1,3,512,512]{3,0,2,1:T(1,128)S(1)}, f32[1,3,512,512]{3,0,2,1:T(1,128)S(1)}, f32[1,3,512,512]{3,0,2,1:T(1,128)S(1)}) fusion(f32[4,3,512,512]{3,0,2,1:T(4,128)} %all-gather.9.cloned.1.call-done), kind=kLoop, calls=%fused_computation.473 | loop fusion | bytes 25165824 | tf_op jit(solution)/shard_map/slice | solution.py:165
  566.0 2.1 broadcast_in_dim.225
  568.1 3.4 mul.714
  571.5 2.2 broadcast_multiply_fusion
  580.9 2.0 add_bitcast_fusion.2
  588.8 3.3 reduce_sum.54
  592.1 2.9 reduce_sum.55
  595.6 2.5 fusion.207
  599.4 3.0 collective-permute-start.14
  607.0 73.1 %all-reduce.105 = f32[512,4,3,2]{1,3,2,0:T(2,128)} all-reduce(f32[512,4,3,2]{1,3,2,0:T(2,128)} %multiply_bitcast_fusion), channel_id=5, replica_groups=mesh['rows'=128] {'rows'}, use_global_device_ids=true, to_apply=%region_7.8.clone | all-reduce | flops 12288 | bytes 98304
  700.6 2.7 copy.311
  703.9 2.1 add_add_fusion
  706.1 4.8 scatter-add.36
  712.5 4.8 scatter-add.39
  717.3 2.1 fusion.6
  720.7 3.9 reshape.453
  729.3 1.9 dynamic_update_slice.101
  732.0 1.9 dynamic_update_slice.102
  (395 shorter events, 179.8 us)
Async XLA Ops:
  7.2 35.2 %copy-start.41 = (f32[3,4,8192]{2,1,0:T(4,128)S(1)}, f32[3,4,8192]{2,1,0:T(4,128)}, u32[]{:S(2)}) copy-start(f32[3,4,8192]{2,1,0:T(4,128)} %param.29) | copy-start | bytes 1179652
  7.2 16.2 %copy-start.61 = (s32[4]{0:T(128)S(1)}, s32[4]{0:T(128)}, u32[]{:S(2)}) copy-start(s32[4]{0:T(128)} %param.34) | copy-start | bytes 52
  7.2 16.4 %copy-start.70 = (s32[4]{0:T(128)S(1)}, s32[4]{0:T(128)}, u32[]{:S(2)}) copy-start(s32[4]{0:T(128)} %param.35) | copy-start | bytes 52
  7.2 182.1 %all-gather.11.cloned.1.call-start = ((), (), s32[]{:S(2)}) async-start(), calls=%async_computation.2 | async-start | bytes 3170304 | tf_op jit(solution)/shard_map/all_gather | solution.py:114
  11.0 90.0 %collective-permute-start = (f32[3,1,8192]{2,1,0:T(1,128)}, f32[3,1,8192]{2,1,0:T(1,128)}, u32[]{:S(2)}, u32[]{:S(2)}) collective-permute-start(f32[3,1,8192]{2,1,0:T(1,128)} %get-tuple-element.359), channel_id=1, source_target_pairs={{0,1},{1,2},{2,3},{3,4},{4,5},{5,6},{6,7},{7,8},{8,9},{9,10},{10,1... | collective-permute-start | bytes 294920 | tf_op jit(solution)/shard_map/ppermute | solution.py:27
  13.0 88.1 %collective-permute-start.1 = (f32[3,1,8192]{2,1,0:T(1,128)}, f32[3,1,8192]{2,1,0:T(1,128)}, u32[]{:S(2)}, u32[]{:S(2)}) collective-permute-start(f32[3,1,8192]{2,1,0:T(1,128)} %get-tuple-element.360), channel_id=1, source_target_pairs={{1,0},{2,1},{3,2},{4,3},{5,4},{6,5},{7,6},{8,7},{9,8},{10,9},{11,1... | collective-permute-start | bytes 294920 | tf_op jit(solution)/shard_map/ppermute | solution.py:28
  17.2 87.5 %collective-permute-start.2 = (f32[12,1,4096]{2,1,0:T(1,128)}, f32[12,1,4096]{2,1,0:T(1,128)}, u32[]{:S(2)}, u32[]{:S(2)}) collective-permute-start(f32[12,1,4096]{2,1,0:T(1,128)} %get-tuple-element.295), channel_id=1, source_target_pairs={{0,1},{1,2},{2,3},{3,4},{4,5},{5,6},{6,7},{7,8},{8,9},{9,10},{10,1... | collective-permute-start | bytes 589832 | tf_op jit(solution)/shard_map/ppermute | solution.py:27
  22.1 82.6 %collective-permute-start.3 = (f32[12,1,4096]{2,1,0:T(1,128)}, f32[12,1,4096]{2,1,0:T(1,128)}, u32[]{:S(2)}, u32[]{:S(2)}) collective-permute-start(f32[12,1,4096]{2,1,0:T(1,128)} %get-tuple-element.296), channel_id=1, source_target_pairs={{1,0},{2,1},{3,2},{4,3},{5,4},{6,5},{7,6},{8,7},{9,8},{10,9},{11,1... | collective-permute-start | bytes 589832 | tf_op jit(solution)/shard_map/ppermute | solution.py:28
  103.8 23.8 %copy-start.27 = (f32[6,8194]{1,0:T(8,128)}, f32[6,8194]{1,0:T(8,128)S(1)}, u32[]{:S(2)}) copy-start(f32[6,8194]{1,0:T(8,128)S(1)} %get-tuple-element.322) | copy-start | bytes 589972
  124.7 177.4 %all-gather.7.cloned.1.call-start = ((), (), s32[]{:S(2)}) async-start(), calls=%async_computation | async-start | bytes 12681216 | tf_op jit(solution)/shard_map/all_gather | solution.py:160
  124.8 2.8 copy-start.28
  124.8 2.8 copy-start.49
  124.8 2.8 copy-start.52
  124.8 2.8 copy-start.53
  124.8 3.3 copy-start.31
  127.5 4.8 copy-start.58
  128.3 4.9 collective-permute-start.6
  130.7 3.8 collective-permute-start.7
  194.5 3.0 copy-start.68
  194.5 7.7 %copy-start.66 = (pred[4]{0:T(512)(128)(4,1)S(1)}, pred[4]{0:T(512)(128)(4,1)}, u32[]{:S(2)}) copy-start(pred[4]{0:T(512)(128)(4,1)} %get-tuple-element.372) | copy-start | bytes 16
  194.5 12.3 %copy-start.64 = (pred[4]{0:T(512)(128)(4,1)S(1)}, pred[4]{0:T(512)(128)(4,1)}, u32[]{:S(2)}) copy-start(pred[4]{0:T(512)(128)(4,1)} %get-tuple-element.371) | copy-start | bytes 16
  194.5 16.9 %copy-start.62 = (pred[4]{0:T(512)(128)(4,1)S(1)}, pred[4]{0:T(512)(128)(4,1)}, u32[]{:S(2)}) copy-start(pred[4]{0:T(512)(128)(4,1)} %get-tuple-element.370) | copy-start | bytes 16
  218.2 320.6 %all-gather.9.cloned.1.call-start = ((), (), s32[]{:S(2)}) async-start(), calls=%async_computation.1 | async-start | bytes 12681216 | tf_op jit(solution)/shard_map/all_gather | solution.py:160
  220.1 59.7 %collective-permute-start.4 = (f32[3,1,8192]{2,1,0:T(1,128)}, f32[3,1,8192]{2,1,0:T(1,128)}, u32[]{:S(2)}, u32[]{:S(2)}) collective-permute-start(f32[3,1,8192]{2,1,0:T(1,128)} %get-tuple-element.357), channel_id=1, source_target_pairs={{0,1},{1,2},{2,3},{3,4},{4,5},{5,6},{6,7},{7,8},{8,9},{9,10},{10,1... | collective-permute-start | bytes 294920 | tf_op jit(solution)/shard_map/ppermute | solution.py:27
  222.9 56.9 %collective-permute-start.5 = (f32[3,1,8192]{2,1,0:T(1,128)S(1)}, f32[3,1,8192]{2,1,0:T(1,128)}, u32[]{:S(2)}, u32[]{:S(2)}) collective-permute-start(f32[3,1,8192]{2,1,0:T(1,128)S(1)} %get-tuple-element.358), channel_id=1, source_target_pairs={{1,0},{2,1},{3,2},{4,3},{5,4},{6,5},{7,6},{8,7},{9,8},{10,9},{11,1... | collective-permute-start | bytes 294920 | tf_op jit(solution)/shard_map/ppermute | solution.py:28
  274.7 2.4 copy-start.39
  277.1 2.7 copy-start
  277.1 2.7 copy-start.8
  277.2 2.6 copy-start.40
  279.8 2.5 copy-start.50
  286.6 5.1 collective-permute-start.8
  289.2 6.3 collective-permute-start.9
  342.0 5.2 copy-start.11
  343.8 3.4 copy-start.15
  464.9 255.8 %all-gather.13.cloned.1.call-start = ((), (), s32[]{:S(2)}) async-start(), calls=%async_computation.3 | async-start | bytes 3170304 | tf_op jit(solution)/shard_map/all_gather | solution.py:114
  465.3 3.4 copy-start.12
  471.2 7.3 copy-start.60
  472.8 39.3 %collective-permute-start.13 = (f32[12,1,4096]{2,1,0:T(1,128)}, f32[12,1,4096]{2,1,0:T(1,128)}, u32[]{:S(2)}, u32[]{:S(2)}) collective-permute-start(f32[12,1,4096]{2,1,0:T(1,128)} %get-tuple-element.339), channel_id=1, source_target_pairs={{1,0},{2,1},{3,2},{4,3},{5,4},{6,5},{7,6},{8,7},{9,8},{10,9},{11,1... | collective-permute-start | bytes 589832 | tf_op jit(solution)/shard_map/ppermute | solution.py:28
  474.1 31.5 %collective-permute-start.12 = (f32[12,1,4096]{2,1,0:T(1,128)}, f32[12,1,4096]{2,1,0:T(1,128)}, u32[]{:S(2)}, u32[]{:S(2)}) collective-permute-start(f32[12,1,4096]{2,1,0:T(1,128)} %get-tuple-element.340), channel_id=1, source_target_pairs={{0,1},{1,2},{2,3},{3,4},{4,5},{5,6},{6,7},{7,8},{8,9},{9,10},{10,1... | collective-permute-start | bytes 589832 | tf_op jit(solution)/shard_map/ppermute | solution.py:27
  481.4 2.8 copy-start.30
  481.4 2.8 copy-start.51
  481.5 2.8 copy-start.54
  481.5 2.8 copy-start.55
  487.0 4.2 copy-start.57
  487.5 3.7 copy-start.42
  487.5 3.7 copy-start.56
  487.5 4.6 copy-start.24
  488.0 4.1 copy-start.13
  488.0 4.1 copy-start.16
  488.0 8.3 %collective-permute-start.10 = (f32[3,1,8192]{2,1,0:T(1,128)S(1)}, f32[3,1,8192]{2,1,0:T(1,128)S(1)}, u32[]{:S(2)}, u32[]{:S(2)}) collective-permute-start(f32[3,1,8192]{2,1,0:T(1,128)S(1)} %get-tuple-element.306), channel_id=1, source_target_pairs={{0,1},{1,2},{2,3},{3,4},{4,5},{5,6},{6,7},{7,8},{8,9},{9,10},{10,1... | collective-permute-start | bytes 294920 | tf_op jit(solution)/shard_map/ppermute | solution.py:27
  494.0 5.4 collective-permute-start.11
  573.8 2.1 copy-start.7
  575.9 2.4 copy-start.38
  580.9 3.7 copy-start.17
  584.7 2.1 copy-start.45
  592.1 10.4 %copy-start.18 = (f32[4,1,10,4098]{3,2,0,1:T(8,128)S(1)}, f32[4,1,10,4098]{3,2,0,1:T(8,128)}, u32[]{:S(2)}) copy-start(f32[4,1,10,4098]{3,2,0,1:T(8,128)} %copy-done.17) | copy-start | bytes 1967044
  592.1 10.4 %copy-start.20 = (f32[4,1,10,4098]{3,2,0,1:T(8,128)S(1)}, f32[4,1,10,4098]{3,2,0,1:T(8,128)}, u32[]{:S(2)}) copy-start(f32[4,1,10,4098]{3,2,0,1:T(8,128)} %copy-done.19) | copy-start | bytes 1967044
  592.1 10.4 %copy-start.22 = (f32[4,1,10,4098]{3,2,0,1:T(8,128)S(1)}, f32[4,1,10,4098]{3,2,0,1:T(8,128)}, u32[]{:S(2)}) copy-start(f32[4,1,10,4098]{3,2,0,1:T(8,128)} %copy-done.21) | copy-start | bytes 1967044
  598.1 112.7 %collective-permute-start.15 = (f32[12,1,4096]{2,1,0:T(1,128)}, f32[12,1,4096]{2,1,0:T(1,128)}, u32[]{:S(2)}, u32[]{:S(2)}) collective-permute-start(f32[12,1,4096]{2,1,0:T(1,128)} %get-tuple-element.337), channel_id=1, source_target_pairs={{1,0},{2,1},{3,2},{4,3},{5,4},{6,5},{7,6},{8,7},{9,8},{10,9},{11,1... | collective-permute-start | bytes 589832 | tf_op jit(solution)/shard_map/ppermute | solution.py:28
  599.4 103.8 %collective-permute-start.14 = (f32[12,1,4096]{2,1,0:T(1,128)}, f32[12,1,4096]{2,1,0:T(1,128)S(1)}, u32[]{:S(2)}, u32[]{:S(2)}) collective-permute-start(f32[12,1,4096]{2,1,0:T(1,128)} %get-tuple-element.338), channel_id=1, source_target_pairs={{0,1},{1,2},{2,3},{3,4},{4,5},{5,6},{6,7},{7,8},{8,9},{9,10},{10,1... | collective-permute-start | bytes 589832 | tf_op jit(solution)/shard_map/ppermute | solution.py:27
  703.9 13.4 %copy-start.47 = (f32[4,3,4096]{2,0,1:T(4,128)S(1)}, f32[4,3,4096]{2,0,1:T(4,128)}, u32[]{:S(2)}) copy-start(f32[4,3,4096]{2,0,1:T(4,128)} %mul.663) | copy-start | bytes 589828
  724.6 3.9 copy-start.67
  724.6 6.6 copy-start.65
  724.6 9.3 %copy-start.63 = (pred[4]{0:T(512)(128)(4,1)S(1)}, pred[4]{0:T(512)(128)(4,1)}, u32[]{:S(2)}) copy-start(pred[4]{0:T(512)(128)(4,1)} %get-tuple-element.370) | copy-start | bytes 16
  (27 other events, 40.4 us)
Sparse Core Ops, SparseCore 0:
  124.8 64.3 all-gather.10
  218.3 71.8 all-gather.6
  465.0 73.7 all-gather.8
  595.8 66.1 all-gather.12
where the time goes:
time: 756 us; the launch traced here: 743 us
  local copies, waits for them, and re-layouts  245 us (32%)
  blocking collectives  232 us (31%)
  other arithmetic  117 us (15%)
  waiting for transfers between devices  74.1 us (10%)
  starting transfers between devices  36.4 us (5%)
  between operations  35 us (5%)
    unnamed x2, blocking collectives  147 us
    all_gather x2, blocking collectives, child_frame(): lax.all_gather(parent_edges(parent_now, child_cols), 'rows', axis=3, tile...  84.9 us
    slice x2, local copies, waits for them, and re-layouts, adjoint_step(): whole_bands[nested]  54.1 us
    all_gather x2, waiting for transfers between devices, restrict(): shard_rows = lax.all_gather(coarse_means, 'rows', axis=2, tiled=True)  52.6 us
    ppermute x8, starting transfers between devices, extended(): before = lax.ppermute(last, axis, up)  25 us
    all_gather x2, waiting for transfers between devices, adjoint_step(): whole_bands = lax.all_gather(band_cot, 'rows', axis=2, tiled=True)  20.2 us
    scatter-add x4, local copies, waits for them, and re-layouts, rims_back(): return inner.at[..., -1, :].add(received[..., 3, :])  15.3 us
    scatter-add x4, local copies, waits for them, and re-layouts, rims_back(): inner = inner.at[..., 0, :].add(received[..., 0, :])  15.3 us
  transfers between devices with their start and end apart: 20, of which 3 were waited for; matrix products, arithmetic and copies ran while one was open for 20% of the time, Pallas kernels for 0%

commit v1 on v0

v1 whole, which is shorter than its diff:
```python
import functools

import jax
import jax.numpy as jnp
from jax import lax
from jax.experimental import pallas as pl
from jax.experimental.pallas import tpu as pltpu
from jax.sharding import PartitionSpec as P

MESH = pl.DeviceIdType.MESH
P_ROWS = 4
P_COLS = 8192
C_ROWS = 8
C_COLS = 4096
NCHILD = 4
RATIO = 8
FOOT_ROWS = 128
FOOT_COLS = 512
BAND = 2048
TILE = 128
PADDED = C_COLS + 2 * TILE
CHUNK = 512
HALF = 0.15
DRAG = 0.015
FIELDS = 11
UNIT = 256
UNITS = FIELDS * NCHILD * (FOOT_COLS // UNIT)
ROW_UNITS = 6 * NCHILD * (FOOT_COLS // UNIT)
BACK = 3 * NCHILD * (FOOT_COLS // TILE)
BACK_FIRST = 80
EDGE = 8


def column_shifts(wide, width):
    ahead = pltpu.roll(wide, wide.shape[1] - 1, 1)[:, TILE : TILE + width]
    behind = pltpu.roll(wide, 1, 1)[:, TILE : TILE + width]
    return ahead, behind


def row_shifts(block, before, after):
    row = lax.broadcasted_iota(jnp.int32, block.shape, 0)
    ahead = jnp.where(row == C_ROWS - 1, after, pltpu.roll(block, C_ROWS - 1, 0))
    behind = jnp.where(row == 0, before, pltpu.roll(block, 1, 0))
    return ahead, behind


def split3(value):
    high = value.astype(jnp.bfloat16)
    rest = value - high.astype(jnp.float32)
    mid = rest.astype(jnp.bfloat16)
    low = (rest - mid.astype(jnp.float32)).astype(jnp.bfloat16)
    return high, mid, low


def exact_dot(rows, matrix):
    return sum(jnp.dot(part, matrix, preferred_element_type=jnp.float32) for part in split3(rows))


def coastal_kernel(
    n,
    rows_smem,
    win_hbm,
    frame_hbm,
    halo_hbm,
    old_hbm,
    now_hbm,
    depth_hbm,
    mid_hbm,
    end_hbm,
    next_out,
    gold_out,
    gnow_out,
    edge_out,
    back_out,
    halo_out,
    old,
    now,
    nxt,
    depth,
    mid,
    end,
    a2,
    a1,
    slopes1,
    slopes2,
    send_rows,
    halo_rows,
    win,
    frame,
    frames,
    fvals,
    gathered,
    picked,
    special,
    rowbuf,
    specbuf,
    lhs,
    spread,
    sums,
    rest,
    pairs,
    returned,
    placed,
    qrow,
    edges,
    packet,
    load_sem,
    store_sem,
    halo_send,
    halo_recv,
    ag_send,
    ag_recv,
    t_send,
    t_recv,
):
    me = lax.axis_index("rows")
    up = lax.rem(me + 1, n)
    down = lax.rem(me + n - 1, n)
    has_before = jnp.where(me > 0, 1.0, 0.0)
    has_after = jnp.where(me < n - 1, 1.0, 0.0)
    centre = pl.ds(TILE, C_COLS)

    barrier = pltpu.get_barrier_semaphore()

    def greet(j, carry):
        pl.semaphore_signal(barrier, inc=1, device_id=(lax.rem(me + j, n),), device_id_type=MESH)
        return carry

    lax.fori_loop(1, n, greet, 0)

    loads = [
        pltpu.make_async_copy(now_hbm, now.at[:, :, :, centre], load_sem.at[0]),
        pltpu.make_async_copy(old_hbm, old, load_sem.at[1]),
        pltpu.make_async_copy(depth_hbm, depth.at[:, :, centre], load_sem.at[2]),
        pltpu.make_async_copy(mid_hbm, mid, load_sem.at[3]),
        pltpu.make_async_copy(end_hbm, end, load_sem.at[4]),
        pltpu.make_async_copy(win_hbm, win, load_sem.at[5]),
        pltpu.make_async_copy(frame_hbm, frame, load_sem.at[6]),
    ]
    for load in loads:
        load.start()

    for array in (a2, a1):
        array[:, :, :, 0:TILE] = jnp.zeros((NCHILD, 3, C_ROWS, TILE), jnp.float32)
        array[:, :, :, TILE + C_COLS :] = jnp.zeros((NCHILD, 3, C_ROWS, TILE), jnp.float32)
    depth[:, :, 0:TILE] = jnp.zeros((NCHILD, C_ROWS, TILE), jnp.float32)
    depth[:, :, TILE + C_COLS :] = jnp.zeros((NCHILD, C_ROWS, TILE), jnp.float32)
    ocean_rows = n * P_ROWS
    frames[0:EDGE] = jnp.zeros((EDGE, 1, TILE), jnp.float32)
    frames[pl.ds(EDGE + ocean_rows, EDGE)] = jnp.zeros((EDGE, 1, TILE), jnp.float32)
    gathered[0:EDGE] = jnp.zeros((EDGE, 1, UNIT), jnp.float32)
    gathered[pl.ds(EDGE + ocean_rows, EDGE)] = jnp.zeros((EDGE, 1, UNIT), jnp.float32)
    qrow[...] = jnp.zeros_like(qrow)
    packet[...] = jnp.zeros_like(packet)

    loads[0].wait()
    loads[6].wait()
    for nested in range(NCHILD):
        for part in range(3):
            send_rows[0, nested, 0, part : part + 1, :] = now[nested, part, 0:1, centre]
            send_rows[0, nested, 1, part : part + 1, :] = now[nested, part, C_ROWS - 1 : C_ROWS, centre]

    pl.semaphore_wait(barrier, n - 1)

    def halo_copies(stage, nested):
        return (
            pltpu.make_async_remote_copy(
                send_rows.at[stage, nested, 0],
                halo_rows.at[stage, nested, 1],
                halo_send.at[stage, nested, 0],
                halo_recv.at[stage, nested, 1],
                device_id=(down,),
                device_id_type=MESH,
            ),
            pltpu.make_async_remote_copy(
                send_rows.at[stage, nested, 1],
                halo_rows.at[stage, nested, 0],
                halo_send.at[stage, nested, 1],
                halo_recv.at[stage, nested, 0],
                device_id=(up,),
                device_id_type=MESH,
            ),
        )

    def halo_start(stage, nested):
        for copy in halo_copies(stage, nested):
            copy.start()

    def halo_wait(stage, nested):
        for copy in halo_copies(stage, nested):
            copy.wait_recv()

    mine = pl.ds(EDGE + me * P_ROWS, P_ROWS)
    frames[mine] = frame[...]

    def send_frame(j, carry):
        pltpu.make_async_remote_copy(
            frame,
            frames.at[mine],
            ag_send.at[0],
            ag_recv.at[0],
            device_id=(lax.rem(me + j, n),),
            device_id_type=MESH,
        ).start()
        return carry

    lax.fori_loop(1, n, send_frame, 0)
    for nested in range(NCHILD):
        halo_start(0, nested)

    loads[5].wait()

    def send_unit(j, carry):
        unit = lax.rem(me + j, UNITS)

        @pl.when(unit != me)
        def _():
            pltpu.make_async_remote_copy(
                win.at[unit],
                gathered.at[mine],
                t_send.at[0],
                t_recv.at[0],
                device_id=(unit,),
                device_id_type=MESH,
            ).start()

        @pl.when(unit == me)
        def _():
            pltpu.make_async_copy(win.at[unit], gathered.at[mine], t_recv.at[0]).start()

        return carry

    lax.fori_loop(0, UNITS, send_unit, 0)

    @pl.when(me < UNITS)
    def _():
        whole = gathered.at[pl.ds(EDGE, ocean_rows)]
        pltpu.make_async_copy(whole, whole, t_recv.at[0]).wait()
        grid_index = lax.rem(me // (FOOT_COLS // UNIT), NCHILD)
        first = rows_smem[0]
        for nested in range(1, NCHILD):
            first = jnp.where(grid_index == nested, rows_smem[nested], first)
        special[0:3] = gathered[pl.ds(EDGE + first - 2, 3)]
        special[3:6] = gathered[pl.ds(EDGE + first + FOOT_ROWS - 1, 3)]

        def pick(j, carry):
            picked[j] = gathered[EDGE + first + j]
            return carry

        lax.fori_loop(0, FOOT_ROWS, pick, 0)

        for side, target in ((0, 0), (1, n - 1)):
            source = special.at[pl.ds(3 * side, 3)]

            @pl.when(me != target)
            def _():
                pltpu.make_async_remote_copy(
                    source,
                    specbuf.at[me],
                    t_send.at[1],
                    t_recv.at[1],
                    device_id=(target,),
                    device_id_type=MESH,
                ).start()

            @pl.when(me == target)
            def _():
                pltpu.make_async_copy(source, specbuf.at[me], t_recv.at[1]).start()

        @pl.when(me < ROW_UNITS)
        def _():
            def send_row(j, carry):
                target = lax.rem(me + j, n)
                pltpu.make_async_remote_copy(
                    picked.at[target],
                    rowbuf.at[me],
                    t_send.at[2],
                    t_recv.at[2],
                    device_id=(target,),
                    device_id_type=MESH,
                ).start()
                return carry

            lax.fori_loop(1, n, send_row, 0)
            pltpu.make_async_copy(picked.at[me], rowbuf.at[me], t_recv.at[2]).start()

    all_but = frames.at[pl.ds(0, (n - 1) * P_ROWS)]
    pltpu.make_async_copy(all_but, all_but, ag_recv.at[0]).wait()
    lane = lax.broadcasted_iota(jnp.int32, (1, TILE), 1)

    def lanes_of(offset):
        value = frames[EDGE + rows_smem[0] + me + offset]
        for nested in range(1, NCHILD):
            other = frames[EDGE + rows_smem[nested] + me + offset]
            value = jnp.where(lane >= 32 * nested, other, value)
        return value

    south, middle, north = lanes_of(-1), lanes_of(0), lanes_of(1)

    def lane_field(row, index):
        return row if index == 0 else pltpu.roll(row, TILE - index, 1)

    e_w, e_c, e_e = [lane_field(middle, i) for i in (0, 1, 2)]
    u_w, u_c, u_e = [lane_field(middle, i) for i in (3, 4, 5)]
    v_w, v_c, v_e = [lane_field(middle, i) for i in (6, 7, 8)]
    e_s, u_s, v_s = [lane_field(south, i) for i in (1, 4, 7)]
    e_n, u_n, v_n = [lane_field(north, i) for i in (1, 4, 7)]
    e_o, u_o, v_o, b_c, ce_c, cu_c, cv_c = [lane_field(middle, i) for i in range(9, 16)]
    e_2 = e_o - HALF * (
        b_c * ((u_e - u_w) + (v_n - v_s)) + (e_e * u_e - e_w * u_w) + (e_n * v_n - e_s * v_s)
    )
    u_2 = u_o - HALF * (u_c * (u_e - u_w) + v_c * (u_n - u_s) + (e_e - e_w)) - DRAG * u_c
    v_2 = v_o - HALF * (u_c * (v_e - v_w) + v_c * (v_n - v_s) + (e_n - e_s)) - DRAG * v_c
    for index, value in enumerate((e_c, u_c, v_c, e_2, u_2, v_2, b_c, ce_c, cu_c, cv_c)):
        fvals[index : index + 1, :] = value
    for nested in range(NCHILD):
        for side in range(2):
            where = 32 * nested + 16 * side
            lanes = slice(0, TILE) if side == 0 else slice(TILE + C_COLS, PADDED)
            for part in range(3):
                for base, array in ((0, now), (3, nxt)):
                    cell = fvals[base + part : base + part + 1, where : where + 1]
                    array[nested, part, :, lanes] = jnp.broadcast_to(cell, (C_ROWS, TILE))

    def forward(stage, nested, state, base, target, slopes):
        def chunk(j, carry):
            here = pl.multiple_of(j * CHUNK, CHUNK)
            wide = pl.ds(here, CHUNK + 2 * TILE)
            plain = pl.ds(here, CHUNK)
            inner = pl.ds(here + TILE, CHUNK)
            shifted = []
            for part in range(3):
                block = state[nested, part, :, wide]
                mid_block = block[:, TILE : TILE + CHUNK]
                before = halo_rows[stage, nested, 0, part : part + 1, plain] * has_before
                after = halo_rows[stage, nested, 1, part : part + 1, plain] * has_after
                shifted.append(
                    (mid_block,) + column_shifts(block, CHUNK) + row_shifts(mid_block, before, after)
                )
            (e, ee, ew, en, es), (u, ue, uw, un, us), (v, ve, vw, vn, vs) = shifted
            bed = depth[nested, :, inner]
            ux, uy, vx, vy = ue - uw, un - us, ve - vw, vn - vs
            slopes[0, nested, :, plain] = ux
            slopes[1, nested, :, plain] = uy
            slopes[2, nested, :, plain] = vx
            slopes[3, nested, :, plain] = vy
            news = (
                base(0, inner, plain)
                - HALF * (bed * (ux + vy) + (ee * ue - ew * uw) + (en * vn - es * vs)),
                base(1, inner, plain) - HALF * (u * ux + v * uy + (ee - ew)) - DRAG * u,
                base(2, inner, plain) - HALF * (u * vx + v * vy + (en - es)) - DRAG * v,
            )
            for part in range(3):
                target(part, inner, plain, news[part], j)
            return carry

        lax.fori_loop(0, C_COLS // CHUNK, chunk, 0)

    def add_sums(which, nested, part, value, j):
        row = (nested * 3 + part) * 4 + j // 2
        sums[which, pl.ds(row, 1), pl.ds(pl.multiple_of(lax.rem(j, 2) * CHUNK, CHUNK), CHUNK)] = (
            jnp.sum(value, axis=0, keepdims=True)
        )

    def stage_a(nested, carry):
        halo_wait(0, nested)

        def target(part, inner, plain, value, j):
            nxt[nested, part, :, inner] = value
            send_rows[1, nested, 0, part : part + 1, plain] = value[0:1]
            send_rows[1, nested, 1, part : part + 1, plain] = value[C_ROWS - 1 :]
            add_sums(0, nested, part, value, j)

        forward(0, nested, now, lambda part, inner, plain: old[nested, part, :, plain], target, slopes1)
        halo_start(1, nested)
        return carry

    for index in (1, 2, 3, 4):
        loads[index].wait()
    lax.fori_loop(0, NCHILD, stage_a, 0)

    def stage_b(nested, carry):
        halo_wait(1, nested)

        def target(part, inner, plain, value, j):
            old[nested, part, :, plain] = value
            add_sums(1, nested, part, value, j)

        forward(1, nested, nxt, lambda part, inner, plain: now[nested, part, :, inner], target, slopes2)
        return carry

    lax.fori_loop(0, NCHILD, stage_b, 0)
    store_next = pltpu.make_async_copy(old, next_out, store_sem.at[0])
    store_next.start()

    fine = lax.broadcasted_iota(jnp.int32, (RATIO * TILE, TILE), 0) // RATIO
    coarse = lax.broadcasted_iota(jnp.int32, (RATIO * TILE, TILE), 1)
    gather_matrix = jnp.where(fine == coarse, 1.0 / (RATIO * RATIO), 0.0).astype(jnp.bfloat16)
    fine_t = lax.broadcasted_iota(jnp.int32, (TILE, RATIO * TILE), 1) // RATIO
    coarse_t = lax.broadcasted_iota(jnp.int32, (TILE, RATIO * TILE), 0)
    spread_matrix = jnp.where(fine_t == coarse_t, 1.0 / (RATIO * RATIO), 0.0).astype(jnp.bfloat16)
    for which in range(2):
        rest[which] = exact_dot(sums[which], gather_matrix)
    for unit in range(BACK):
        for which in range(2):
            pairs[unit, which : which + 1, :] = rest[which, unit : unit + 1, :]

    span = FOOT_ROWS
    pad = ocean_rows
    returned[0:pad] = jnp.zeros((pad, 2, TILE), jnp.float32)
    returned[pl.ds(pad + span, pad)] = jnp.zeros((pad, 2, TILE), jnp.float32)

    def send_back(j, carry):
        unit = lax.rem(me + j, BACK)
        owner = unit + BACK_FIRST

        @pl.when(owner != me)
        def _():
            pltpu.make_async_remote_copy(
                pairs.at[unit],
                returned.at[pad + me],
                t_send.at[3],
                t_recv.at[3],
                device_id=(owner,),
                device_id_type=MESH,
            ).start()

        @pl.when(owner == me)
        def _():
            pltpu.make_async_copy(pairs.at[unit], returned.at[pad + me], t_recv.at[3]).start()

        return carry

    lax.fori_loop(0, BACK, send_back, 0)

    all_rows = rowbuf.at[pl.ds(0, ROW_UNITS)]
    pltpu.make_async_copy(all_rows, all_rows, t_recv.at[2]).wait()
    parts_of = FOOT_COLS // UNIT
    for which in range(2):
        for nested in range(NCHILD):
            for part in range(3):
                for half in range(parts_of):
                    unit = ((3 * which + part) * NCHILD + nested) * parts_of + half
                    for piece in range(UNIT // TILE):
                        row = (nested * 3 + part) * 4 + half * (UNIT // TILE) + piece
                        lhs[which, row : row + 1, :] = rowbuf[unit, :, TILE * piece : TILE * (piece + 1)]
    spread[0] = exact_dot(lhs[0], spread_matrix)

    def spread_at(which, nested, part, j):
        row = (nested * 3 + part) * 4 + j // 2
        return spread[which, pl.ds(row, 1), pl.ds(pl.multiple_of(lax.rem(j, 2) * CHUNK, CHUNK), CHUNK)]

    def put_products(stage, nested, plain, bed, v, ae, au, av):
        for index, value in enumerate((ae, av, v * au, bed * ae + v * av)):
            send_rows[stage, nested, 0, index : index + 1, plain] = value[0:1]
            send_rows[stage, nested, 1, index : index + 1, plain] = value[C_ROWS - 1 :]

    def stage_c(nested, carry):
        def chunk(j, inner_carry):
            here = pl.multiple_of(j * CHUNK, CHUNK)
            plain = pl.ds(here, CHUNK)
            inner = pl.ds(here + TILE, CHUNK)
            scaled = []
            for part in range(3):
                total = end[nested, part, :, plain] + spread_at(0, nested, part, j)
                end[nested, part, :, plain] = total
                scaled.append(HALF * total)
                a2[nested, part, :, inner] = scaled[-1]
            put_products(2, nested, plain, depth[nested, :, inner], nxt[nested, 2, :, inner], *scaled)
            return inner_carry

        lax.fori_loop(0, C_COLS // CHUNK, chunk, 0)
        halo_start(2, nested)
        return carry

    lax.fori_loop(0, NCHILD, stage_c, 0)

    @pl.when((me == 0) | (me == n - 1))
    def _():
        all_special = specbuf.at[pl.ds(0, UNITS)]
        pltpu.make_async_copy(all_special, all_special, t_recv.at[1]).wait()
        sign = jnp.where(me == 0, -1.0, 1.0)
        offset = jnp.where(me == 0, -1, 1)
        wide_lane = lax.broadcasted_iota(jnp.int32, (1, FOOT_COLS), 1)
        for nested in range(NCHILD):

            def line(field, row):
                unit = (field * NCHILD + nested) * parts_of
                return jnp.concatenate([specbuf[unit + half, row] for half in range(parts_of)], axis=1)

            ce, cu, cv = [HALF * line(field, 1) for field in range(3)]
            u1, v1 = line(7, 1), line(8, 1)
            side_row = frames[EDGE + rows_smem[nested] + me + offset]
            west = side_row[:, 32 * nested + 7 : 32 * nested + 8]
            east = side_row[:, 32 * nested + 23 : 32 * nested + 24]
            v_east = jnp.where(
                wide_lane == FOOT_COLS - 1, east, pltpu.roll(v1, FOOT_COLS - 1, 1)
            )
            v_west = jnp.where(wide_lane == 0, west, pltpu.roll(v1, 1, 1))
            v2 = (
                line(9, 1)
                - HALF
                * (
                    u1 * (v_east - v_west)
                    + v1 * (line(8, 2) - line(8, 0))
                    + (line(6, 2) - line(6, 0))
                )
                - DRAG * v1
            )
            e_q, v_q = [
                jnp.concatenate(
                    [rest[0, (nested * 3 + part) * 4 + q : (nested * 3 + part) * 4 + q + 1, :] for q in range(4)],
                    axis=1,
                )
                for part in (0, 2)
            ]
            qrow[nested, 0:1, :] = sign * (v_q * ce + cv)
            qrow[nested, 1:2, :] = sign * (v2 * cu)
            qrow[nested, 2:3, :] = sign * (line(10, 1) * ce + v2 * cv + e_q * ce)

    for nested in range(NCHILD):
        row0 = nested * 12
        for side in range(2):
            sign = -1.0 if side == 0 else 1.0
            where = 32 * nested + 16 * side
            cell = 0 if side == 0 else TILE - 1
            chunk_row = 0 if side == 0 else 3
            u2, bed, ce, cu, cv = [fvals[i : i + 1, where : where + 1] for i in (4, 6, 7, 8, 9)]
            ce, cu, cv = HALF * ce, HALF * cu, HALF * cv
            e_q = rest[0, row0 + chunk_row : row0 + chunk_row + 1, cell : cell + 1]
            u_q = rest[0, row0 + 4 + chunk_row : row0 + 5 + chunk_row, cell : cell + 1]
            adds = (
                sign * (u_q * ce + cu),
                sign * (bed * ce + u2 * cu + e_q * ce),
                sign * (u2 * cv),
            )
            for part in range(3):
                row = row0 + 4 * part + chunk_row
                lhs[1, row : row + 1, :] += jnp.where(lane == cell, adds[part], 0.0)
        for part in range(3):
            for q in range(4):
                row = row0 + 4 * part + q
                lhs[1, row : row + 1, :] += qrow[nested, part : part + 1, TILE * q : TILE * (q + 1)]
    spread[1] = exact_dot(lhs[1], spread_matrix)

    def adjoint(stage, nested, state, cots, slopes, target):
        def chunk(j, carry):
            here = pl.multiple_of(j * CHUNK, CHUNK)
            wide = pl.ds(here, CHUNK + 2 * TILE)
            plain = pl.ds(here, CHUNK)
            inner = pl.ds(here + TILE, CHUNK)
            cut = slice(TILE, TILE + CHUNK)
            wae, wau, wav = [cots[nested, part, :, wide] for part in range(3)]
            wu = state[nested, 1, :, wide]
            wbed = depth[nested, :, wide]
            ae, au, av, u, bed = wae[:, cut], wau[:, cut], wav[:, cut], wu[:, cut], wbed[:, cut]
            e, v = state[nested, 0, :, inner], state[nested, 2, :, inner]

            def dx(field):
                ahead, behind = column_shifts(field, CHUNK)
                return ahead - behind

            def dy(field, index):
                before = halo_rows[stage, nested, 0, index : index + 1, plain] * has_before
                after = halo_rows[stage, nested, 1, index : index + 1, plain] * has_after
                ahead, behind = row_shifts(field, before, after)
                return ahead - behind

            xe, ye = dx(wae), dy(ae, 0)
            ge = u * xe + v * ye + dx(wau) + dy(av, 1)
            gu = (
                dx(wbed * wae + wu * wau)
                + dy(v * au, 2)
                + e * xe
                - slopes[0, nested, :, plain] * au
                - slopes[2, nested, :, plain] * av
                - 0.1 * au
            )
            gv = (
                dy(bed * ae + v * av, 3)
                + dx(wu * wav)
                + e * ye
                - slopes[1, nested, :, plain] * au
                - slopes[3, nested, :, plain] * av
                - 0.1 * av
            )
            target(inner, plain, j, (ge, gu, gv))
            return carry

        lax.fori_loop(0, C_COLS // CHUNK, chunk, 0)

    def frame_cots(nested, state, cots, first):
        for side in range(2):
            near = pl.ds(TILE, TILE) if side == 0 else pl.ds(C_COLS, TILE)
            far = pl.ds(0, TILE) if side == 0 else pl.ds(TILE + C_COLS, TILE)
            cell = 0 if side == 0 else TILE - 1
            sign = 1.0 if side == 0 else -1.0
            ae, au, av = [cots[nested, part, :, near] for part in range(3)]
            u, bed = state[nested, 1, :, near], depth[nested, :, near]
            ef, uf = state[nested, 0, :, far], state[nested, 1, :, far]
            values = (uf * ae + au, bed * ae + u * au + ef * ae, u * av)
            for part in range(3):
                column = sign * jnp.sum(values[part], axis=0, keepdims=True)[:, cell : cell + 1]
                packet[...] = jnp.where(
                    lane == nested * 16 + side * 8 + first + part, column, packet[...]
                )

    def stage_d(nested, carry):
        halo_wait(2, nested)

        def target(inner, plain, j, grads):
            scaled = []
            for part in range(3):
                total = mid[nested, part, :, plain] + grads[part] + spread_at(1, nested, part, j)
                mid[nested, part, :, plain] = total
                scaled.append(HALF * total)
                a1[nested, part, :, inner] = scaled[-1]
            put_products(3, nested, plain, depth[nested, :, inner], now[nested, 2, :, inner], *scaled)

        adjoint(2, nested, nxt, a2, slopes2, target)
        halo_start(3, nested)
        frame_cots(nested, nxt, a2, 0)
        return carry

    lax.fori_loop(0, NCHILD, stage_d, 0)
    store_gold = pltpu.make_async_copy(mid, gold_out, store_sem.at[1])
    store_gold.start()

    def stage_e1(nested, carry):
        frame_cots(nested, now, a1, 3)
        return carry

    lax.fori_loop(0, NCHILD, stage_e1, 0)

    edges[me] = packet[...]

    def send_edge(j, carry):
        pltpu.make_async_remote_copy(
            packet,
            edges.at[me],
            ag_send.at[1],
            ag_recv.at[1],
            device_id=(lax.rem(me + j, n),),
            device_id_type=MESH,
        ).start()
        return carry

    lax.fori_loop(1, n, send_edge, 0)

    @pl.when(me >= BACK_FIRST)
    def _():
        all_back = returned.at[pl.ds(pad, span)]
        pltpu.make_async_copy(all_back, all_back, t_recv.at[3]).wait()
        grid_index = (me - BACK_FIRST) // 12
        first = rows_smem[0]
        for nested in range(1, NCHILD):
            first = jnp.where(grid_index == nested, rows_smem[nested], first)
        placed[0:EDGE] = jnp.zeros((EDGE, 2, TILE), jnp.float32)
        placed[pl.ds(EDGE + ocean_rows, EDGE)] = jnp.zeros((EDGE, 2, TILE), jnp.float32)

        def place(j, carry):
            placed[EDGE + j] = returned[pad + j - first]
            return carry

        lax.fori_loop(0, ocean_rows, place, 0)

        def send_placed(j, carry):
            target = lax.rem(me + j, n)
            pltpu.make_async_remote_copy(
                placed.at[pl.ds(EDGE + target * P_ROWS - 2, 8)],
                back_out.at[me - BACK_FIRST],
                t_send.at[4],
                t_recv.at[4],
                device_id=(target,),
                device_id_type=MESH,
            ).start()
            return carry

        lax.fori_loop(1, n, send_placed, 0)
        pltpu.make_async_copy(
            placed.at[pl.ds(EDGE + me * P_ROWS - 2, 8)], back_out.at[me - BACK_FIRST], t_recv.at[4]
        ).start()

    ocean_up = pltpu.make_async_remote_copy(
        halo_hbm.at[1], halo_out.at[0], load_sem.at[7], load_sem.at[8], device_id=(up,), device_id_type=MESH
    )
    ocean_down = pltpu.make_async_remote_copy(
        halo_hbm.at[0], halo_out.at[1], load_sem.at[9], load_sem.at[10], device_id=(down,), device_id_type=MESH
    )
    ocean_up.start()
    ocean_down.start()

    def stage_e(nested, carry):
        halo_wait(3, nested)

        def target(inner, plain, j, grads):
            for part in range(3):
                end[nested, part, :, plain] = end[nested, part, :, plain] + grads[part]

        adjoint(3, nested, now, a1, slopes1, target)
        return carry

    lax.fori_loop(0, NCHILD, stage_e, 0)
    store_gnow = pltpu.make_async_copy(end, gnow_out, store_sem.at[2])
    store_gnow.start()

    all_edges = edges.at[pl.ds(0, n - 1)]
    pltpu.make_async_copy(all_edges, all_edges, ag_recv.at[1]).wait()
    store_edges = pltpu.make_async_copy(edges, edge_out, store_sem.at[3])
    store_edges.start()

    ocean_up.wait()
    ocean_down.wait()
    pltpu.make_async_copy(back_out, back_out, t_recv.at[4]).wait()
    for store in (store_next, store_gold, store_gnow, store_edges):
        store.wait()

    pltpu.make_async_copy(all_but, all_but, ag_send.at[0]).wait()
    pltpu.make_async_copy(all_edges, all_edges, ag_send.at[1]).wait()

    def drain_halo(nested, carry):
        for stage in range(4):
            for copy in halo_copies(stage, nested):
                copy.wait_send()
        return carry

    lax.fori_loop(0, NCHILD, drain_halo, 0)

    @pl.when(me < UNITS)
    def _():
        sent = win.at[pl.ds(0, UNITS - 1)]
        pltpu.make_async_copy(sent, sent, t_send.at[0]).wait()
        for target in (0, n - 1):

            @pl.when(me != target)
            def _():
                one = special.at[pl.ds(0, 3)]
                pltpu.make_async_copy(one, one, t_send.at[1]).wait()

    @pl.when(me >= UNITS)
    def _():
        pltpu.make_async_copy(win, win, t_send.at[0]).wait()

    @pl.when(me < ROW_UNITS)
    def _():
        sent = picked.at[pl.ds(0, n - 1)]
        pltpu.make_async_copy(sent, sent, t_send.at[2]).wait()

    @pl.when(me >= BACK_FIRST)
    def _():
        sent = pairs.at[pl.ds(0, BACK - 1)]
        pltpu.make_async_copy(sent, sent, t_send.at[3]).wait()
        gone = returned.at[pl.ds(0, (n - 1) * 8)]
        pltpu.make_async_copy(gone, gone, t_send.at[4]).wait()

    @pl.when(me < BACK_FIRST)
    def _():
        pltpu.make_async_copy(pairs, pairs, t_send.at[3]).wait()


def coastal(n, child_rows, win, frame, halo, old, now, depth, mid, end):
    f32 = jnp.float32
    anywhere = pl.BlockSpec(memory_space=pl.ANY)
    grid_shape = (NCHILD, 3, C_ROWS, C_COLS)
    wide_shape = (NCHILD, 3, C_ROWS, PADDED)
    ocean_rows = n * P_ROWS
    dma = pltpu.SemaphoreType.DMA
    return pl.pallas_call(
        functools.partial(coastal_kernel, n),
        out_shape=[jax.ShapeDtypeStruct(grid_shape, f32)] * 3
        + [
            jax.ShapeDtypeStruct((n, 1, TILE), f32),
            jax.ShapeDtypeStruct((BACK, 8, 2, TILE), f32),
            jax.ShapeDtypeStruct(halo.shape, f32),
        ],
        in_specs=[pl.BlockSpec(memory_space=pltpu.SMEM)] + [anywhere] * 8,
        out_specs=[anywhere] * 6,
        scratch_shapes=[
            pltpu.VMEM(grid_shape, f32),
            pltpu.VMEM(wide_shape, f32),
            pltpu.VMEM(wide_shape, f32),
            pltpu.VMEM((NCHILD, C_ROWS, PADDED), f32),
            pltpu.VMEM(grid_shape, f32),
            pltpu.VMEM(grid_shape, f32),
            pltpu.VMEM(wide_shape, f32),
            pltpu.VMEM(wide_shape, f32),
            pltpu.VMEM((4, NCHILD, C_ROWS, C_COLS), f32),
            pltpu.VMEM((4, NCHILD, C_ROWS, C_COLS), f32),
            pltpu.VMEM((4, NCHILD, 2, 4, C_COLS), f32),
            pltpu.VMEM((4, NCHILD, 2, 4, C_COLS), f32),
            pltpu.VMEM(win.shape, f32),
            pltpu.VMEM((P_ROWS, 1, TILE), f32),
            pltpu.VMEM((ocean_rows + 2 * EDGE, 1, TILE), f32),
            pltpu.VMEM((16, TILE), f32),
            pltpu.VMEM((ocean_rows + 2 * EDGE, 1, UNIT), f32),
            pltpu.VMEM((FOOT_ROWS, 1, UNIT), f32),
            pltpu.VMEM((6, 1, UNIT), f32),
            pltpu.VMEM((ROW_UNITS, 1, UNIT), f32),
            pltpu.VMEM((UNITS, 3, 1, UNIT), f32),
            pltpu.VMEM((2, BACK, TILE), f32),
            pltpu.VMEM((2, BACK, RATIO * TILE), f32),
            pltpu.VMEM((2, BACK, RATIO * TILE), f32),
            pltpu.VMEM((2, BACK, TILE), f32),
            pltpu.VMEM((BACK, 2, TILE), f32),
            pltpu.VMEM((2 * ocean_rows + FOOT_ROWS, 2, TILE), f32),
            pltpu.VMEM((ocean_rows + 2 * EDGE, 2, TILE), f32),
            pltpu.VMEM((NCHILD, 8, FOOT_COLS), f32),
            pltpu.VMEM((n, 1, TILE), f32),
            pltpu.VMEM((1, TILE), f32),
            dma((11,)),
            dma((4,)),
            dma((4, NCHILD, 2)),
            dma((4, NCHILD, 2)),
            dma((2,)),
            dma((2,)),
            dma((5,)),
            dma((5,)),
        ],
        compiler_params=pltpu.CompilerParams(
            collective_id=0, has_side_effects=True, vmem_limit_bytes=48 * 1024 * 1024
        ),
    )(child_rows, win, frame, halo, old, now, depth, mid, end)


def windows(parent_old, parent_now, parent_depth, cot_mid, cot_end, child_cols):
    fields = jnp.concatenate(
        [cot_end, cot_mid, parent_now, parent_old[2:], parent_depth[None]], axis=0
    )
    parts = []
    for nested in range(NCHILD):
        parts.append(lax.dynamic_slice_in_dim(fields, child_cols[nested], FOOT_COLS, 2))
    win = jnp.stack(parts, axis=1)
    win = win.reshape(FIELDS, NCHILD, P_ROWS, FOOT_COLS // UNIT, UNIT)
    win = jnp.transpose(win, (0, 1, 3, 2, 4)).reshape(UNITS, P_ROWS, 1, UNIT)
    padded = jnp.pad(parent_now, ((0, 0), (0, 0), (1, 1)))
    packet = []
    for nested in range(NCHILD):
        for column in (child_cols[nested] - 1, child_cols[nested] + FOOT_COLS):
            around = lax.dynamic_slice_in_dim(padded, column, 3, 2)
            packet.append(jnp.transpose(around, (1, 0, 2)).reshape(P_ROWS, 9))
            for array in (parent_old, parent_depth[None], cot_end):
                packet.append(jnp.transpose(lax.dynamic_slice_in_dim(array, column, 1, 2)[..., 0]))
    return win, jnp.concatenate(packet, axis=1).reshape(P_ROWS, 1, TILE)


def dx(field):
    padded = jnp.pad(field, [(0, 0)] * (field.ndim - 1) + [(1, 1)])
    return padded[..., 2:] - padded[..., :-2]


def dy(field):
    padded = jnp.pad(field, [(0, 0)] * (field.ndim - 2) + [(1, 1), (0, 0)])
    return padded[..., 2:, :] - padded[..., :-2, :]


def step(old, state, depth):
    e, u, v = state
    return jnp.stack(
        [
            old[0] - HALF * (depth * (dx(u) + dy(v)) + dx(e * u) + dy(e * v)),
            old[1] - HALF * (u * dx(u) + v * dy(u) + dx(e)) - DRAG * u,
            old[2] - HALF * (u * dx(v) + v * dy(v) + dy(e)) - DRAG * v,
        ]
    )


def pull(state, cots, depth):
    e, u, v = state
    ae, au, av = [HALF * cots[i] for i in range(3)]
    xe, ye = dx(ae), dy(ae)
    return jnp.stack(
        [
            u * xe + v * ye + dx(au) + dy(av),
            dx(depth * ae + u * au) + dy(v * au) + e * xe - dx(u) * au - dx(v) * av - 0.1 * au,
            dy(depth * ae + v * av) + dx(u * av) + e * ye - dy(u) * au - dy(v) * av - 0.1 * av,
        ]
    )


def ocean(n, halo, own, edges, back, child_rows, child_cols):
    me = lax.axis_index("rows")
    before = jnp.where(me > 0, halo[0], 0.0).reshape(13, 3, P_COLS)
    after = jnp.where(me < n - 1, halo[1], 0.0).reshape(13, 3, P_COLS)
    tall = jnp.concatenate([before, own, after], axis=1)
    old, now, depth, mid, end = tall[0:3], tall[3:6], tall[6], tall[7:10], tall[10:13]
    row = me * P_ROWS - 3 + jnp.arange(10)
    inside = ((row >= 0) & (row < n * P_ROWS))[:, None]
    column = jnp.arange(P_COLS)[None, :]
    back = jnp.transpose(back.reshape(NCHILD, 3, 4, 8, 2, TILE), (4, 0, 1, 3, 2, 5)).reshape(
        2, NCHILD, 3, 8, FOOT_COLS
    )
    back = jnp.pad(back, ((0, 0), (0, 0), (0, 0), (1, 1), (0, 0)))
    covered = jnp.zeros((10, P_COLS), bool)
    means = [jnp.zeros((3, 10, P_COLS), jnp.float32) for _ in range(2)]
    extra = [jnp.zeros((3, 10, P_COLS), jnp.float32) for _ in range(2)]
    for nested in range(NCHILD):
        foot = row - child_rows[nested]
        in_rows = ((foot >= 0) & (foot < FOOT_ROWS))[:, None]
        left = child_cols[nested]
        covered = covered | (in_rows & (column >= left) & (column < left + FOOT_COLS))
        for which in range(2):
            means[which] = lax.dynamic_update_slice_in_dim(means[which], back[which, nested], left, 2)
        line = edges[jnp.clip(foot, 0, FOOT_ROWS - 1), 0]
        line = jnp.where(in_rows, line, 0.0)
        for side, at in ((0, left - 1), (1, left + FOOT_COLS)):
            for which in range(2):
                first = nested * 16 + side * 8 + 3 * which
                cells = jnp.transpose(line[:, first : first + 3])[:, :, None]
                extra[which] = jnp.where(column == at, cells, extra[which])
    raw2 = jnp.where(inside, step(old, now, depth), 0.0)
    state2 = jnp.where(covered, means[0], raw2)
    state3 = jnp.where(covered, means[1], step(now, state2, depth))
    cot3 = jnp.where(covered, 0.0, end)
    cot2 = mid + pull(state2, cot3, depth) + extra[0]
    cot2 = jnp.where(covered | ~inside, 0.0, cot2)
    cot1 = cot3 + pull(now, cot2, depth) + extra[1]
    mine = slice(3, 3 + P_ROWS)
    return state3[:, mine], cot2[:, mine], cot1[:, mine]


def shards(
    n,
    parent_old,
    parent_now,
    child_old,
    child_now,
    parent_depth,
    child_depth,
    child_rows,
    child_cols,
    parent_cot_mid,
    parent_cot_end,
    child_cot_mid,
    child_cot_end,
):
    win, frame = windows(parent_old, parent_now, parent_depth, parent_cot_mid, parent_cot_end, child_cols)
    own = jnp.concatenate(
        [parent_old, parent_now, parent_depth[None], parent_cot_mid, parent_cot_end], axis=0
    )
    halo = jnp.stack([own[:, 0:3], own[:, 1:4]]).reshape(2, 39, P_COLS)
    child_end, child_gold, child_gnow, edges, back, halos = coastal(
        n, child_rows, win, frame, halo, child_old, child_now, child_depth, child_cot_mid, child_cot_end
    )
    parent_end, parent_gold, parent_gnow = ocean(n, halos, own, edges, back, child_rows, child_cols)
    return (parent_end, child_end, parent_gold, parent_gnow, child_gold, child_gnow)


def solution(mesh):
    ocean_spec = P(None, "rows", None)
    coast_spec = P(None, None, "rows", None)
    return jax.shard_map(
        functools.partial(shards, mesh.shape["rows"]),
        mesh=mesh,
        in_specs=(
            ocean_spec,
            ocean_spec,
            coast_spec,
            coast_spec,
            P("rows", None),
            P(None, "rows", None),
            P(),
            P(),
            ocean_spec,
            ocean_spec,
            coast_spec,
            coast_spec,
        ),
        out_specs=(ocean_spec, coast_spec, ocean_spec, ocean_spec, coast_spec, coast_spec),
        check_vma=False,
    )
```

time: 756 us -> 212 us (0.28); the launches traced: 743 us -> 211 us
  blocking collectives: 232 us -> 0 us
  local copies, waits for them, and re-layouts: 245 us -> 66.2 us
  Pallas kernels: 0 us -> 81.9 us
  other arithmetic: 117 us -> 40.1 us
  waiting for transfers between devices: 74.1 us -> 0 us
  starting transfers between devices: 36.4 us -> 0 us
  between operations: 35 us -> 22.4 us
    unnamed x2 -> x0, blocking collectives: 147 us -> none
    all_gather x2 -> x0, blocking collectives: 84.9 us -> none  [child_frame(): lax.all_gather(parent_edges(parent_now, child_cols), 'rows', axis=3, tile...]
    pallas_call x0 -> x1, Pallas kernels: none -> 81.9 us  [coastal(): pl.pallas_call(functools.partial(coastal_kernel, n), out_shape=[jax.Shape...]
    slice x18 -> x10, local copies, waits for them, and re-layouts: 87 us -> 6.86 us  [the longest x7 2.94 us: ocean(): return (state3[:, mine], cot2[:, mine], cot1[:, mine])]
    all_gather x4 -> x0, waiting for transfers between devices: 72.8 us -> none  [the longest x2 52.6 us: restrict(): shard_rows = lax.all_gather(coarse_means, 'rows', axis=2, tiled=True)]
    dynamic_update_slice x32 -> x8, local copies, waits for them, and re-layouts: 53.9 us -> 16.6 us  [ocean(): lax.dynamic_update_slice_in_dim(means[which], back[which, nested], left, 2)]
    ppermute x16 -> x0, starting transfers between devices: 35.8 us -> none  [the longest x8 25 us: extended(): before = lax.ppermute(last, axis, up)]
    scatter-add x8 -> x0, local copies, waits for them, and re-layouts: 30.5 us -> none  [the longest x4 15.3 us: rims_back(): return inner.at[..., -1, :].add(received[..., 3, :])]
  transfers between devices with their start and end apart: 20 -> 0, of which waited for: 3 -> 0; matrix products, arithmetic and copies ran while one was open for 20% -> 0% of each run, Pallas kernels for 0% -> 0%
where the time goes in v1:
time: 212 us; the launch traced here: 211 us
  Pallas kernels  81.9 us (39%)
  local copies, waits for them, and re-layouts  66.2 us (31%)
  other arithmetic  40.1 us (19%)
  between operations  22.4 us (11%)
    pallas_call x1, Pallas kernels, coastal(): pl.pallas_call(functools.partial(coastal_kernel, n), out_shape=[jax.Shape...  81.9 us
    dynamic_update_slice x8, local copies, waits for them, and re-layouts, ocean(): lax.dynamic_update_slice_in_dim(means[which], back[which, nested], left, 2)  16.6 us
    unnamed x85, local copies, waits for them, and re-layouts  15 us
    transpose x15, local copies, waits for them, and re-layouts, ocean(): cells = jnp.transpose(line[:, first:first + 3])[:, :, None]  5.81 us
    another operation x2, other arithmetic, pull(): jnp.stack([u * xe + v * ye + dx(au) + dy(av), dx(depth * ae + u * au) + d...  4.97 us
    another operation x3, other arithmetic, step(): jnp.stack([old[0] - HALF * (depth * (dx(u) + dy(v)) + dx(e * u) + dy(e *...  4.29 us

profile of v1, /device:TPU:0, one launch (start us, length us, event | category | flops | bytes accessed | tf_op | source)
XLA Modules:
  0.0 210.7 jit_solution(4798018025299271521)
XLA Ops:
  0.7 1.1 constant_dynamic-update-slice_fusion.6
  1.8 1.0 constant_dynamic-update-slice_fusion.5
  3.0 0.9 constant_dynamic-update-slice_fusion.3
  3.8 0.8 constant_dynamic-update-slice_fusion.1
  4.6 0.8 constant_dynamic-update-slice_fusion
  5.4 1.6 slice_dynamic-update-slice_fusion
  7.0 0.7 bitcast_dynamic-update-slice_fusion.1
  15.3 1.3 constant_dynamic-slice_fusion.27
  31.6 1.0 constant_dynamic-slice_fusion
  35.2 2.7 %fusion.60 = (f32[13,3,8192]{2,1,0:T(4,128)}, f32[13,3,8192]{2,1,0:T(4,128)}) fusion(f32[13,4,8192]{2,1,0:T(4,128)S(1)} %get-tuple-element.73), kind=kLoop, calls=%fused_computation.225 | loop fusion | bytes 5111808 | tf_op jit(solution)/shard_map/slice | solution.py:940
  37.9 2.0 stack.78
  39.9 1.7 stack.77
  41.6 3.0 %pad_maximum_fusion.halo_hbm = f32[2,39,8192]{2,1,0:T(8,128)} fusion(f32[1,39,8192]{2,1,0:T(8,128)S(1)} %stack.78, f32[1,39,8192]{2,1,0:T(8,128)} %stack.77), kind=kLoop, calls=%fused_computation.4 | loop fusion | flops 638976 | bytes 5111808 | tf_op jit(solution)/shard_map/stack | solution.py:940
  44.6 81.9 %shard_map.163 = (f32[4,3,8,4096]{3,2,1,0:T(8,128)S(1)}, f32[4,3,8,4096]{3,2,1,0:T(8,128)S(1)}, f32[4,3,8,4096]{3,2,1,0:T(8,128)S(1)}, f32[128,1,128]{2,1,0:T(1,...) custom-call(s32[4]{0:T(128)S(1)} %copy-done.5, f32[88,4,1,256]{3,2,1,0:T(1,128)S(1)} %reshape.293.win_hbm, ...), custom_call_target="tpu_custom_call" | custom-call | tf_op jit(solution)/shard_map/pallas_call | solution.py:768
  126.5 1.1 copy-done
  128.3 0.8 fusion.30
  129.1 1.2 broadcast.464.clone
  130.4 2.1 dynamic_update_slice.24
  132.4 2.0 dynamic_update_slice.25
  134.5 2.0 dynamic_update_slice.26
  136.5 2.0 dynamic_update_slice.27
  138.6 3.4 %slice_select_fusion.1 = (f32[1,39,8192]{2,1,0:T(8,128)}, f32[1,39,8192]{2,1,0:T(8,128)}) fusion(f32[2,39,8192]{2,1,0:T(8,128)} %get-tuple-element.13, pred[]{:T(512)S(6)} %gt.3, pred[]{:T(512)S(6)} %lt.214), kind=kLoop, calls=%fused_computation.23 | loop fusion | flops 638976 | bytes 5111810 | tf_op jit(solution)/shard_map/jit(_where)/select_n | solution.py:882
  142.0 2.7 %select_n.251 = f32[13,3,8192]{2,1,0:T(4,128)} reshape(f32[1,39,8192]{2,1,0:T(8,128)} %get-tuple-element.38) | data formatting | bytes 2555904 | tf_op jit(solution)/shard_map/jit(_where)/select_n | solution.py:883
  144.7 2.7 %select_n.248 = f32[13,3,8192]{2,1,0:T(4,128)} reshape(f32[1,39,8192]{2,1,0:T(8,128)} %get-tuple-element.37) | data formatting | bytes 2555904 | tf_op jit(solution)/shard_map/jit(_where)/select_n | solution.py:882
  147.4 0.7 fusion.61
  148.1 0.7 compare_and_fusion.4
  148.8 1.2 iota_compare_fusion.9
  150.6 1.2 compare_and_fusion.2
  151.9 1.2 iota_compare_fusion.13
  153.5 1.2 broadcast.464.clone.1
  154.8 2.1 dynamic_update_slice.28
  156.9 2.1 dynamic_update_slice.29
  159.0 2.1 dynamic_update_slice.30
  161.1 2.1 dynamic_update_slice.31
  163.1 1.6 fusion.58
  165.4 0.9 copy-done.9
  166.5 1.1 fusion.11
  167.6 0.7 fusion.13
  168.3 0.7 copy-done.22
  169.9 2.5 %subtract_bitcast_fusion.1 = (f32[1,10,8192]{2,1,0:T(8,128)}, f32[1,10,8192]{2,1,0:T(8,128)}, f32[1,10,8192]{2,1,0:T(8,128)}) fusion(f32[10,8192]{1,0:T(8,128)S(1)} %get-tuple-element.56, f32[10,8192]{1,0:T(8,128)S(1)} %get-tuple-element.23, f32[10,8192]{1,0:T(8,128)S(1)} %get-tuple-element.57, f32[3,10,8192]{2,1,0:T(8,128)S(1)} %get-tuple-element.100, ...), kind=kLoop, calls=%fused_computation.70 | loop fusion | flops 2539520 | bytes 4259840 | tf_op jit(solution)/shard_map/stack | solution.py:858
  172.4 1.0 multiply_add_fusion.3
  173.5 2.5 %fusion.17 = (f32[1,10,8192]{2,1,0:T(8,128)}, f32[1,10,8192]{2,1,0:T(8,128)}, f32[10,8192]{1,0:T(8,128)}) fusion(f32[10,8192]{1,0:T(8,128)S(1)} %get-tuple-element.36, f32[10,8192]{1,0:T(8,128)S(1)} %get-tuple-element.33, f32[3,10,8192]{2,1,0:T(8,128)S(1)} %get-tuple-element.99, f32[10,8192]{1,0:T(8,128)S(1)} %get-tuple-element.58, ...), kind=kLoop, calls=%fused_computation.53 | loop fusion | flops 2539520 | bytes 4587520 | tf_op jit(solution)/shard_map/stack | solution.py:871
  176.0 1.3 fusion.47
  178.1 0.7 copy.91
  178.8 0.7 copy.90
  180.1 0.7 slice_bitcast_fusion.6
  181.4 0.7 copy.88
  182.1 1.2 fusion.41
  184.0 0.7 slice_bitcast_fusion.7
  186.5 0.7 broadcast_select_fusion.3
  187.5 3.0 %fusion.2 = f32[3,10,8192]{2,1,0:T(8,128)S(1)} fusion(f32[13,3,8192]{2,1,0:T(4,128)} %select_n.251, f32[13,4,8192]{2,1,0:T(4,128)} %copy-done.6, f32[13,3,8192]{2,1,0:T(4,128)} %select_n.248, f32[1,10,8192]{2,1,0:T(8,128)} %get-tuple-element.30, f32[1,10,8192]{2,1,0:T(8,128)} %get-tuple-element.29, f32[1,10,8192]{2,1,0:T(8,128)} %get-tuple-element.50, ...), kind=kLoop, calls=%fused_computation.18 | loop fusion | flops 3686400 | bytes 6374336 | tf_op jit(solution)/shard_map/jit(_where)/select_n | solution.py:915
  190.8 0.8 copy-done.12
  192.4 2.0 multiply_add_fusion.1
  194.4 2.1 slice_select_fusion.3
  196.5 0.8 slice.537
  197.4 2.4 %fusion.15 = (f32[1,10,8192]{2,1,0:T(8,128)}, f32[1,10,8192]{2,1,0:T(8,128)}) fusion(f32[10,8192]{1,0:T(8,128)S(1)} %copy-done.16, f32[10,8192]{1,0:T(8,128)S(1)} %get-tuple-element.41, f32[10,8192]{1,0:T(8,128)S(1)} %get-tuple-element.39, f32[3,10,8192]{2,1,0:T(8,128)S(1)} %fusion.2, f32[10,8192]{1,0:T(8,128)S(1)} %copy-done.14, ...), kind=kLoop, calls=%fused_computation.49 | loop fusion | flops 2457600 | bytes 3932160 | tf_op jit(solution)/shard_map/stack | solution.py:871
  200.1 1.4 select_select_fusion
  201.7 0.7 slice.552
  202.5 0.7 slice.551
  203.2 0.7 slice.549
  204.0 3.2 %fusion.18 = f32[3,4,8192]{2,1,0:T(4,128)} fusion(f32[3,10,8192]{2,1,0:T(8,128)} %copy-done.10, f32[1,10,8192]{2,1,0:T(8,128)} %get-tuple-element.32, f32[1,10,8192]{2,1,0:T(8,128)} %get-tuple-element.31, f32[1,10,8192]{2,1,0:T(8,128)} %get-tuple-element.63, f32[3,10,8192]{2,1,0:T(8,128)} %select_select_fusion, f32[3,4]{1,0:T(4,128)S(1)} %copy.117, ...), kind=kLoop, calls=%fused_computation.81 | loop fusion | flops 884736 | bytes 2203888 | tf_op jit(solution)/shard_map/add | solution.py:916
  207.2 1.1 copy.142
  208.4 1.1 copy.143
  209.5 1.1 copy.144
  (145 shorter events, 14.2 us)
Async XLA Ops:
  0.6 2.2 %copy-start.31 = (f32[4,8192]{1,0:T(4,128)S(1)}, f32[4,8192]{1,0:T(4,128)}, u32[]{:S(2)}) copy-start(f32[4,8192]{1,0:T(4,128)} %param.16) | copy-start | bytes 393220
  0.6 2.2 %copy-start.30 = (f32[3,4,8192]{2,1,0:T(4,128)S(1)}, f32[3,4,8192]{2,1,0:T(4,128)}, u32[]{:S(2)}) copy-start(f32[3,4,8192]{2,1,0:T(4,128)} %param.20) | copy-start | bytes 1179652
  0.7 2.3 %copy-start.32 = (f32[3,4,8192]{2,1,0:T(4,128)S(1)}, f32[3,4,8192]{2,1,0:T(4,128)}, u32[]{:S(2)}) copy-start(f32[3,4,8192]{2,1,0:T(4,128)} %param.21) | copy-start | bytes 1179652
  2.8 1.8 copy-start.25
  3.0 4.7 %copy-start.33 = (s32[4]{0:T(128)S(1)}, s32[4]{0:T(128)}, u32[]{:S(2)}) copy-start(s32[4]{0:T(128)} %param.19) | copy-start | bytes 52
  3.8 31.4 %copy-start.6 = (f32[13,4,8192]{2,1,0:T(4,128)}, f32[13,4,8192]{2,1,0:T(4,128)S(1)}, u32[]{:S(2)}) copy-start(f32[13,4,8192]{2,1,0:T(4,128)S(1)} %get-tuple-element.73) | copy-start | bytes 5111812
  37.8 2.1 copy-start.21
  41.6 3.0 %copy-start.4 = (f32[4,8,4096]{2,1,0:T(8,128)S(1)}, f32[4,8,4096]{2,1,0:T(8,128)}, u32[]{:S(2)}) copy-start(f32[4,8,4096]{2,1,0:T(8,128)} %depth_hbm.1) | copy-start | bytes 1572868
  41.6 3.0 %copy-start.5 = (s32[4]{0:T(128)S(1)}, s32[4]{0:T(128)}, u32[]{:S(2)}) copy-start(s32[4]{0:T(128)} %rows_smem.1) | copy-start | bytes 52
  126.5 1.1 copy-start
  127.7 0.6 copy-start.2
  150.6 14.1 %copy-start.34 = (pred[10]{0:T(512)(128)(4,1)}, pred[10]{0:T(512)(128)(4,1)S(1)}, u32[]{:S(2)}) copy-start(pred[10]{0:T(512)(128)(4,1)S(1)} %get-tuple-element.134) | copy-start | bytes 34
  163.1 1.8 copy-start.7
  163.1 2.3 %copy-start.8 = (f32[13,3,8192]{2,1,0:T(4,128)S(1)}, f32[13,3,8192]{2,1,0:T(4,128)}, u32[]{:S(2)}) copy-start(f32[13,3,8192]{2,1,0:T(4,128)} %select_n.251) | copy-start | bytes 3833860
  163.1 3.2 %copy-start.9 = (f32[13,3,8192]{2,1,0:T(4,128)S(1)}, f32[13,3,8192]{2,1,0:T(4,128)}, u32[]{:S(2)}) copy-start(f32[13,3,8192]{2,1,0:T(4,128)} %select_n.248) | copy-start | bytes 3833860
  164.8 1.7 copy-start.15
  164.8 5.1 %copy-start.11 = (f32[10,8192]{1,0:T(8,128)}, f32[10,8192]{1,0:T(8,128)S(1)}, u32[]{:S(2)}) copy-start(f32[10,8192]{1,0:T(8,128)S(1)} %get-tuple-element.23) | copy-start | bytes 983044
  166.5 3.4 %copy-start.13 = (f32[10,8192]{1,0:T(8,128)}, f32[10,8192]{1,0:T(8,128)S(1)}, u32[]{:S(2)}) copy-start(f32[10,8192]{1,0:T(8,128)S(1)} %get-tuple-element.26) | copy-start | bytes 983044
  167.5 1.4 copy-start.22
  168.3 4.2 %copy-start.23 = (f32[10,8192]{1,0:T(8,128)}, f32[10,8192]{1,0:T(8,128)S(1)}, u32[]{:S(2)}) copy-start(f32[10,8192]{1,0:T(8,128)S(1)} %get-tuple-element.21) | copy-start | bytes 983044
  169.6 3.9 %copy-start.10 = (f32[3,10,8192]{2,1,0:T(8,128)}, f32[3,10,8192]{2,1,0:T(8,128)S(1)}, u32[]{:S(2)}) copy-start(f32[3,10,8192]{2,1,0:T(8,128)S(1)} %get-tuple-element.99) | copy-start | bytes 2949124
  169.7 3.8 %copy-start.17 = (f32[10,8192]{1,0:T(8,128)}, f32[10,8192]{1,0:T(8,128)S(1)}, u32[]{:S(2)}) copy-start(f32[10,8192]{1,0:T(8,128)S(1)} %get-tuple-element.56) | copy-start | bytes 983044
  169.7 3.8 %copy-start.19 = (f32[10,8192]{1,0:T(8,128)}, f32[10,8192]{1,0:T(8,128)S(1)}, u32[]{:S(2)}) copy-start(f32[10,8192]{1,0:T(8,128)S(1)} %get-tuple-element.58) | copy-start | bytes 983044
  173.5 3.9 %copy-start.3 = (f32[128,1,128]{2,1,0:T(1,128)S(1)}, f32[128,1,128]{2,1,0:T(1,128)}, u32[]{:S(2)}) copy-start(f32[128,1,128]{2,1,0:T(1,128)} %copy-done.2) | copy-start | bytes 196612
  187.5 3.3 %copy-start.26 = (f32[10,8192]{1,0:T(8,128)S(1)}, f32[10,8192]{1,0:T(8,128)}, u32[]{:S(2)}) copy-start(f32[10,8192]{1,0:T(8,128)} %get-tuple-element.54) | copy-start | bytes 983044
  187.5 3.3 %copy-start.27 = (f32[10,8192]{1,0:T(8,128)S(1)}, f32[10,8192]{1,0:T(8,128)}, u32[]{:S(2)}) copy-start(f32[10,8192]{1,0:T(8,128)} %get-tuple-element.55) | copy-start | bytes 983044
  190.5 1.0 copy-start.12
  190.5 1.2 copy-start.14
  190.6 1.3 copy-start.16
  190.6 1.5 copy-start.18
  190.6 1.6 copy-start.20
  190.6 1.8 copy-start.24
  192.4 2.1 copy-start.28
  192.4 2.1 copy-start.29
  204.0 3.2 %copy-start.1 = (f32[4,3,8,4096]{3,2,1,0:T(8,128)S(1)}, f32[4,3,8,4096]{3,2,1,0:T(8,128)}, u32[]{:S(2)}) copy-start(f32[4,3,8,4096]{3,2,1,0:T(8,128)} %copy-done) | copy-start | bytes 4718596

commit v2 on v1

--- a/solution.py
+++ b/solution.py
@@ -44,6 +44,34 @@
     return ahead, behind
 
 
+def rates(shifted, bed):
+    (e, ee, ew, en, es), (u, ue, uw, un, us), (v, ve, vw, vn, vs) = shifted
+    ux, uy, vx, vy = ue - uw, un - us, ve - vw, vn - vs
+    changes = (
+        HALF * (bed * (ux + vy) + (ee * ue - ew * uw) + (en * vn - es * vs)),
+        HALF * (u * ux + v * uy + (ee - ew)) + DRAG * u,
+        HALF * (u * vx + v * vy + (en - es)) + DRAG * v,
+    )
+    return changes, (ux, uy, vx, vy)
+
+
+def pulled(wides, e, v, dy, slopes):
+    wae, wau, wav, wu, wbed = wides
+    width = wae.shape[1] - 2 * TILE
+    ae, au, av, u, bed = [wide[:, TILE : TILE + width] for wide in wides]
+    ux, uy, vx, vy = slopes
+
+    def dx(field):
+        ahead, behind = column_shifts(field, width)
+        return ahead - behind
+
+    xe, ye = dx(wae), dy(ae, 0)
+    ge = u * xe + v * ye + dx(wau) + dy(av, 1)
+    gu = dx(wbed * wae + wu * wau) + dy(v * au, 2) + e * xe - ux * au - vx * av - 0.1 * au
+    gv = dy(bed * ae + v * av, 3) + dx(wu * wav) + e * ye - uy * au - vy * av - 0.1 * av
+    return ge, gu, gv
+
+
 def split3(value):
     high = value.astype(jnp.bfloat16)
     rest = value - high.astype(jnp.float32)
@@ -61,7 +89,11 @@
     rows_smem,
     win_hbm,
     frame_hbm,
-    halo_hbm,
+    strip0,
+    strip1,
+    strip2,
+    strip3,
+    strip4,
     old_hbm,
     now_hbm,
     depth_hbm,
@@ -72,7 +104,11 @@
     gnow_out,
     edge_out,
     back_out,
-    halo_out,
+    halo0,
+    halo1,
+    halo2,
+    halo3,
+    halo4,
     old,
     now,
     nxt,
@@ -112,6 +148,8 @@
     ag_recv,
     t_send,
     t_recv,
+    strip_send,
+    strip_recv,
 ):
     me = lax.axis_index("rows")
     up = lax.rem(me + 1, n)
@@ -337,19 +375,11 @@
                 shifted.append(
                     (mid_block,) + column_shifts(block, CHUNK) + row_shifts(mid_block, before, after)
                 )
-            (e, ee, ew, en, es), (u, ue, uw, un, us), (v, ve, vw, vn, vs) = shifted
-            bed = depth[nested, :, inner]
-            ux, uy, vx, vy = ue - uw, un - us, ve - vw, vn - vs
-            slopes[0, nested, :, plain] = ux
-            slopes[1, nested, :, plain] = uy
-            slopes[2, nested, :, plain] = vx
-            slopes[3, nested, :, plain] = vy
-            news = (
-                base(0, inner, plain)
-                - HALF * (bed * (ux + vy) + (ee * ue - ew * uw) + (en * vn - es * vs)),
-                base(1, inner, plain) - HALF * (u * ux + v * uy + (ee - ew)) - DRAG * u,
-                base(2, inner, plain) - HALF * (u * vx + v * vy + (en - es)) - DRAG * v,
-            )
+            changes, found = rates(shifted, depth[nested, :, inner])
+            for index, slope in enumerate(found):
+                slopes[index, nested, :, plain] = slope
+            bases = [base(part, inner, plain) for part in range(3)]
+            news = [start - change for start, change in zip(bases, changes)]
             for part in range(3):
                 target(part, inner, plain, news[part], j)
             return carry
@@ -549,16 +579,9 @@
             wide = pl.ds(here, CHUNK + 2 * TILE)
             plain = pl.ds(here, CHUNK)
             inner = pl.ds(here + TILE, CHUNK)
-            cut = slice(TILE, TILE + CHUNK)
-            wae, wau, wav = [cots[nested, part, :, wide] for part in range(3)]
-            wu = state[nested, 1, :, wide]
-            wbed = depth[nested, :, wide]
-            ae, au, av, u, bed = wae[:, cut], wau[:, cut], wav[:, cut], wu[:, cut], wbed[:, cut]
+            wides = [cots[nested, part, :, wide] for part in range(3)]
+            wides += [state[nested, 1, :, wide], depth[nested, :, wide]]
             e, v = state[nested, 0, :, inner], state[nested, 2, :, inner]
-
-            def dx(field):
-                ahead, behind = column_shifts(field, CHUNK)
-                return ahead - behind
 
             def dy(field, index):
                 before = halo_rows[stage, nested, 0, index : index + 1, plain] * has_before
@@ -566,25 +589,8 @@
                 ahead, behind = row_shifts(field, before, after)
                 return ahead - behind
 
-            xe, ye = dx(wae), dy(ae, 0)
-            ge = u * xe + v * ye + dx(wau) + dy(av, 1)
-            gu = (
-                dx(wbed * wae + wu * wau)
-                + dy(v * au, 2)
-                + e * xe
-                - slopes[0, nested, :, plain] * au
-                - slopes[2, nested, :, plain] * av
-                - 0.1 * au
-            )
-            gv = (
-                dy(bed * ae + v * av, 3)
-                + dx(wu * wav)
-                + e * ye
-                - slopes[1, nested, :, plain] * au
-                - slopes[3, nested, :, plain] * av
-                - 0.1 * av
-            )
-            target(inner, plain, j, (ge, gu, gv))
+            grads = pulled(wides, e, v, dy, [slopes[i, nested, :, plain] for i in range(4)])
+            target(inner, plain, j, grads)
             return carry
 
         lax.fori_loop(0, C_COLS // CHUNK, chunk, 0)
@@ -681,14 +687,22 @@
             placed.at[pl.ds(EDGE + me * P_ROWS - 2, 8)], back_out.at[me - BACK_FIRST], t_recv.at[4]
         ).start()
 
-    ocean_up = pltpu.make_async_remote_copy(
-        halo_hbm.at[1], halo_out.at[0], load_sem.at[7], load_sem.at[8], device_id=(up,), device_id_type=MESH
-    )
-    ocean_down = pltpu.make_async_remote_copy(
-        halo_hbm.at[0], halo_out.at[1], load_sem.at[9], load_sem.at[10], device_id=(down,), device_id_type=MESH
-    )
-    ocean_up.start()
-    ocean_down.start()
+    ocean_copies = []
+    for index, (strip, halo) in enumerate(
+        zip((strip0, strip1, strip2, strip3, strip4), (halo0, halo1, halo2, halo3, halo4))
+    ):
+        for side, target in ((0, up), (1, down)):
+            ocean_copies.append(
+                pltpu.make_async_remote_copy(
+                    strip,
+                    halo.at[side],
+                    strip_send.at[index, side],
+                    strip_recv.at[index, side],
+                    device_id=(target,),
+                    device_id_type=MESH,
+                )
+            )
+            ocean_copies[-1].start()
 
     def stage_e(nested, carry):
         halo_wait(3, nested)
@@ -709,8 +723,8 @@
     store_edges = pltpu.make_async_copy(edges, edge_out, store_sem.at[3])
     store_edges.start()
 
-    ocean_up.wait()
-    ocean_down.wait()
+    for copy in ocean_copies:
+        copy.wait()
     pltpu.make_async_copy(back_out, back_out, t_recv.at[4]).wait()
     for store in (store_next, store_gold, store_gnow, store_edges):
         store.wait()
@@ -758,7 +772,7 @@
         pltpu.make_async_copy(pairs, pairs, t_send.at[3]).wait()
 
 
-def coastal(n, child_rows, win, frame, halo, old, now, depth, mid, end):
+def coastal(n, child_rows, win, frame, strips, old, now, depth, mid, end):
     f32 = jnp.float32
     anywhere = pl.BlockSpec(memory_space=pl.ANY)
     grid_shape = (NCHILD, 3, C_ROWS, C_COLS)
@@ -771,10 +785,10 @@
         + [
             jax.ShapeDtypeStruct((n, 1, TILE), f32),
             jax.ShapeDtypeStruct((BACK, 8, 2, TILE), f32),
-            jax.ShapeDtypeStruct(halo.shape, f32),
-        ],
-        in_specs=[pl.BlockSpec(memory_space=pltpu.SMEM)] + [anywhere] * 8,
-        out_specs=[anywhere] * 6,
+        ]
+        + [jax.ShapeDtypeStruct((2,) + strip.shape, f32) for strip in strips],
+        in_specs=[pl.BlockSpec(memory_space=pltpu.SMEM)] + [anywhere] * 12,
+        out_specs=[anywhere] * 10,
         scratch_shapes=[
             pltpu.VMEM(grid_shape, f32),
             pltpu.VMEM(wide_shape, f32),
@@ -807,7 +821,7 @@
             pltpu.VMEM((NCHILD, 8, FOOT_COLS), f32),
             pltpu.VMEM((n, 1, TILE), f32),
             pltpu.VMEM((1, TILE), f32),
-            dma((11,)),
+            dma((7,)),
             dma((4,)),
             dma((4, NCHILD, 2)),
             dma((4, NCHILD, 2)),
@@ -815,107 +829,263 @@
             dma((2,)),
             dma((5,)),
             dma((5,)),
+            dma((5, 2)),
+            dma((5, 2)),
         ],
         compiler_params=pltpu.CompilerParams(
             collective_id=0, has_side_effects=True, vmem_limit_bytes=48 * 1024 * 1024
         ),
-    )(child_rows, win, frame, halo, old, now, depth, mid, end)
-
-
-def windows(parent_old, parent_now, parent_depth, cot_mid, cot_end, child_cols):
-    fields = jnp.concatenate(
-        [cot_end, cot_mid, parent_now, parent_old[2:], parent_depth[None]], axis=0
-    )
-    parts = []
+    )(child_rows, win, frame, *strips, old, now, depth, mid, end)
+
+
+def window_kernel(cols, old, now, depth, mid, end, win, frame):
+    lane = lax.broadcasted_iota(jnp.int32, (P_ROWS, TILE), 1)
+    packet = jnp.zeros((P_ROWS, TILE), jnp.float32)
+    reach = FOOT_COLS + 2 * TILE
+    halves = FOOT_COLS // UNIT
     for nested in range(NCHILD):
-        parts.append(lax.dynamic_slice_in_dim(fields, child_cols[nested], FOOT_COLS, 2))
-    win = jnp.stack(parts, axis=1)
-    win = win.reshape(FIELDS, NCHILD, P_ROWS, FOOT_COLS // UNIT, UNIT)
-    win = jnp.transpose(win, (0, 1, 3, 2, 4)).reshape(UNITS, P_ROWS, 1, UNIT)
-    padded = jnp.pad(parent_now, ((0, 0), (0, 0), (1, 1)))
-    packet = []
+        left = cols[nested]
+        start = jnp.clip((left - 2) // TILE * TILE, 0, P_COLS - reach)
+        start = pl.multiple_of(start, TILE)
+        shift = reach - (left - start)
+
+        def turned(ref, part):
+            if part is None:
+                block = ref[:, pl.ds(start, reach)]
+            else:
+                block = ref[part, :, pl.ds(start, reach)]
+            return pltpu.roll(block, shift, 1)
+
+        lists = [(end, i) for i in range(3)] + [(mid, i) for i in range(3)]
+        lists += [(now, i) for i in range(3)] + [(old, 2), (depth, None), (old, 0), (old, 1)]
+        blocks = [turned(*item) for item in lists]
+        for field in range(FIELDS):
+            for half in range(halves):
+                unit = (field * NCHILD + nested) * halves + half
+                for row in range(P_ROWS):
+                    win[unit, row] = blocks[field][row : row + 1, half * UNIT : (half + 1) * UNIT]
+        first_ok = jnp.where(left >= 2, 1.0, 0.0)
+        last_ok = jnp.where(left + FOOT_COLS + 1 < P_COLS, 1.0, 0.0)
+        for side, lanes in enumerate(((reach - 2, reach - 1, 0), (FOOT_COLS - 1, FOOT_COLS, FOOT_COLS + 1))):
+            cells = []
+            for part in range(3):
+                for which, at in enumerate(lanes):
+                    cell = blocks[6 + part][:, at : at + 1]
+                    if side == 0 and which == 0:
+                        cell = cell * first_ok
+                    if side == 1 and which == 2:
+                        cell = cell * last_ok
+                    cells.append(cell)
+            at = lanes[1]
+            for index in (11, 12, 9, 10, 0, 1, 2):
+                cells.append(blocks[index][:, at : at + 1])
+            for index, cell in enumerate(cells):
+                packet = jnp.where(lane == 32 * nested + 16 * side + index, cell, packet)
+    for row in range(P_ROWS):
+        frame[row] = packet[row : row + 1]
+
+
+def windows(old, now, depth, mid, end, child_cols):
+    f32 = jnp.float32
+    return pl.pallas_call(
+        window_kernel,
+        out_shape=[
+            jax.ShapeDtypeStruct((UNITS, P_ROWS, 1, UNIT), f32),
+            jax.ShapeDtypeStruct((P_ROWS, 1, TILE), f32),
+        ],
+        in_specs=[pl.BlockSpec(memory_space=pltpu.SMEM)] + [pl.BlockSpec(memory_space=pltpu.VMEM)] * 5,
+        out_specs=[pl.BlockSpec(memory_space=pltpu.VMEM)] * 2,
+        compiler_params=pltpu.CompilerParams(vmem_limit_bytes=32 * 1024 * 1024),
+    )(child_cols, old, now, depth, mid, end)
+
+
+def ocean_kernel(
+    n,
+    rows,
+    cols,
+    edges,
+    back,
+    old,
+    now,
+    depth,
+    mid,
+    end,
+    old_halo,
+    now_halo,
+    depth_halo,
+    mid_halo,
+    end_halo,
+    state3,
+    cot2,
+    cot1,
+    now8,
+    depth8,
+    second,
+    a2,
+    a1,
+    slopes1,
+    means,
+    cells,
+):
+    me = lax.axis_index("rows")
+    has_before = jnp.where(me > 0, 1.0, 0.0)
+    has_after = jnp.where(me < n - 1, 1.0, 0.0)
+    ends = (slice(0, TILE), slice(TILE + P_COLS, P_COLS + 2 * TILE))
+    for array in (now8, second, a2, a1):
+        for lanes in ends:
+            array[:, :, lanes] = jnp.zeros((3, 8, TILE), jnp.float32)
+    for lanes in ends:
+        depth8[:, lanes] = jnp.zeros((8, TILE), jnp.float32)
+
+    def tall(own, halo, part, plain):
+        index = () if part is None else (part,)
+        below = halo[(0,) + index + (slice(2, 4), plain)] * has_before
+        above = halo[(1,) + index + (slice(0, 2), plain)] * has_after
+        return jnp.concatenate([below, own[index + (slice(None), plain)], above], axis=0)
+
+    row8 = me * P_ROWS - 2 + lax.broadcasted_iota(jnp.int32, (8, 1), 0)
     for nested in range(NCHILD):
-        for column in (child_cols[nested] - 1, child_cols[nested] + FOOT_COLS):
-            around = lax.dynamic_slice_in_dim(padded, column, 3, 2)
-            packet.append(jnp.transpose(around, (1, 0, 2)).reshape(P_ROWS, 9))
-            for array in (parent_old, parent_depth[None], cot_end):
-                packet.append(jnp.transpose(lax.dynamic_slice_in_dim(array, column, 1, 2)[..., 0]))
-    return win, jnp.concatenate(packet, axis=1).reshape(P_ROWS, 1, TILE)
-
-
-def dx(field):
-    padded = jnp.pad(field, [(0, 0)] * (field.ndim - 1) + [(1, 1)])
-    return padded[..., 2:] - padded[..., :-2]
-
-
-def dy(field):
-    padded = jnp.pad(field, [(0, 0)] * (field.ndim - 2) + [(1, 1), (0, 0)])
-    return padded[..., 2:, :] - padded[..., :-2, :]
-
-
-def step(old, state, depth):
-    e, u, v = state
-    return jnp.stack(
-        [
-            old[0] - HALF * (depth * (dx(u) + dy(v)) + dx(e * u) + dy(e * v)),
-            old[1] - HALF * (u * dx(u) + v * dy(u) + dx(e)) - DRAG * u,
-            old[2] - HALF * (u * dx(v) + v * dy(v) + dy(e)) - DRAG * v,
-        ]
-    )
-
-
-def pull(state, cots, depth):
-    e, u, v = state
-    ae, au, av = [HALF * cots[i] for i in range(3)]
-    xe, ye = dx(ae), dy(ae)
-    return jnp.stack(
-        [
-            u * xe + v * ye + dx(au) + dy(av),
-            dx(depth * ae + u * au) + dy(v * au) + e * xe - dx(u) * au - dx(v) * av - 0.1 * au,
-            dy(depth * ae + v * av) + dx(u * av) + e * ye - dy(u) * au - dy(v) * av - 0.1 * av,
-        ]
-    )
-
-
-def ocean(n, halo, own, edges, back, child_rows, child_cols):
-    me = lax.axis_index("rows")
-    before = jnp.where(me > 0, halo[0], 0.0).reshape(13, 3, P_COLS)
-    after = jnp.where(me < n - 1, halo[1], 0.0).reshape(13, 3, P_COLS)
-    tall = jnp.concatenate([before, own, after], axis=1)
-    old, now, depth, mid, end = tall[0:3], tall[3:6], tall[6], tall[7:10], tall[10:13]
-    row = me * P_ROWS - 3 + jnp.arange(10)
-    inside = ((row >= 0) & (row < n * P_ROWS))[:, None]
-    column = jnp.arange(P_COLS)[None, :]
-    back = jnp.transpose(back.reshape(NCHILD, 3, 4, 8, 2, TILE), (4, 0, 1, 3, 2, 5)).reshape(
-        2, NCHILD, 3, 8, FOOT_COLS
-    )
-    back = jnp.pad(back, ((0, 0), (0, 0), (0, 0), (1, 1), (0, 0)))
-    covered = jnp.zeros((10, P_COLS), bool)
-    means = [jnp.zeros((3, 10, P_COLS), jnp.float32) for _ in range(2)]
-    extra = [jnp.zeros((3, 10, P_COLS), jnp.float32) for _ in range(2)]
-    for nested in range(NCHILD):
-        foot = row - child_rows[nested]
-        in_rows = ((foot >= 0) & (foot < FOOT_ROWS))[:, None]
-        left = child_cols[nested]
-        covered = covered | (in_rows & (column >= left) & (column < left + FOOT_COLS))
+        foot = row8 - rows[nested]
+        in_rows = (foot >= 0) & (foot < FOOT_ROWS)
+        lines = jnp.concatenate(
+            [
+                edges[jnp.clip(me * P_ROWS - 2 + t - rows[nested], 0, FOOT_ROWS - 1)]
+                for t in range(8)
+            ],
+            axis=0,
+        )
+        lines = jnp.where(in_rows, lines, 0.0)
+        for side in range(2):
+            for which in range(2):
+                for part in range(3):
+                    at = nested * 16 + side * 8 + 3 * which + part
+                    cells[nested, side, which, part] = jnp.broadcast_to(lines[:, at : at + 1], (8, TILE))
+        shift = cols[nested] - nested * BAND
+        band = slice(nested * BAND, (nested + 1) * BAND)
         for which in range(2):
-            means[which] = lax.dynamic_update_slice_in_dim(means[which], back[which, nested], left, 2)
-        line = edges[jnp.clip(foot, 0, FOOT_ROWS - 1), 0]
-        line = jnp.where(in_rows, line, 0.0)
-        for side, at in ((0, left - 1), (1, left + FOOT_COLS)):
-            for which in range(2):
-                first = nested * 16 + side * 8 + 3 * which
-                cells = jnp.transpose(line[:, first : first + 3])[:, :, None]
-                extra[which] = jnp.where(column == at, cells, extra[which])
-    raw2 = jnp.where(inside, step(old, now, depth), 0.0)
-    state2 = jnp.where(covered, means[0], raw2)
-    state3 = jnp.where(covered, means[1], step(now, state2, depth))
-    cot3 = jnp.where(covered, 0.0, end)
-    cot2 = mid + pull(state2, cot3, depth) + extra[0]
-    cot2 = jnp.where(covered | ~inside, 0.0, cot2)
-    cot1 = cot3 + pull(now, cot2, depth) + extra[1]
-    mine = slice(3, 3 + P_ROWS)
-    return state3[:, mine], cot2[:, mine], cot1[:, mine]
+            for part in range(3):
+                pieces = [back[(nested * 3 + part) * 4 + q, :, which, :] for q in range(4)]
+                pieces.append(jnp.zeros((8, BAND - FOOT_COLS), jnp.float32))
+                means[which, part, :, band] = pltpu.roll(jnp.concatenate(pieces, axis=1), shift, 1)
+
+    def lanes_at(j):
+        here = pl.multiple_of(j * CHUNK, CHUNK)
+        return pl.ds(here, CHUNK), pl.ds(here + TILE, CHUNK), pl.ds(here, CHUNK + 2 * TILE)
+
+    def masks(j):
+        nested = j // (BAND // CHUNK)
+        column = j * CHUNK + lax.broadcasted_iota(jnp.int32, (8, CHUNK), 1)
+        row = me * P_ROWS - 2 + lax.broadcasted_iota(jnp.int32, (8, CHUNK), 0)
+        foot = row - rows[nested]
+        left = cols[nested]
+        covered = (foot >= 0) & (foot < FOOT_ROWS) & (column >= left) & (column < left + FOOT_COLS)
+        inside = (row >= 0) & (row < n * P_ROWS)
+        return covered, inside, nested, column, left
+
+    def assemble(j, carry):
+        plain, inner, wide = lanes_at(j)
+        for part in range(3):
+            now8[part, :, inner] = tall(now, now_halo, part, plain)
+        depth8[:, inner] = tall(depth, depth_halo, None, plain)
+        return carry
+
+    chunks = P_COLS // CHUNK
+    lax.fori_loop(0, chunks, assemble, 0)
+
+    def first_step(j, carry):
+        plain, inner, wide = lanes_at(j)
+        covered, inside, nested, column, left = masks(j)
+        shifted = []
+        for part in range(3):
+            block = now8[part, :, wide]
+            middle = block[:, TILE : TILE + CHUNK]
+            before = now_halo[0, part, 1:2, plain] * has_before
+            after = now_halo[1, part, 2:3, plain] * has_after
+            shifted.append((middle,) + column_shifts(block, CHUNK) + row_shifts(middle, before, after))
+        changes, found = rates(shifted, depth8[:, inner])
+        for index, slope in enumerate(found):
+            slopes1[index, :, plain] = slope
+        for part in range(3):
+            raw = jnp.where(inside, tall(old, old_halo, part, plain) - changes[part], 0.0)
+            second[part, :, inner] = jnp.where(covered, means[0, part, :, plain], raw)
+            a2[part, :, inner] = jnp.where(covered, 0.0, HALF * tall(end, end_halo, part, plain))
+        return carry
+
+    lax.fori_loop(0, chunks, first_step, 0)
+
+    def turn(field):
+        return pltpu.roll(field, 7, 0), pltpu.roll(field, 1, 0)
+
+    def second_step(j, carry):
+        plain, inner, wide = lanes_at(j)
+        covered, inside, nested, column, left = masks(j)
+        shifted = []
+        for part in range(3):
+            block = second[part, :, wide]
+            middle = block[:, TILE : TILE + CHUNK]
+            shifted.append((middle,) + column_shifts(block, CHUNK) + turn(middle))
+        changes, found = rates(shifted, depth8[:, inner])
+        for part in range(3):
+            value = jnp.where(covered, means[1, part, :, plain], now8[part, :, inner] - changes[part])
+            state3[part, :, plain] = value[2:6]
+        add_cots(j, second, a2, found, 0)
+        return carry
+
+    def dy(field, index):
+        ahead, behind = turn(field)
+        return ahead - behind
+
+    def add_cots(j, state, cots, slopes, which):
+        plain, inner, wide = lanes_at(j)
+        covered, inside, nested, column, left = masks(j)
+        wides = [cots[part, :, wide] for part in range(3)] + [state[1, :, wide], depth8[:, wide]]
+        grads = pulled(wides, state[0, :, inner], state[2, :, inner], dy, slopes)
+        for part in range(3):
+            extra = jnp.where(column == left - 1, jnp.concatenate([cells[nested, 0, which, part]] * 4, axis=1), 0.0)
+            extra += jnp.where(
+                column == left + FOOT_COLS, jnp.concatenate([cells[nested, 1, which, part]] * 4, axis=1), 0.0
+            )
+            value = grads[part] + extra
+            if which == 0:
+                value = jnp.where(covered | ~inside, 0.0, tall(mid, mid_halo, part, plain) + value)
+                cot2[part, :, plain] = value[2:6]
+                a1[part, :, inner] = HALF * value
+            else:
+                kept = jnp.where(covered, 0.0, tall(end, end_halo, part, plain))
+                cot1[part, :, plain] = (kept + value)[2:6]
+
+    lax.fori_loop(0, chunks, second_step, 0)
+
+    def last_step(j, carry):
+        plain, inner, wide = lanes_at(j)
+        add_cots(j, now8, a1, [slopes1[i, :, plain] for i in range(4)], 1)
+        return carry
+
+    lax.fori_loop(0, chunks, last_step, 0)
+
+
+def ocean(n, child_rows, child_cols, edges, back, strips, halos):
+    f32 = jnp.float32
+    smem = pl.BlockSpec(memory_space=pltpu.SMEM)
+    vmem = pl.BlockSpec(memory_space=pltpu.VMEM)
+    wide = P_COLS + 2 * TILE
+    return pl.pallas_call(
+        functools.partial(ocean_kernel, n),
+        out_shape=[jax.ShapeDtypeStruct((3, P_ROWS, P_COLS), f32)] * 3,
+        in_specs=[smem] * 2 + [vmem] * 12,
+        out_specs=[vmem] * 3,
+        scratch_shapes=[
+            pltpu.VMEM((3, 8, wide), f32),
+            pltpu.VMEM((8, wide), f32),
+            pltpu.VMEM((3, 8, wide), f32),
+            pltpu.VMEM((3, 8, wide), f32),
+            pltpu.VMEM((3, 8, wide), f32),
+            pltpu.VMEM((4, 8, P_COLS), f32),
+            pltpu.VMEM((2, 3, 8, P_COLS), f32),
+            pltpu.VMEM((NCHILD, 2, 2, 3, 8, TILE), f32),
+        ],
+        compiler_params=pltpu.CompilerParams(vmem_limit_bytes=48 * 1024 * 1024),
+    )(child_rows, child_cols, edges, back, *strips, *halos)
 
 
 def shards(
@@ -933,15 +1103,12 @@
     child_cot_mid,
     child_cot_end,
 ):
-    win, frame = windows(parent_old, parent_now, parent_depth, parent_cot_mid, parent_cot_end, child_cols)
-    own = jnp.concatenate(
-        [parent_old, parent_now, parent_depth[None], parent_cot_mid, parent_cot_end], axis=0
+    strips = (parent_old, parent_now, parent_depth, parent_cot_mid, parent_cot_end)
+    win, frame = windows(*strips, child_cols)
+    child_end, child_gold, child_gnow, edges, back, *halos = coastal(
+        n, child_rows, win, frame, strips, child_old, child_now, child_depth, child_cot_mid, child_cot_end
     )
-    halo = jnp.stack([own[:, 0:3], own[:, 1:4]]).reshape(2, 39, P_COLS)
-    child_end, child_gold, child_gnow, edges, back, halos = coastal(
-        n, child_rows, win, frame, halo, child_old, child_now, child_depth, child_cot_mid, child_cot_end
-    )
-    parent_end, parent_gold, parent_gnow = ocean(n, halos, own, edges, back, child_rows, child_cols)
+    parent_end, parent_gold, parent_gnow = ocean(n, child_rows, child_cols, edges, back, strips, halos)
     return (parent_end, child_end, parent_gold, parent_gnow, child_gold, child_gnow)
 
 

time: 212 us -> 110 us (0.52)
  local copies, waits for them, and re-layouts: 66.2 us -> 12.8 us
  other arithmetic: 40.1 us -> 0 us
  between operations: 22.4 us -> 0.76 us
  Pallas kernels: 81.9 us -> 96.2 us
    dynamic_update_slice x8 -> x0, local copies, waits for them, and re-layouts: 16.6 us -> none  [ocean(): lax.dynamic_update_slice_in_dim(means[which], back[which, nested], left, 2)]
    another operation x6 -> x0, other arithmetic: 12.3 us -> none  [the longest x2 4.97 us: pull(): jnp.stack([u * xe + v * ye + dx(au) + dy(av), dx(depth * ae + u * au) + d...]
    select_n x9 -> x0, other arithmetic: 11.5 us -> none  [the longest x1 3.44 us: ocean(): before = jnp.where(me > 0, halo[0], 0.0).reshape(13, 3, P_COLS)]
    pallas_call x0 -> x2, Pallas kernels: none -> 10.2 us  [the longest x1 8.8 us: ocean(): pl.pallas_call(functools.partial(ocean_kernel, n), out_shape=[jax.ShapeDt...]
    slice x10 -> x0, local copies, waits for them, and re-layouts: 6.86 us -> none  [the longest x7 2.94 us: ocean(): return (state3[:, mine], cot2[:, mine], cot1[:, mine])]
    another operation x6 -> x0, local copies, waits for them, and re-layouts: 6.41 us -> none  [the longest x2 3.73 us: shards(): halo = jnp.stack([own[:, 0:3], own[:, 1:4]]).reshape(2, 39, P_COLS)]
    add x3 -> x0, other arithmetic: 6.22 us -> none  [the longest x1 3.19 us: ocean(): cot1 = cot3 + pull(now, cot2, depth) + extra[1]]
    transpose x25 -> x0, local copies, waits for them, and re-layouts: 6.01 us -> none  [the longest x15 5.81 us: ocean(): cells = jnp.transpose(line[:, first:first + 3])[:, :, None]]
where the time goes in v2:
time: 110 us
  Pallas kernels  96.2 us (87%)
  local copies, waits for them, and re-layouts  12.8 us (12%)
    pallas_call x1, Pallas kernels, coastal(): pl.pallas_call(functools.partial(coastal_kernel, n), out_shape=[jax.Shape...  86.1 us
    unnamed x39, local copies, waits for them, and re-layouts  12.8 us
    pallas_call x1, Pallas kernels, ocean(): pl.pallas_call(functools.partial(ocean_kernel, n), out_shape=[jax.ShapeDt...  8.8 us

profile of v2, /device:TPU:0, one launch (start us, length us, event | category | flops | bytes accessed | tf_op | source)
XLA Modules:
  0.0 109.8 jit_solution(7116427970459144984)
XLA Ops:
  0.6 0.0 copy-start
  0.6 1.0 copy-done
  1.6 0.0 copy-start.2
  1.6 1.0 copy-done.2
  2.6 0.0 copy-start.4
  2.6 1.0 copy-done.4
  3.6 0.0 copy-start.6
  3.6 1.0 copy-done.6
  4.6 0.0 copy-start.8
  4.6 0.9 copy-done.8
  5.5 0.0 copy-start.12
  5.5 0.7 copy-done.12
  6.2 0.0 copy-start.1
  6.2 0.0 copy-start.3
  6.2 0.0 copy-start.5
  6.2 0.0 copy-start.7
  6.2 0.0 copy-start.9
  6.2 0.0 copy-start.14
  6.2 1.4 %shard_map.163 = (f32[88,4,1,256]{3,2,1,0:T(1,128)S(1)}, f32[4,1,128]{2,1,0:T(1,128)S(1)}) custom-call(s32[4]{0:T(128)S(1)} %copy-done.12, f32[3,4,8192]{2,1,0:T(4,128)S(1)} %copy-done, f32[3,4,8192]{2,1,0:T(4,128)S(1)} %copy-done.2, f32[4,8192]{1,0:T(4,128)S(1)} %copy-done.8, f32[3,4,8192]{2,1,0:T(4,128)S(1)} %copy-done.4, f32[3,4,8192]{2,1,0:T(4,128)S(1)} %copy-done.6), custom_call_target="tpu_custom_call" | custom-call | tf_op jit(solution)/shard_map/pallas_call | solution.py:890
  7.6 0.0 copy-done.1
  7.6 0.0 copy-done.3
  7.6 0.0 copy-done.5
  7.6 0.0 copy-done.7
  7.6 0.0 copy-done.9
  7.6 0.0 copy-done.14
  7.6 0.0 copy-start.11
  7.6 1.0 copy-done.11
  8.7 0.0 copy-start.13
  8.7 86.1 %shard_map.164 = (f32[4,3,8,4096]{3,2,1,0:T(8,128)}, f32[4,3,8,4096]{3,2,1,0:T(8,128)}, f32[4,3,8,4096]{3,2,1,0:T(8,128)}, f32[128,1,128]{2,1,0:T(1,128)S(1)}, f...) custom-call(s32[4]{0:T(128)S(1)} %copy-done.14, ...), custom_call_target="tpu_custom_call" | custom-call | tf_op jit(solution)/shard_map/pallas_call | solution.py:782
  94.8 0.0 copy-done.13
  94.8 0.0 copy-start.10
  94.8 1.1 %copy-done.10 = f32[2,3,4,8192]{3,2,1,0:T(4,128)S(1)} copy-done((f32[2,3,4,8192]{3,2,1,0:T(4,128)S(1)}, f32[2,3,4,8192]{3,2,1,0:T(4,128)}, u32[]{:S(2)}) %copy-start.10) | copy-done | bytes 786456
  95.9 0.0 copy-start.17
  95.9 8.8 %shard_map.165 = (f32[3,4,8192]{2,1,0:T(4,128)}, f32[3,4,8192]{2,1,0:T(4,128)}, f32[3,4,8192]{2,1,0:T(4,128)}) custom-call(s32[4]{0:T(128)S(1)} %copy-done.14, s32[4]{0:T(128)S(1)} %copy-done.13, f32[128,1,128]{2,1,0:T(1,128)S(1)} %get-tuple-element.23.edges, f32[48,8,2,128]{3,2,1,0:T(2,128)S(1)} %get-tuple-element.24.back, f32[3,4,8192]{2,1,0:T(4,128)S(1)} %copy-done.1, ...), custom_call_target="tpu_custom_call" | custom-call | tf_op jit(solution)/shard_map/pallas_call | solution.py:1072
  104.7 0.0 copy-done.17
  104.7 0.0 copy-start.16
  104.7 1.1 %copy.21 = f32[4,3,8,4096]{3,2,1,0:T(8,128)} copy(f32[4,3,8,4096]{3,2,1,0:T(8,128)S(1)} %copy-done.17) | data formatting | bytes 3145728
  105.9 0.8 copy-done.16
  106.7 0.0 copy-start.15
  106.7 1.1 %copy.22 = f32[4,3,8,4096]{3,2,1,0:T(8,128)} copy(f32[4,3,8,4096]{3,2,1,0:T(8,128)S(1)} %copy-done.16) | data formatting | bytes 3145728
  107.8 0.8 copy-done.15
  108.7 1.1 %copy.23 = f32[4,3,8,4096]{3,2,1,0:T(8,128)} copy(f32[4,3,8,4096]{3,2,1,0:T(8,128)S(1)} %copy-done.15) | data formatting | bytes 3145728
Async XLA Ops:
  0.6 1.0 copy-start
  1.6 1.0 copy-start.2
  2.6 1.0 copy-start.4
  3.6 1.0 copy-start.6
  4.6 0.9 copy-start.8
  5.5 0.7 copy-start.12
  6.2 1.4 %copy-start.1 = (f32[3,4,8192]{2,1,0:T(4,128)S(1)}, f32[3,4,8192]{2,1,0:T(4,128)}, u32[]{:S(2)}) copy-start(f32[3,4,8192]{2,1,0:T(4,128)} %old.3) | copy-start | bytes 1179652
  6.2 1.4 %copy-start.3 = (f32[3,4,8192]{2,1,0:T(4,128)S(1)}, f32[3,4,8192]{2,1,0:T(4,128)}, u32[]{:S(2)}) copy-start(f32[3,4,8192]{2,1,0:T(4,128)} %now.3) | copy-start | bytes 1179652
  6.2 1.4 %copy-start.5 = (f32[3,4,8192]{2,1,0:T(4,128)S(1)}, f32[3,4,8192]{2,1,0:T(4,128)}, u32[]{:S(2)}) copy-start(f32[3,4,8192]{2,1,0:T(4,128)} %mid.3) | copy-start | bytes 1179652
  6.2 1.4 %copy-start.7 = (f32[3,4,8192]{2,1,0:T(4,128)S(1)}, f32[3,4,8192]{2,1,0:T(4,128)}, u32[]{:S(2)}) copy-start(f32[3,4,8192]{2,1,0:T(4,128)} %end.3) | copy-start | bytes 1179652
  6.2 1.4 %copy-start.9 = (f32[4,8192]{1,0:T(4,128)S(1)}, f32[4,8192]{1,0:T(4,128)}, u32[]{:S(2)}) copy-start(f32[4,8192]{1,0:T(4,128)} %depth.3) | copy-start | bytes 393220
  6.2 1.4 %copy-start.14 = (s32[4]{0:T(128)S(1)}, s32[4]{0:T(128)}, u32[]{:S(2)}) copy-start(s32[4]{0:T(128)} %rows.1) | copy-start | bytes 52
  7.6 1.0 copy-start.11
  8.7 86.1 %copy-start.13 = (s32[4]{0:T(128)S(1)}, s32[4]{0:T(128)}, u32[]{:S(2)}) copy-start(s32[4]{0:T(128)} %cols.3) | copy-start | bytes 52
  94.8 1.1 %copy-start.10 = (f32[2,3,4,8192]{3,2,1,0:T(4,128)S(1)}, f32[2,3,4,8192]{3,2,1,0:T(4,128)}, u32[]{:S(2)}) copy-start(f32[2,3,4,8192]{3,2,1,0:T(4,128)} %get-tuple-element.29.end_halo) | copy-start | bytes 2359300
  95.9 8.8 %copy-start.17 = (f32[4,3,8,4096]{3,2,1,0:T(8,128)S(1)}, f32[4,3,8,4096]{3,2,1,0:T(8,128)}, u32[]{:S(2)}) copy-start(f32[4,3,8,4096]{3,2,1,0:T(8,128)} %get-tuple-element.43) | copy-start | bytes 4718596
  104.7 2.0 %copy-start.16 = (f32[4,3,8,4096]{3,2,1,0:T(8,128)S(1)}, f32[4,3,8,4096]{3,2,1,0:T(8,128)}, u32[]{:S(2)}) copy-start(f32[4,3,8,4096]{3,2,1,0:T(8,128)} %get-tuple-element.46) | copy-start | bytes 4718596
  106.7 2.0 %copy-start.15 = (f32[4,3,8,4096]{3,2,1,0:T(8,128)S(1)}, f32[4,3,8,4096]{3,2,1,0:T(8,128)}, u32[]{:S(2)}) copy-start(f32[4,3,8,4096]{3,2,1,0:T(8,128)} %get-tuple-element.47) | copy-start | bytes 4718596

commit v3 on v1

v3 whole, which is shorter than its diff:
```python
import functools

import jax
import jax.numpy as jnp
from jax import lax
from jax.experimental import pallas as pl
from jax.experimental.pallas import tpu as pltpu
from jax.sharding import PartitionSpec as P

MESH = pl.DeviceIdType.MESH
P_ROWS = 4
P_COLS = 8192
C_ROWS = 8
C_COLS = 4096
NCHILD = 4
RATIO = 8
FOOT_ROWS = 128
FOOT_COLS = 512
BAND = 2048
TILE = 128
PADDED = C_COLS + 2 * TILE
CHUNK = 512
HALF = 0.15
DRAG = 0.015
PARTS = FOOT_COLS // TILE
ROW_UNITS = 6 * NCHILD * PARTS
SIDE_UNITS = 2 * NCHILD * PARTS
SIDE_FIRST = 96
BACK = 3 * NCHILD * PARTS
BACK_FIRST = 80
EDGE = 8


def column_shifts(wide, width):
    ahead = pltpu.roll(wide, wide.shape[1] - 1, 1)[:, TILE : TILE + width]
    behind = pltpu.roll(wide, 1, 1)[:, TILE : TILE + width]
    return ahead, behind


def row_shifts(block, before, after):
    row = lax.broadcasted_iota(jnp.int32, block.shape, 0)
    ahead = jnp.where(row == C_ROWS - 1, after, pltpu.roll(block, C_ROWS - 1, 0))
    behind = jnp.where(row == 0, before, pltpu.roll(block, 1, 0))
    return ahead, behind


def moved_left(block, amount, bits):
    width = block.shape[1]
    amounts = jnp.full(block.shape, amount, jnp.int32)
    for bit in range(bits):
        block = jnp.where((amounts >> bit) & 1 == 1, pltpu.roll(block, width - (1 << bit), 1), block)
    return block


def cut_window(tiles, amount):
    shape = tiles[0].shape
    amounts = jnp.full(shape, amount, jnp.int32)
    blank = jnp.zeros(shape, jnp.float32)
    wanted = PARTS + 3
    for bit, count in ((10, wanted + 7), (9, wanted + 3), (8, wanted + 1), (7, wanted)):
        step = 1 << (bit - 7)
        chosen = (amounts >> bit) & 1 == 1
        tiles = [
            jnp.where(chosen, tiles[q + step] if q + step < len(tiles) else blank, tiles[q])
            for q in range(count)
        ]
    return moved_left(jnp.concatenate(tiles, axis=1), amount, 7)


def rates(shifted, bed):
    (e, ee, ew, en, es), (u, ue, uw, un, us), (v, ve, vw, vn, vs) = shifted
    ux, uy, vx, vy = ue - uw, un - us, ve - vw, vn - vs
    changes = (
        HALF * (bed * (ux + vy) + (ee * ue - ew * uw) + (en * vn - es * vs)),
        HALF * (u * ux + v * uy + (ee - ew)) + DRAG * u,
        HALF * (u * vx + v * vy + (en - es)) + DRAG * v,
    )
    return changes, (ux, uy, vx, vy)


def pulled(wides, e, v, dy, slopes):
    wae, wau, wav, wu, wbed = wides
    width = wae.shape[1] - 2 * TILE
    ae, au, av, u, bed = [wide[:, TILE : TILE + width] for wide in wides]
    ux, uy, vx, vy = slopes

    def dx(field):
        ahead, behind = column_shifts(field, width)
        return ahead - behind

    xe, ye = dx(wae), dy(ae, 0)
    ge = u * xe + v * ye + dx(wau) + dy(av, 1)
    gu = dx(wbed * wae + wu * wau) + dy(v * au, 2) + e * xe - ux * au - vx * av - 0.1 * au
    gv = dy(bed * ae + v * av, 3) + dx(wu * wav) + e * ye - uy * au - vy * av - 0.1 * av
    return ge, gu, gv


def split3(value):
    high = value.astype(jnp.bfloat16)
    rest = value - high.astype(jnp.float32)
    mid = rest.astype(jnp.bfloat16)
    low = (rest - mid.astype(jnp.float32)).astype(jnp.bfloat16)
    return high, mid, low


def exact_dot(rows, matrix):
    return sum(jnp.dot(part, matrix, preferred_element_type=jnp.float32) for part in split3(rows))


def coastal_kernel(n, rows_smem, cols_smem, *refs):
    strips_hbm, refs = refs[:5], refs[5:]
    old_hbm, now_hbm, depth_hbm, mid_hbm, end_hbm = refs[:5]
    next_out, gold_out, gnow_out, pend_out, pgold_out, pgnow_out = refs[5:11]
    (
        old,
        now,
        nxt,
        depth,
        mid,
        end,
        a2,
        a1,
        slopes1,
        slopes2,
        first_send,
        first_halo,
        send_rows,
        halo_rows,
        win,
        side_win,
        frame,
        frames,
        fvals,
        gathered,
        side_gathered,
        picked,
        beside,
        side_picked,
        rowbuf,
        besides,
        side_rows,
        lhs,
        spread,
        sums,
        rest,
        pairs,
        returned,
        placed,
        qrow,
        edges,
        packet,
        p_old,
        p_now,
        p_depth,
        p_mid,
        p_end,
        now8,
        depth8,
        second8,
        a28,
        a18,
        pslopes,
        means,
        cells,
        back,
        pend,
        pgold,
        pgnow,
        ocean_send,
        ocean_halo,
        load_sem,
        store_sem,
        halo_send,
        halo_recv,
        ag_send,
        ag_recv,
        t_send,
        t_recv,
        ocean_send_sem,
        ocean_recv_sem,
    ) = refs[11:]
    me = lax.axis_index("rows")
    up = lax.rem(me + 1, n)
    down = lax.rem(me + n - 1, n)
    has_before = jnp.where(me > 0, 1.0, 0.0)
    has_after = jnp.where(me < n - 1, 1.0, 0.0)
    centre = pl.ds(TILE, C_COLS)

    barrier = pltpu.get_barrier_semaphore()

    def greet(j, carry):
        pl.semaphore_signal(barrier, inc=1, device_id=(lax.rem(me + j, n),), device_id_type=MESH)
        return carry

    lax.fori_loop(1, n, greet, 0)

    strips = (p_old, p_now, p_depth, p_mid, p_end)
    loads = [
        pltpu.make_async_copy(source, target, load_sem.at[index])
        for index, (source, target) in enumerate(
            zip(
                strips_hbm + (now_hbm, depth_hbm, old_hbm, end_hbm, mid_hbm),
                strips + (now.at[:, :, :, centre], depth.at[:, :, centre], old, end, mid),
            )
        )
    ]
    for load in loads:
        load.start()

    for array in (a2, a1):
        array[:, :, :, 0:TILE] = jnp.zeros((NCHILD, 3, C_ROWS, TILE), jnp.float32)
        array[:, :, :, TILE + C_COLS :] = jnp.zeros((NCHILD, 3, C_ROWS, TILE), jnp.float32)
    depth[:, :, 0:TILE] = jnp.zeros((NCHILD, C_ROWS, TILE), jnp.float32)
    depth[:, :, TILE + C_COLS :] = jnp.zeros((NCHILD, C_ROWS, TILE), jnp.float32)
    ocean_rows = n * P_ROWS
    frames[0:EDGE] = jnp.zeros((EDGE, 1, TILE), jnp.float32)
    frames[pl.ds(EDGE + ocean_rows, EDGE)] = jnp.zeros((EDGE, 1, TILE), jnp.float32)
    for array in (gathered, side_gathered):
        array[0:EDGE] = jnp.zeros((EDGE, 1, TILE), jnp.float32)
        array[pl.ds(EDGE + ocean_rows, EDGE)] = jnp.zeros((EDGE, 1, TILE), jnp.float32)
    pad = ocean_rows
    span = FOOT_ROWS
    returned[0:pad] = jnp.zeros((pad, 2, TILE), jnp.float32)
    returned[pl.ds(pad + span, pad)] = jnp.zeros((pad, 2, TILE), jnp.float32)
    for array in (now8, second8, a28, a18):
        for lanes in (slice(0, TILE), slice(TILE + P_COLS, P_COLS + 2 * TILE)):
            array[:, :, lanes] = jnp.zeros((3, 8, TILE), jnp.float32)
        array[:, 6:8, :] = jnp.zeros((3, 2, P_COLS + 2 * TILE), jnp.float32)
    depth8[:, 0:TILE] = jnp.zeros((8, TILE), jnp.float32)
    depth8[:, TILE + P_COLS :] = jnp.zeros((8, TILE), jnp.float32)
    depth8[6:8, :] = jnp.zeros((2, P_COLS + 2 * TILE), jnp.float32)
    qrow[...] = jnp.zeros_like(qrow)
    packet[...] = jnp.zeros_like(packet)

    lane = lax.broadcasted_iota(jnp.int32, (1, TILE), 1)
    whole_ocean = pl.ds(TILE, P_COLS)

    for index in range(5):
        loads[index].wait()

    def band_tiles(nested, blocks):
        first = nested * (BAND // TILE) - 1
        tiles = []
        for q in range(first, first + BAND // TILE + 2):
            if q < 0 or q >= P_COLS // TILE:
                tiles.append(jnp.zeros((P_ROWS * len(blocks), TILE), jnp.float32))
            else:
                tiles.append(jnp.concatenate([block(q) for block in blocks], axis=0))
        return cut_window(tiles, cols_smem[nested] - nested * BAND)

    lane4 = lax.broadcasted_iota(jnp.int32, (P_ROWS, TILE), 1)
    raw_cells = jnp.zeros((P_ROWS, TILE), jnp.float32)
    for nested in range(NCHILD):
        def block_of(ref, part):
            if part is None:
                return lambda q: ref[:, TILE * q : TILE * (q + 1)]
            return lambda q: ref[part, :, TILE * q : TILE * (q + 1)]

        sources = [(p_end, 0), (p_end, 1), (p_end, 2), (p_mid, 0), (p_mid, 1), (p_mid, 2)]
        sources += [(p_now, 0), (p_now, 1), (p_now, 2), (p_old, 0), (p_old, 1), (p_old, 2), (p_depth, None)]
        blocks = []
        for first in range(0, len(sources), 2):
            pair = [block_of(*source) for source in sources[first : first + 2]]
            both = band_tiles(nested, pair)
            blocks += [both[P_ROWS * i : P_ROWS * (i + 1)] for i in range(len(pair))]
        for field in range(6):
            for piece in range(PARTS):
                unit = (field * NCHILD + nested) * PARTS + piece
                for row in range(P_ROWS):
                    win[unit, row] = blocks[field][row : row + 1, (piece + 1) * TILE : (piece + 2) * TILE]
        foot_end = TILE + FOOT_COLS
        for side, lanes in enumerate(
            ((TILE - 2, TILE - 1, TILE), (foot_end - 1, foot_end, foot_end + 1))
        ):
            found = [blocks[6 + part][:, at : at + 1] for part in range(3) for at in lanes]
            at = lanes[1]
            for index in (9, 10, 11, 12, 0, 1, 2):
                found.append(blocks[index][:, at : at + 1])
            for index, cell in enumerate(found):
                raw_cells = jnp.where(lane4 == 32 * nested + 16 * side + index, cell, raw_cells)
    for row in range(P_ROWS):
        frame[row] = raw_cells[row : row + 1]

    for side, row in ((0, 0), (1, P_ROWS - 1)):
        for part in range(3):
            ocean_send[side, part] = p_now[part, row : row + 1, :]
        ocean_send[side, 3] = p_depth[row : row + 1, :]
    loads[5].wait()
    loads[6].wait()
    for nested in range(NCHILD):
        for side, row in ((0, 0), (1, C_ROWS - 1)):
            for part in range(3):
                first_send[nested, side, part] = now[nested, part, row : row + 1, centre]
            first_send[nested, side, 3] = depth[nested, row : row + 1, centre]

    pl.semaphore_wait(barrier, n - 1)

    def remote(source, target, send, recv, device):
        return pltpu.make_async_remote_copy(
            source, target, send, recv, device_id=(device,), device_id_type=MESH
        )

    def ocean_copies(first, count, stage):
        fields = pl.ds(first, count)
        return (
            remote(
                ocean_send.at[0, fields],
                ocean_halo.at[1, fields],
                ocean_send_sem.at[stage, 0],
                ocean_recv_sem.at[stage, 1],
                down,
            ),
            remote(
                ocean_send.at[1, fields],
                ocean_halo.at[0, fields],
                ocean_send_sem.at[stage, 1],
                ocean_recv_sem.at[stage, 0],
                up,
            ),
        )

    ocean_stages = ((0, 4, 0), (4, 6, 1), (10, 3, 2))

    def ocean_start(stage):
        for copy in ocean_copies(*ocean_stages[stage]):
            copy.start()

    def ocean_wait(stage):
        for copy in ocean_copies(*ocean_stages[stage]):
            copy.wait_recv()

    def halo_copies(stage, nested):
        if stage == 0:
            sources = (first_send.at[nested, 0], first_send.at[nested, 1])
            targets = (first_halo.at[nested, 1], first_halo.at[nested, 0])
        else:
            sources = (send_rows.at[stage - 1, nested, 0], send_rows.at[stage - 1, nested, 1])
            targets = (halo_rows.at[stage - 1, nested, 1], halo_rows.at[stage - 1, nested, 0])
        return (
            remote(sources[0], targets[0], halo_send.at[stage, nested, 0], halo_recv.at[stage, nested, 1], down),
            remote(sources[1], targets[1], halo_send.at[stage, nested, 1], halo_recv.at[stage, nested, 0], up),
        )

    def halo_row(stage, nested, side, part, plain):
        kept = has_before if side == 0 else has_after
        if stage == 0:
            return first_halo[nested, side, part, :, plain] * kept
        return halo_rows[stage - 1, nested, side, part, :, plain] * kept

    def put_row(stage, nested, part, plain, value):
        send_rows[stage - 1, nested, 0, part, :, plain] = value[0:1]
        send_rows[stage - 1, nested, 1, part, :, plain] = value[C_ROWS - 1 :]

    def halo_start(stage, nested):
        for copy in halo_copies(stage, nested):
            copy.start()

    def halo_wait(stage, nested):
        for copy in halo_copies(stage, nested):
            copy.wait_recv()

    mine = pl.ds(EDGE + me * P_ROWS, P_ROWS)
    frames[mine] = frame[...]
    def deal(count, first, source, target, send, recv):
        own = (me >= first) & (me < first + count)
        place = lax.rem(me + (n // count + 1) * count - first, count)

        def one(j, carry):
            unit = lax.rem(place + j, count)
            remote(source(unit), target, send, recv, first + unit).start()
            return carry

        lax.fori_loop(jnp.where(own, 1, 0), count, one, 0)

        @pl.when(own)
        def _():
            pltpu.make_async_copy(source(place), target, recv).start()

    def every(source, target, send, recv):
        def one(j, carry):
            other = lax.rem(me + j, n)
            remote(source(other), target, send, recv, other).start()
            return carry

        lax.fori_loop(1, n, one, 0)

    def grid_first(grid_index):
        first = rows_smem[0]
        for nested in range(1, NCHILD):
            first = jnp.where(grid_index == nested, rows_smem[nested], first)
        return first

    deal(ROW_UNITS, 0, lambda unit: win.at[unit], gathered.at[mine], t_send.at[0], t_recv.at[0])
    every(lambda other: frame, frames.at[mine], ag_send.at[0], ag_recv.at[0])
    ocean_start(0)
    for nested in range(NCHILD):
        halo_start(0, nested)

    @pl.when(me < ROW_UNITS)
    def _():
        whole = gathered.at[pl.ds(EDGE, ocean_rows)]
        pltpu.make_async_copy(whole, whole, t_recv.at[0]).wait()
        first = grid_first(lax.rem(me // PARTS, NCHILD))
        picked[...] = gathered[pl.ds(EDGE + first, FOOT_ROWS)]
        every(lambda other: picked.at[other], rowbuf.at[me], t_send.at[2], t_recv.at[2])
        pltpu.make_async_copy(picked.at[me], rowbuf.at[me], t_recv.at[2]).start()

        @pl.when(me < ROW_UNITS // 2)
        def _():
            beside[0:1] = gathered[pl.ds(EDGE + first - 1, 1)]
            beside[1:2] = gathered[pl.ds(EDGE + first + FOOT_ROWS, 1)]
            for side, target in ((0, 0), (1, n - 1)):

                @pl.when(me != target)
                def _():
                    remote(beside.at[side], besides.at[me], t_send.at[1], t_recv.at[1], target).start()

                @pl.when(me == target)
                def _():
                    pltpu.make_async_copy(beside.at[side], besides.at[me], t_recv.at[1]).start()

    def ocean_lanes(j):
        here = pl.multiple_of(j * CHUNK, CHUNK)
        return pl.ds(here, CHUNK), pl.ds(here + TILE, CHUNK), pl.ds(here, CHUNK + 2 * TILE)

    def ocean_edge(side, field, plain):
        return ocean_halo[side, field, :, plain] * (has_before if side == 0 else has_after)

    def put8(array, part, inner, own, field, plain):
        array[part, 1:5, inner] = own
        if field is not None:
            array[part, 0:1, inner] = ocean_edge(0, field, plain)
            array[part, 5:6, inner] = ocean_edge(1, field, plain)

    chunks = P_COLS // CHUNK
    ocean_wait(0)

    def assemble(j, carry):
        plain, inner, wide = ocean_lanes(j)
        for part in range(3):
            put8(now8, part, inner, p_now[part, :, plain], part, plain)
        depth8[1:5, inner] = p_depth[:, plain]
        depth8[0:1, inner] = ocean_edge(0, 3, plain)
        depth8[5:6, inner] = ocean_edge(1, 3, plain)
        return carry

    lax.fori_loop(0, chunks, assemble, 0)

    def turn(field):
        return pltpu.roll(field, 7, 0), pltpu.roll(field, 1, 0)

    def ocean_rates(state, j):
        plain, inner, wide = ocean_lanes(j)
        shifted = []
        for part in range(3):
            block = state[part, :, wide]
            middle = block[:, TILE : TILE + CHUNK]
            shifted.append((middle,) + column_shifts(block, CHUNK) + turn(middle))
        return rates(shifted, depth8[:, inner])

    def ocean_first(j, carry):
        plain, inner, wide = ocean_lanes(j)
        changes, found = ocean_rates(now8, j)
        for index, slope in enumerate(found):
            pslopes[index, :, plain] = slope
        for part in range(3):
            second8[part, 1:5, inner] = p_old[part, :, plain] - changes[part][1:5]
        return carry

    lax.fori_loop(0, chunks, ocean_first, 0)

    for nested in range(NCHILD):
        def first_product(q):
            tile = slice(TILE * q, TILE * (q + 1))
            return second8[2, 1:5, TILE * (q + 1) : TILE * (q + 2)] * p_end[1, :, tile]

        def second_product(q):
            tile = slice(TILE * q, TILE * (q + 1))
            v_2 = second8[2, 1:5, TILE * (q + 1) : TILE * (q + 2)]
            return p_depth[:, tile] * p_end[0, :, tile] + v_2 * p_end[2, :, tile]

        value = band_tiles(nested, (first_product, second_product))
        for which in range(2):
            for piece in range(PARTS):
                unit = (which * NCHILD + nested) * PARTS + piece
                for row in range(P_ROWS):
                    at = which * P_ROWS + row
                    side_win[unit, row] = value[at : at + 1, (piece + 1) * TILE : (piece + 2) * TILE]
    deal(SIDE_UNITS, SIDE_FIRST, lambda unit: side_win.at[unit], side_gathered.at[mine], t_send.at[5], t_recv.at[5])

    all_but = frames.at[pl.ds(0, (n - 1) * P_ROWS)]
    pltpu.make_async_copy(all_but, all_but, ag_recv.at[0]).wait()

    def lanes_of(offset):
        value = frames[EDGE + rows_smem[0] + me + offset]
        for nested in range(1, NCHILD):
            other = frames[EDGE + rows_smem[nested] + me + offset]
            value = jnp.where(lane >= 32 * nested, other, value)
        return value

    south, middle, north = lanes_of(-1), lanes_of(0), lanes_of(1)

    def lane_field(row, index):
        return row if index == 0 else pltpu.roll(row, TILE - index, 1)

    e_w, e_c, e_e = [lane_field(middle, i) for i in (0, 1, 2)]
    u_w, u_c, u_e = [lane_field(middle, i) for i in (3, 4, 5)]
    v_w, v_c, v_e = [lane_field(middle, i) for i in (6, 7, 8)]
    e_s, u_s, v_s = [lane_field(south, i) for i in (1, 4, 7)]
    e_n, u_n, v_n = [lane_field(north, i) for i in (1, 4, 7)]
    e_o, u_o, v_o, b_c, ce_c, cu_c, cv_c = [lane_field(middle, i) for i in range(9, 16)]
    e_2 = e_o - HALF * (
        b_c * ((u_e - u_w) + (v_n - v_s)) + (e_e * u_e - e_w * u_w) + (e_n * v_n - e_s * v_s)
    )
    u_2 = u_o - HALF * (u_c * (u_e - u_w) + v_c * (u_n - u_s) + (e_e - e_w)) - DRAG * u_c
    v_2 = v_o - HALF * (u_c * (v_e - v_w) + v_c * (v_n - v_s) + (e_n - e_s)) - DRAG * v_c
    for index, value in enumerate((e_c, u_c, v_c, e_2, u_2, v_2, b_c, ce_c, cu_c, cv_c)):
        fvals[index : index + 1, :] = value
    for nested in range(NCHILD):
        for side in range(2):
            where = 32 * nested + 16 * side
            lanes = slice(0, TILE) if side == 0 else slice(TILE + C_COLS, PADDED)
            for part in range(3):
                for base, array in ((0, now), (3, nxt)):
                    cell = fvals[base + part : base + part + 1, where : where + 1]
                    array[nested, part, :, lanes] = jnp.broadcast_to(cell, (C_ROWS, TILE))

    def forward(stage, nested, state, base, target, slopes):
        def chunk(j, carry):
            here = pl.multiple_of(j * CHUNK, CHUNK)
            wide = pl.ds(here, CHUNK + 2 * TILE)
            plain = pl.ds(here, CHUNK)
            inner = pl.ds(here + TILE, CHUNK)
            shifted = []
            for part in range(3):
                block = state[nested, part, :, wide]
                mid_block = block[:, TILE : TILE + CHUNK]
                before = halo_row(stage, nested, 0, part, plain)
                after = halo_row(stage, nested, 1, part, plain)
                shifted.append(
                    (mid_block,) + column_shifts(block, CHUNK) + row_shifts(mid_block, before, after)
                )
            changes, found = rates(shifted, depth[nested, :, inner])
            for index, slope in enumerate(found):
                slopes[index, nested, :, plain] = slope
            bases = [base(part, inner, plain) for part in range(3)]
            news = [start - change for start, change in zip(bases, changes)]
            for part in range(3):
                target(part, inner, plain, news[part], j)
            return carry

        lax.fori_loop(0, C_COLS // CHUNK, chunk, 0)

    def add_sums(which, nested, part, value, j):
        row = (nested * 3 + part) * 4 + j // 2
        sums[which, pl.ds(row, 1), pl.ds(pl.multiple_of(lax.rem(j, 2) * CHUNK, CHUNK), CHUNK)] = (
            jnp.sum(value, axis=0, keepdims=True)
        )

    def stage_a(nested, carry):
        halo_wait(0, nested)

        def target(part, inner, plain, value, j):
            nxt[nested, part, :, inner] = value
            put_row(1, nested, part, plain, value)
            add_sums(0, nested, part, value, j)

        forward(0, nested, now, lambda part, inner, plain: old[nested, part, :, plain], target, slopes1)
        halo_start(1, nested)
        return carry

    for index in (7, 8, 9):
        loads[index].wait()
    lax.fori_loop(0, NCHILD, stage_a, 0)

    def stage_b(nested, carry):
        halo_wait(1, nested)

        def target(part, inner, plain, value, j):
            old[nested, part, :, plain] = value
            add_sums(1, nested, part, value, j)

        forward(1, nested, nxt, lambda part, inner, plain: now[nested, part, :, inner], target, slopes2)
        return carry

    lax.fori_loop(0, NCHILD, stage_b, 0)
    store_next = pltpu.make_async_copy(old, next_out, store_sem.at[0])
    store_next.start()

    fine = lax.broadcasted_iota(jnp.int32, (RATIO * TILE, TILE), 0) // RATIO
    coarse = lax.broadcasted_iota(jnp.int32, (RATIO * TILE, TILE), 1)
    gather_matrix = jnp.where(fine == coarse, 1.0 / (RATIO * RATIO), 0.0).astype(jnp.bfloat16)
    fine_t = lax.broadcasted_iota(jnp.int32, (TILE, RATIO * TILE), 1) // RATIO
    coarse_t = lax.broadcasted_iota(jnp.int32, (TILE, RATIO * TILE), 0)
    spread_matrix = jnp.where(fine_t == coarse_t, 1.0 / (RATIO * RATIO), 0.0).astype(jnp.bfloat16)
    for which in range(2):
        rest[which] = exact_dot(sums[which], gather_matrix)
    for unit in range(BACK):
        for which in range(2):
            pairs[unit, which : which + 1, :] = rest[which, unit : unit + 1, :]

    deal(BACK, BACK_FIRST, lambda unit: pairs.at[unit], returned.at[pad + me], t_send.at[3], t_recv.at[3])

    @pl.when(me >= SIDE_FIRST)
    def _():
        whole = side_gathered.at[pl.ds(EDGE, ocean_rows)]
        pltpu.make_async_copy(whole, whole, t_recv.at[5]).wait()
        first = grid_first(lax.rem((me - SIDE_FIRST) // PARTS, NCHILD))
        side_picked[0:1] = side_gathered[pl.ds(EDGE + first - 1, 1)]
        side_picked[1:2] = side_gathered[pl.ds(EDGE + first + FOOT_ROWS, 1)]
        for side, target in ((0, 0), (1, n - 1)):
            place = side_rows.at[me - SIDE_FIRST]

            @pl.when(me != target)
            def _():
                remote(side_picked.at[side], place, t_send.at[6], t_recv.at[6], target).start()

            @pl.when(me == target)
            def _():
                pltpu.make_async_copy(side_picked.at[side], place, t_recv.at[6]).start()

    pltpu.make_async_copy(rowbuf, rowbuf, t_recv.at[2]).wait()
    for which in range(2):
        for nested in range(NCHILD):
            for part in range(3):
                for piece in range(PARTS):
                    unit = ((3 * which + part) * NCHILD + nested) * PARTS + piece
                    row = (nested * 3 + part) * PARTS + piece
                    lhs[which, row : row + 1, :] = rowbuf[unit]
    spread[0] = exact_dot(lhs[0], spread_matrix)

    def spread_at(which, nested, part, j):
        row = (nested * 3 + part) * 4 + j // 2
        return spread[which, pl.ds(row, 1), pl.ds(pl.multiple_of(lax.rem(j, 2) * CHUNK, CHUNK), CHUNK)]

    def stage_c(nested, carry):
        def chunk(j, inner_carry):
            here = pl.multiple_of(j * CHUNK, CHUNK)
            plain = pl.ds(here, CHUNK)
            inner = pl.ds(here + TILE, CHUNK)
            scaled = []
            for part in range(3):
                total = end[nested, part, :, plain] + spread_at(0, nested, part, j)
                end[nested, part, :, plain] = total
                scaled.append(HALF * total)
                a2[nested, part, :, inner] = scaled[-1]
                put_row(2, nested, part, plain, scaled[-1])
            return inner_carry

        lax.fori_loop(0, C_COLS // CHUNK, chunk, 0)
        halo_start(2, nested)
        return carry

    lax.fori_loop(0, NCHILD, stage_c, 0)

    @pl.when((me == 0) | (me == n - 1))
    def _():
        pltpu.make_async_copy(besides, besides, t_recv.at[1]).wait()
        pltpu.make_async_copy(side_rows, side_rows, t_recv.at[6]).wait()
        sign = jnp.where(me == 0, -1.0, 1.0)
        for nested in range(NCHILD):

            def line(array, field):
                unit = (field * NCHILD + nested) * PARTS
                return HALF * jnp.concatenate([array[unit + piece] for piece in range(PARTS)], axis=1)

            ce, cv = line(besides, 0), line(besides, 2)
            e_q, v_q = [
                jnp.concatenate(
                    [rest[0, (nested * 3 + part) * 4 + q : (nested * 3 + part) * 4 + q + 1, :] for q in range(4)],
                    axis=1,
                )
                for part in (0, 2)
            ]
            qrow[nested, 0:1, :] = sign * (v_q * ce + cv)
            qrow[nested, 1:2, :] = sign * line(side_rows, 0)
            qrow[nested, 2:3, :] = sign * (line(side_rows, 1) + e_q * ce)

    for nested in range(NCHILD):
        row0 = nested * 12
        for side in range(2):
            sign = -1.0 if side == 0 else 1.0
            where = 32 * nested + 16 * side
            cell = 0 if side == 0 else TILE - 1
            chunk_row = 0 if side == 0 else 3
            u2, bed, ce, cu, cv = [fvals[i : i + 1, where : where + 1] for i in (4, 6, 7, 8, 9)]
            ce, cu, cv = HALF * ce, HALF * cu, HALF * cv
            e_q = rest[0, row0 + chunk_row : row0 + chunk_row + 1, cell : cell + 1]
            u_q = rest[0, row0 + 4 + chunk_row : row0 + 5 + chunk_row, cell : cell + 1]
            adds = (
                sign * (u_q * ce + cu),
                sign * (bed * ce + u2 * cu + e_q * ce),
                sign * (u2 * cv),
            )
            for part in range(3):
                row = row0 + 4 * part + chunk_row
                lhs[1, row : row + 1, :] += jnp.where(lane == cell, adds[part], 0.0)
        for part in range(3):
            for q in range(4):
                row = row0 + 4 * part + q
                lhs[1, row : row + 1, :] += qrow[nested, part : part + 1, TILE * q : TILE * (q + 1)]
    spread[1] = exact_dot(lhs[1], spread_matrix)

    def adjoint(stage, nested, state, cots, slopes, target, beside_it):
        def chunk(j, carry):
            beside_it(nested * (C_COLS // CHUNK) + j)
            here = pl.multiple_of(j * CHUNK, CHUNK)
            wide = pl.ds(here, CHUNK + 2 * TILE)
            plain = pl.ds(here, CHUNK)
            inner = pl.ds(here + TILE, CHUNK)
            wides = [cots[nested, part, :, wide] for part in range(3)]
            wides += [state[nested, 1, :, wide], depth[nested, :, wide]]
            e, v = state[nested, 0, :, inner], state[nested, 2, :, inner]

            edge_fields = []
            for side in range(2):
                he, hu, hv = [halo_row(stage, nested, side, part, plain) for part in range(3)]
                sv = halo_row(1 if stage == 2 else 0, nested, side, 2, plain)
                sb = halo_row(0, nested, side, 3, plain)
                edge_fields.append((he, hv, sv * hu, sb * he + sv * hv))

            def dy(field, index):
                ahead, behind = row_shifts(field, edge_fields[0][index], edge_fields[1][index])
                return ahead - behind

            grads = pulled(wides, e, v, dy, [slopes[i, nested, :, plain] for i in range(4)])
            target(inner, plain, j, grads)
            return carry

        lax.fori_loop(0, C_COLS // CHUNK, chunk, 0)

    def frame_cots(nested, state, cots, first):
        for side in range(2):
            near = pl.ds(TILE, TILE) if side == 0 else pl.ds(C_COLS, TILE)
            far = pl.ds(0, TILE) if side == 0 else pl.ds(TILE + C_COLS, TILE)
            cell = 0 if side == 0 else TILE - 1
            sign = 1.0 if side == 0 else -1.0
            ae, au, av = [cots[nested, part, :, near] for part in range(3)]
            u, bed = state[nested, 1, :, near], depth[nested, :, near]
            ef, uf = state[nested, 0, :, far], state[nested, 1, :, far]
            values = (uf * ae + au, bed * ae + u * au + ef * ae, u * av)
            for part in range(3):
                column = sign * jnp.sum(values[part], axis=0, keepdims=True)[:, cell : cell + 1]
                packet[...] = jnp.where(
                    lane == nested * 16 + side * 8 + first + part, column, packet[...]
                )

    steps = NCHILD * (C_COLS // CHUNK)
    each = -(-n // steps)

    @pl.when(me >= BACK_FIRST)
    def _():
        all_back = returned.at[pl.ds(pad, span)]
        pltpu.make_async_copy(all_back, all_back, t_recv.at[3]).wait()
        first = grid_first((me - BACK_FIRST) // (3 * PARTS))
        placed[...] = returned[pl.ds(pad - first, ocean_rows)]
        pltpu.make_async_copy(
            placed.at[pl.ds(me * P_ROWS, P_ROWS)], back.at[me - BACK_FIRST], t_recv.at[4]
        ).start()

    def some_placed(it):
        @pl.when(me >= BACK_FIRST)
        def _():
            for index in range(each):
                j = it * each + index

                @pl.when((j > 0) & (j < n))
                def _():
                    target = lax.rem(me + j, n)
                    remote(
                        placed.at[pl.ds(target * P_ROWS, P_ROWS)],
                        back.at[me - BACK_FIRST],
                        t_send.at[4],
                        t_recv.at[4],
                        target,
                    ).start()

    def some_edges(it):
        for index in range(each):
            j = it * each + index

            @pl.when((j > 0) & (j < n))
            def _():
                target = lax.rem(me + j, n)
                remote(packet, edges.at[me], ag_send.at[1], ag_recv.at[1], target).start()

    def stage_d(nested, carry):
        halo_wait(2, nested)

        def target(inner, plain, j, grads):
            scaled = []
            for part in range(3):
                total = mid[nested, part, :, plain] + grads[part] + spread_at(1, nested, part, j)
                mid[nested, part, :, plain] = total
                scaled.append(HALF * total)
                a1[nested, part, :, inner] = scaled[-1]
                put_row(3, nested, part, plain, scaled[-1])

        adjoint(2, nested, nxt, a2, slopes2, target, some_placed)
        halo_start(3, nested)
        frame_cots(nested, nxt, a2, 0)
        frame_cots(nested, now, a1, 3)
        return carry

    lax.fori_loop(0, NCHILD, stage_d, 0)
    store_gold = pltpu.make_async_copy(mid, gold_out, store_sem.at[1])
    store_gold.start()

    edges[me] = packet[...]

    def stage_e(nested, carry):
        halo_wait(3, nested)

        def target(inner, plain, j, grads):
            for part in range(3):
                end[nested, part, :, plain] = end[nested, part, :, plain] + grads[part]

        adjoint(3, nested, now, a1, slopes1, target, some_edges)
        return carry

    lax.fori_loop(0, NCHILD // 2, stage_e, 0)

    row4 = me * P_ROWS + lax.broadcasted_iota(jnp.int32, (P_ROWS, CHUNK), 0)
    column4 = lax.broadcasted_iota(jnp.int32, (P_ROWS, CHUNK), 1)

    def covered_at(j):
        nested = j // (BAND // CHUNK)
        foot = row4 - rows_smem[nested]
        column = j * CHUNK + column4 - cols_smem[nested]
        return (foot >= 0) & (foot < FOOT_ROWS) & (column >= 0) & (column < FOOT_COLS)

    pltpu.make_async_copy(back, back, t_recv.at[4]).wait()
    for nested in range(NCHILD):
        right = cols_smem[nested] - nested * BAND
        fine_shift = TILE - lax.rem(right, TILE)
        tiles = jnp.full((2 * P_ROWS, TILE), right // TILE, jnp.int32)
        band = nested * BAND
        blank = jnp.zeros((2 * P_ROWS, TILE), jnp.float32)
        for part in range(3):
            rows_of = [
                jnp.concatenate(
                    [back[(nested * 3 + part) * PARTS + q, :, which, :] for q in range(PARTS)], axis=1
                )
                for which in range(2)
            ]
            both = jnp.concatenate([blank, jnp.concatenate(rows_of, axis=0), blank], axis=1)
            both = moved_left(both, fine_shift, 8)
            held = [both[:, TILE * q : TILE * (q + 1)] for q in range(PARTS + 1)]
            held += [blank] * (BAND // TILE - PARTS - 1)
            for bit in range(4):
                step = 1 << bit
                chosen = (tiles >> bit) & 1 == 1
                held = [
                    jnp.where(chosen, held[q - step] if q >= step else blank, held[q])
                    for q in range(len(held))
                ]
            for q, tile in enumerate(held):
                for which in range(2):
                    means[which, part, :, band + TILE * q : band + TILE * (q + 1)] = tile[
                        P_ROWS * which : P_ROWS * (which + 1)
                    ]

    def ocean_second(j, carry):
        plain, inner, wide = ocean_lanes(j)
        covered = covered_at(j)
        for part in range(3):
            state = jnp.where(covered, means[0, part, :, plain], second8[part, 1:5, inner])
            cot = jnp.where(covered, 0.0, HALF * p_end[part, :, plain])
            second8[part, 1:5, inner] = state
            a28[part, 1:5, inner] = cot
            for side, row in ((0, 0), (1, P_ROWS - 1)):
                ocean_send[side, 4 + part, :, plain] = state[row : row + 1]
                ocean_send[side, 7 + part, :, plain] = cot[row : row + 1]
        return carry

    lax.fori_loop(0, chunks, ocean_second, 0)
    ocean_start(1)

    lax.fori_loop(NCHILD // 2, NCHILD, stage_e, 0)
    store_gnow = pltpu.make_async_copy(end, gnow_out, store_sem.at[2])
    store_gnow.start()

    ocean_wait(1)

    def ocean_edges(j, carry):
        plain, inner, wide = ocean_lanes(j)
        for part in range(3):
            for array, first in ((second8, 4), (a28, 7)):
                array[part, 0:1, inner] = ocean_edge(0, first + part, plain)
                array[part, 5:6, inner] = ocean_edge(1, first + part, plain)
        return carry

    lax.fori_loop(0, chunks, ocean_edges, 0)

    def ocean_dy(field, index):
        ahead, behind = turn(field)
        return ahead - behind

    def ocean_pull(j, state, cots, slopes):
        plain, inner, wide = ocean_lanes(j)
        wides = [cots[part, :, wide] for part in range(3)] + [state[1, :, wide], depth8[:, wide]]
        return pulled(wides, state[0, :, inner], state[2, :, inner], ocean_dy, slopes)

    def ocean_third(j, carry):
        plain, inner, wide = ocean_lanes(j)
        covered = covered_at(j)
        changes, found = ocean_rates(second8, j)
        grads = ocean_pull(j, second8, a28, found)
        for part in range(3):
            pend[part, :, plain] = jnp.where(
                covered, means[1, part, :, plain], p_now[part, :, plain] - changes[part][1:5]
            )
            cot = jnp.where(covered, 0.0, p_mid[part, :, plain] + grads[part][1:5])
            pgold[part, :, plain] = cot
            for side, row in ((0, 0), (1, P_ROWS - 1)):
                ocean_send[side, 10 + part, :, plain] = cot[row : row + 1]
        return carry

    lax.fori_loop(0, chunks, ocean_third, 0)
    ocean_start(2)
    store_pend = pltpu.make_async_copy(pend, pend_out, store_sem.at[3])
    store_pend.start()

    all_edges = edges.at[pl.ds(0, n - 1)]
    pltpu.make_async_copy(all_edges, all_edges, ag_recv.at[1]).wait()
    row8 = me * P_ROWS - 1 + lax.broadcasted_iota(jnp.int32, (8, 1), 0)
    for nested in range(NCHILD):
        foot = row8 - rows_smem[nested]
        lines = jnp.concatenate(
            [
                edges[jnp.clip(me * P_ROWS - 1 + t - rows_smem[nested], 0, FOOT_ROWS - 1)]
                for t in range(8)
            ],
            axis=0,
        )
        lines = jnp.where((foot >= 0) & (foot < FOOT_ROWS), lines, 0.0)
        for side in range(2):
            for which in range(2):
                for part in range(3):
                    at = nested * 16 + side * 8 + 3 * which + part
                    cells[nested, side, which, part] = jnp.broadcast_to(lines[:, at : at + 1], (8, TILE))
    ocean_wait(2)
    column8 = lax.broadcasted_iota(jnp.int32, (8, CHUNK), 1)

    def beside_at(j, which, part):
        nested = j // (BAND // CHUNK)
        column = j * CHUNK + column8 - cols_smem[nested]
        west, east = [
            jnp.concatenate([cells[nested, side, which, part]] * (CHUNK // TILE), axis=1) for side in range(2)
        ]
        return jnp.where(column == -1, west, 0.0) + jnp.where(column == FOOT_COLS, east, 0.0)

    def ocean_fourth(j, carry):
        plain, inner, wide = ocean_lanes(j)
        for part in range(3):
            extra = beside_at(j, 0, part)
            cot = pgold[part, :, plain] + extra[1:5]
            pgold[part, :, plain] = cot
            a18[part, 1:5, inner] = HALF * cot
            a18[part, 0:1, inner] = HALF * (ocean_edge(0, 10 + part, plain) + extra[0:1])
            a18[part, 5:6, inner] = HALF * (ocean_edge(1, 10 + part, plain) + extra[5:6])
        return carry

    lax.fori_loop(0, chunks, ocean_fourth, 0)
    store_pgold = pltpu.make_async_copy(pgold, pgold_out, store_sem.at[4])
    store_pgold.start()

    def ocean_last(j, carry):
        plain, inner, wide = ocean_lanes(j)
        covered = covered_at(j)
        grads = ocean_pull(j, now8, a18, [pslopes[i, :, plain] for i in range(4)])
        for part in range(3):
            kept = jnp.where(covered, 0.0, p_end[part, :, plain])
            pgnow[part, :, plain] = kept + (grads[part] + beside_at(j, 1, part))[1:5]
        return carry

    lax.fori_loop(0, chunks, ocean_last, 0)
    store_pgnow = pltpu.make_async_copy(pgnow, pgnow_out, store_sem.at[5])
    store_pgnow.start()
    for store in (store_next, store_gold, store_gnow, store_pend, store_pgold, store_pgnow):
        store.wait()

    pltpu.make_async_copy(all_but, all_but, ag_send.at[0]).wait()
    pltpu.make_async_copy(all_edges, all_edges, ag_send.at[1]).wait()

    def drain_halo(nested, carry):
        for stage in range(4):
            for copy in halo_copies(stage, nested):
                copy.wait_send()
        return carry

    lax.fori_loop(0, NCHILD, drain_halo, 0)
    for stage in range(3):
        for copy in ocean_copies(*ocean_stages[stage]):
            copy.wait_send()

    def drain(count, first, like, send):
        own = (me >= first) & (me < first + count)

        @pl.when(own)
        def _():
            sent = like.at[pl.ds(0, count - 1)]
            pltpu.make_async_copy(sent, sent, send).wait()

        @pl.when(jnp.logical_not(own))
        def _():
            pltpu.make_async_copy(like, like, send).wait()

    drain(ROW_UNITS, 0, win, t_send.at[0])
    drain(SIDE_UNITS, SIDE_FIRST, side_win, t_send.at[5])
    drain(BACK, BACK_FIRST, pairs, t_send.at[3])

    @pl.when(me < ROW_UNITS)
    def _():
        sent = picked.at[pl.ds(0, n - 1)]
        pltpu.make_async_copy(sent, sent, t_send.at[2]).wait()

    for target in (0, n - 1):

        @pl.when((me != target) & (me < ROW_UNITS // 2))
        def _():
            one = beside.at[0]
            pltpu.make_async_copy(one, one, t_send.at[1]).wait()

        @pl.when((me != target) & (me >= SIDE_FIRST))
        def _():
            one = side_picked.at[0]
            pltpu.make_async_copy(one, one, t_send.at[6]).wait()

    @pl.when(me >= BACK_FIRST)
    def _():
        gone = placed.at[pl.ds(0, (n - 1) * P_ROWS)]
        pltpu.make_async_copy(gone, gone, t_send.at[4]).wait()


def everything(n, child_rows, child_cols, strips, coast):
    f32 = jnp.float32
    anywhere = pl.BlockSpec(memory_space=pl.ANY)
    smem = pl.BlockSpec(memory_space=pltpu.SMEM)
    grid_shape = (NCHILD, 3, C_ROWS, C_COLS)
    wide_shape = (NCHILD, 3, C_ROWS, PADDED)
    ocean_shape = (3, P_ROWS, P_COLS)
    tall_shape = (3, 8, P_COLS + 2 * TILE)
    ocean_rows = n * P_ROWS
    dma = pltpu.SemaphoreType.DMA
    shapes = [
        grid_shape,
        wide_shape,
        wide_shape,
        (NCHILD, C_ROWS, PADDED),
        grid_shape,
        grid_shape,
        wide_shape,
        wide_shape,
        (4, NCHILD, C_ROWS, C_COLS),
        (4, NCHILD, C_ROWS, C_COLS),
        (NCHILD, 2, 4, 1, C_COLS),
        (NCHILD, 2, 4, 1, C_COLS),
        (3, NCHILD, 2, 3, 1, C_COLS),
        (3, NCHILD, 2, 3, 1, C_COLS),
        (ROW_UNITS, P_ROWS, 1, TILE),
        (SIDE_UNITS, P_ROWS, 1, TILE),
        (P_ROWS, 1, TILE),
        (ocean_rows + 2 * EDGE, 1, TILE),
        (16, TILE),
        (ocean_rows + 2 * EDGE, 1, TILE),
        (ocean_rows + 2 * EDGE, 1, TILE),
        (FOOT_ROWS, 1, TILE),
        (2, 1, TILE),
        (2, 1, TILE),
        (ROW_UNITS, 1, TILE),
        (ROW_UNITS // 2, 1, TILE),
        (SIDE_UNITS, 1, TILE),
        (2, BACK, TILE),
        (2, BACK, RATIO * TILE),
        (2, BACK, RATIO * TILE),
        (2, BACK, TILE),
        (BACK, 2, TILE),
        (2 * ocean_rows + FOOT_ROWS, 2, TILE),
        (ocean_rows, 2, TILE),
        (NCHILD, 8, FOOT_COLS),
        (n, 1, TILE),
        (1, TILE),
        ocean_shape,
        ocean_shape,
        (P_ROWS, P_COLS),
        ocean_shape,
        ocean_shape,
        tall_shape,
        tall_shape[1:],
        tall_shape,
        tall_shape,
        tall_shape,
        (4, 8, P_COLS),
        (2, 3, P_ROWS, P_COLS),
        (NCHILD, 2, 2, 3, 8, TILE),
        (BACK, P_ROWS, 2, TILE),
        ocean_shape,
        ocean_shape,
        ocean_shape,
        (2, 13, 1, P_COLS),
        (2, 13, 1, P_COLS),
    ]
    return pl.pallas_call(
        functools.partial(coastal_kernel, n),
        out_shape=[jax.ShapeDtypeStruct(grid_shape, f32)] * 3 + [jax.ShapeDtypeStruct(ocean_shape, f32)] * 3,
        in_specs=[smem] * 2 + [anywhere] * 10,
        out_specs=[anywhere] * 6,
        scratch_shapes=[pltpu.VMEM(shape, f32) for shape in shapes]
        + [
            dma((10,)),
            dma((6,)),
            dma((4, NCHILD, 2)),
            dma((4, NCHILD, 2)),
            dma((2,)),
            dma((2,)),
            dma((7,)),
            dma((7,)),
            dma((3, 2)),
            dma((3, 2)),
        ],
        compiler_params=pltpu.CompilerParams(
            collective_id=0, has_side_effects=True, vmem_limit_bytes=56 * 1024 * 1024
        ),
    )(child_rows, child_cols, *strips, *coast)


def bounce_kernel(*refs):
    sources, targets, held, sems = refs[:6], refs[6:12], refs[12:18], refs[18]
    pieces = []
    for index in range(6):
        for part in range(sources[index].shape[0]):
            pieces.append(
                (
                    pltpu.make_async_copy(
                        sources[index].at[part], held[index].at[part], sems.at[0, index, part]
                    ),
                    pltpu.make_async_copy(
                        held[index].at[part], targets[index].at[part], sems.at[1, index, part]
                    ),
                )
            )
    for fetch, store in pieces:
        fetch.start()
    for fetch, store in pieces:
        fetch.wait()
        store.start()
    for fetch, store in pieces:
        store.wait()


def bounce(arrays):
    anywhere = pl.BlockSpec(memory_space=pl.ANY)
    return pl.pallas_call(
        bounce_kernel,
        out_shape=[jax.ShapeDtypeStruct(array.shape, array.dtype) for array in arrays],
        in_specs=[anywhere] * 6,
        out_specs=[anywhere] * 6,
        scratch_shapes=[pltpu.VMEM(array.shape, array.dtype) for array in arrays]
        + [pltpu.SemaphoreType.DMA((2, 6, NCHILD))],
        compiler_params=pltpu.CompilerParams(vmem_limit_bytes=60 * 1024 * 1024),
    )(*arrays)


def shards(
    n,
    parent_old,
    parent_now,
    child_old,
    child_now,
    parent_depth,
    child_depth,
    child_rows,
    child_cols,
    parent_cot_mid,
    parent_cot_end,
    child_cot_mid,
    child_cot_end,
):
    strips = (parent_old, parent_now, parent_depth, parent_cot_mid, parent_cot_end)
    coast = (child_old, child_now, child_depth, child_cot_mid, child_cot_end)
    results = bounce(everything(n, child_rows, child_cols, strips, coast))
    child_end, child_gold, child_gnow, parent_end, parent_gold, parent_gnow = results
    return (parent_end, child_end, parent_gold, parent_gnow, child_gold, child_gnow)


def solution(mesh):
    ocean_spec = P(None, "rows", None)
    coast_spec = P(None, None, "rows", None)
    return jax.shard_map(
        functools.partial(shards, mesh.shape["rows"]),
        mesh=mesh,
        in_specs=(
            ocean_spec,
            ocean_spec,
            coast_spec,
            coast_spec,
            P("rows", None),
            P(None, "rows", None),
            P(),
            P(),
            ocean_spec,
            ocean_spec,
            coast_spec,
            coast_spec,
        ),
        out_specs=(ocean_spec, coast_spec, ocean_spec, ocean_spec, coast_spec, coast_spec),
        check_vma=False,
    )
```

time: 212 us -> 87.1 us (0.41)
  local copies, waits for them, and re-layouts: 66.2 us -> 0 us
  other arithmetic: 40.1 us -> 0 us
  between operations: 22.4 us -> 0.64 us
  Pallas kernels: 81.9 us -> 86.4 us
    dynamic_update_slice x8 -> x0, local copies, waits for them, and re-layouts: 16.6 us -> none  [ocean(): lax.dynamic_update_slice_in_dim(means[which], back[which, nested], left, 2)]
    unnamed x85 -> x0, local copies, waits for them, and re-layouts: 15 us -> none
    another operation x6 -> x0, other arithmetic: 12.3 us -> none  [the longest x2 4.97 us: pull(): jnp.stack([u * xe + v * ye + dx(au) + dy(av), dx(depth * ae + u * au) + d...]
    select_n x9 -> x0, other arithmetic: 11.5 us -> none  [the longest x1 3.44 us: ocean(): before = jnp.where(me > 0, halo[0], 0.0).reshape(13, 3, P_COLS)]
    slice x10 -> x0, local copies, waits for them, and re-layouts: 6.86 us -> none  [the longest x7 2.94 us: ocean(): return (state3[:, mine], cot2[:, mine], cot1[:, mine])]
    another operation x6 -> x0, local copies, waits for them, and re-layouts: 6.41 us -> none  [the longest x2 3.73 us: shards(): halo = jnp.stack([own[:, 0:3], own[:, 1:4]]).reshape(2, 39, P_COLS)]
    add x3 -> x0, other arithmetic: 6.22 us -> none  [the longest x1 3.19 us: ocean(): cot1 = cot3 + pull(now, cot2, depth) + extra[1]]
    transpose x25 -> x0, local copies, waits for them, and re-layouts: 6.01 us -> none  [the longest x15 5.81 us: ocean(): cells = jnp.transpose(line[:, first:first + 3])[:, :, None]]
where the time goes in v3:
time: 87.1 us; the launch traced here: 87 us
  Pallas kernels  86.4 us (99%)
    pallas_call x1, Pallas kernels, everything(): pl.pallas_call(functools.partial(coastal_kernel, n), out_shape=[jax.Shape...  81.1 us
    pallas_call x1, Pallas kernels, bounce(): pl.pallas_call(bounce_kernel, out_shape=[jax.ShapeDtypeStruct(array.shape...  5.28 us

profile of v3, /device:TPU:0, one launch (start us, length us, event | category | flops | bytes accessed | tf_op | source)
XLA Modules:
  0.0 87.0 jit_solution(15489645213553489361)
XLA Ops:
  0.6 81.1 %shard_map.163 = (f32[4,3,8,4096]{3,2,1,0:T(8,128)}, f32[4,3,8,4096]{3,2,1,0:T(8,128)}, f32[4,3,8,4096]{3,2,1,0:T(8,128)}, f32[3,4,8192]{2,1,0:T(4,128)}, f32[3,4,8192]{2,1,0:T(4,128)}, /*index=5*/f32[3,4,8192]{2,1,0:T(4,128)}) custom-call(s32[4]{0:T(128)} %rows_smem.1, s32[4]{0:T(128)} %cols_smem.1, f32[3,4,8192]{2,1,0:T(4,128)} %refs_0_.1, ...), custom_call_target="tpu_custom_call" | custom-call | tf_op jit(solution)/shard_map/pallas_call | solution.py:1104
  81.7 5.3 %shard_map.164 = (f32[4,3,8,4096]{3,2,1,0:T(8,128)}, f32[4,3,8,4096]{3,2,1,0:T(8,128)}, f32[4,3,8,4096]{3,2,1,0:T(8,128)}, f32[3,4,8192]{2,1,0:T(4,128)}, f32[3,4,8192]{2,1,0:T(4,128)}, /*index=5*/f32[3,4,8192]{2,1,0:T(4,128)}) custom-call(f32[4,3,8,4096]{3,2,1,0:T(8,128)} %get-tuple-element.18.refs_0_, f32[4,3,8,4096]{3,2,1,0:T(8,128)} %get-tuple-element.19.refs_1_, ...), custom_call_target="tpu_custom_call" | custom-call | tf_op jit(solution)/shard_map/pallas_call | solution.py:1154

commit v4 on v3

--- a/solution.py
+++ b/solution.py
@@ -20,14 +20,16 @@
 TILE = 128
 PADDED = C_COLS + 2 * TILE
 CHUNK = 512
+COAST_UNROLL = 8
+OCEAN_UNROLL = 4
 HALF = 0.15
 DRAG = 0.015
 PARTS = FOOT_COLS // TILE
-ROW_UNITS = 6 * NCHILD * PARTS
+ROW_UNITS = 3 * NCHILD * PARTS
 SIDE_UNITS = 2 * NCHILD * PARTS
 SIDE_FIRST = 96
 BACK = 3 * NCHILD * PARTS
-BACK_FIRST = 80
+BACK_FIRST = 48
 EDGE = 8
 
 
@@ -107,7 +109,7 @@
     return sum(jnp.dot(part, matrix, preferred_element_type=jnp.float32) for part in split3(rows))
 
 
-def coastal_kernel(n, rows_smem, cols_smem, *refs):
+def coastal_kernel(n, rows_smem, cols_smem, win_hbm, frame_hbm, *refs):
     strips_hbm, refs = refs[:5], refs[5:]
     old_hbm, now_hbm, depth_hbm, mid_hbm, end_hbm = refs[:5]
     next_out, gold_out, gnow_out, pend_out, pgold_out, pgnow_out = refs[5:11]
@@ -182,8 +184,7 @@
     me = lax.axis_index("rows")
     up = lax.rem(me + 1, n)
     down = lax.rem(me + n - 1, n)
-    has_before = jnp.where(me > 0, 1.0, 0.0)
-    has_after = jnp.where(me < n - 1, 1.0, 0.0)
+    has_before, has_after = me > 0, me < n - 1
     centre = pl.ds(TILE, C_COLS)
 
     barrier = pltpu.get_barrier_semaphore()
@@ -199,44 +200,23 @@
         pltpu.make_async_copy(source, target, load_sem.at[index])
         for index, (source, target) in enumerate(
             zip(
-                strips_hbm + (now_hbm, depth_hbm, old_hbm, end_hbm, mid_hbm),
-                strips + (now.at[:, :, :, centre], depth.at[:, :, centre], old, end, mid),
+                strips_hbm + (now_hbm, depth_hbm, old_hbm, end_hbm, mid_hbm, win_hbm, frame_hbm),
+                strips + (now.at[:, :, :, centre], depth.at[:, :, centre], old, end, mid, win, frame),
             )
         )
     ]
     for load in loads:
         load.start()
 
-    for array in (a2, a1):
-        array[:, :, :, 0:TILE] = jnp.zeros((NCHILD, 3, C_ROWS, TILE), jnp.float32)
-        array[:, :, :, TILE + C_COLS :] = jnp.zeros((NCHILD, 3, C_ROWS, TILE), jnp.float32)
-    depth[:, :, 0:TILE] = jnp.zeros((NCHILD, C_ROWS, TILE), jnp.float32)
-    depth[:, :, TILE + C_COLS :] = jnp.zeros((NCHILD, C_ROWS, TILE), jnp.float32)
     ocean_rows = n * P_ROWS
     frames[0:EDGE] = jnp.zeros((EDGE, 1, TILE), jnp.float32)
     frames[pl.ds(EDGE + ocean_rows, EDGE)] = jnp.zeros((EDGE, 1, TILE), jnp.float32)
-    for array in (gathered, side_gathered):
-        array[0:EDGE] = jnp.zeros((EDGE, 1, TILE), jnp.float32)
-        array[pl.ds(EDGE + ocean_rows, EDGE)] = jnp.zeros((EDGE, 1, TILE), jnp.float32)
+    for array, depth_of in ((gathered, 2), (side_gathered, 1)):
+        array[0:EDGE] = jnp.zeros((EDGE, depth_of, TILE), jnp.float32)
+        array[pl.ds(EDGE + ocean_rows, EDGE)] = jnp.zeros((EDGE, depth_of, TILE), jnp.float32)
     pad = ocean_rows
     span = FOOT_ROWS
-    returned[0:pad] = jnp.zeros((pad, 2, TILE), jnp.float32)
-    returned[pl.ds(pad + span, pad)] = jnp.zeros((pad, 2, TILE), jnp.float32)
-    for array in (now8, second8, a28, a18):
-        for lanes in (slice(0, TILE), slice(TILE + P_COLS, P_COLS + 2 * TILE)):
-            array[:, :, lanes] = jnp.zeros((3, 8, TILE), jnp.float32)
-        array[:, 6:8, :] = jnp.zeros((3, 2, P_COLS + 2 * TILE), jnp.float32)
-    depth8[:, 0:TILE] = jnp.zeros((8, TILE), jnp.float32)
-    depth8[:, TILE + P_COLS :] = jnp.zeros((8, TILE), jnp.float32)
-    depth8[6:8, :] = jnp.zeros((2, P_COLS + 2 * TILE), jnp.float32)
-    qrow[...] = jnp.zeros_like(qrow)
-    packet[...] = jnp.zeros_like(packet)
-
     lane = lax.broadcasted_iota(jnp.int32, (1, TILE), 1)
-    whole_ocean = pl.ds(TILE, P_COLS)
-
-    for index in range(5):
-        loads[index].wait()
 
     def band_tiles(nested, blocks):
         first = nested * (BAND // TILE) - 1
@@ -248,57 +228,27 @@
                 tiles.append(jnp.concatenate([block(q) for block in blocks], axis=0))
         return cut_window(tiles, cols_smem[nested] - nested * BAND)
 
-    lane4 = lax.broadcasted_iota(jnp.int32, (P_ROWS, TILE), 1)
-    raw_cells = jnp.zeros((P_ROWS, TILE), jnp.float32)
-    for nested in range(NCHILD):
-        def block_of(ref, part):
-            if part is None:
-                return lambda q: ref[:, TILE * q : TILE * (q + 1)]
-            return lambda q: ref[part, :, TILE * q : TILE * (q + 1)]
-
-        sources = [(p_end, 0), (p_end, 1), (p_end, 2), (p_mid, 0), (p_mid, 1), (p_mid, 2)]
-        sources += [(p_now, 0), (p_now, 1), (p_now, 2), (p_old, 0), (p_old, 1), (p_old, 2), (p_depth, None)]
-        blocks = []
-        for first in range(0, len(sources), 2):
-            pair = [block_of(*source) for source in sources[first : first + 2]]
-            both = band_tiles(nested, pair)
-            blocks += [both[P_ROWS * i : P_ROWS * (i + 1)] for i in range(len(pair))]
-        for field in range(6):
-            for piece in range(PARTS):
-                unit = (field * NCHILD + nested) * PARTS + piece
-                for row in range(P_ROWS):
-                    win[unit, row] = blocks[field][row : row + 1, (piece + 1) * TILE : (piece + 2) * TILE]
-        foot_end = TILE + FOOT_COLS
-        for side, lanes in enumerate(
-            ((TILE - 2, TILE - 1, TILE), (foot_end - 1, foot_end, foot_end + 1))
-        ):
-            found = [blocks[6 + part][:, at : at + 1] for part in range(3) for at in lanes]
-            at = lanes[1]
-            for index in (9, 10, 11, 12, 0, 1, 2):
-                found.append(blocks[index][:, at : at + 1])
-            for index, cell in enumerate(found):
-                raw_cells = jnp.where(lane4 == 32 * nested + 16 * side + index, cell, raw_cells)
-    for row in range(P_ROWS):
-        frame[row] = raw_cells[row : row + 1]
-
-    for side, row in ((0, 0), (1, P_ROWS - 1)):
-        for part in range(3):
-            ocean_send[side, part] = p_now[part, row : row + 1, :]
-        ocean_send[side, 3] = p_depth[row : row + 1, :]
-    loads[5].wait()
-    loads[6].wait()
-    for nested in range(NCHILD):
-        for side, row in ((0, 0), (1, C_ROWS - 1)):
-            for part in range(3):
-                first_send[nested, side, part] = now[nested, part, row : row + 1, centre]
-            first_send[nested, side, 3] = depth[nested, row : row + 1, centre]
-
+    mine = pl.ds(EDGE + me * P_ROWS, P_ROWS)
+    loads[11].wait()
+    frames[mine] = frame[...]
     pl.semaphore_wait(barrier, n - 1)
 
     def remote(source, target, send, recv, device):
         return pltpu.make_async_remote_copy(
             source, target, send, recv, device_id=(device,), device_id_type=MESH
         )
+
+    def start_both(pair):
+        pl.when(has_before)(pair[0].start)
+        pl.when(has_after)(pair[1].start)
+
+    def wait_both(pair):
+        pl.when(has_after)(pair[0].wait_recv)
+        pl.when(has_before)(pair[1].wait_recv)
+
+    def drain_both(pair):
+        pl.when(has_before)(pair[0].wait_send)
+        pl.when(has_after)(pair[1].wait_send)
 
     def ocean_copies(first, count, stage):
         fields = pl.ds(first, count)
@@ -322,12 +272,10 @@
     ocean_stages = ((0, 4, 0), (4, 6, 1), (10, 3, 2))
 
     def ocean_start(stage):
-        for copy in ocean_copies(*ocean_stages[stage]):
-            copy.start()
+        start_both(ocean_copies(*ocean_stages[stage]))
 
     def ocean_wait(stage):
-        for copy in ocean_copies(*ocean_stages[stage]):
-            copy.wait_recv()
+        wait_both(ocean_copies(*ocean_stages[stage]))
 
     def halo_copies(stage, nested):
         if stage == 0:
@@ -344,23 +292,19 @@
     def halo_row(stage, nested, side, part, plain):
         kept = has_before if side == 0 else has_after
         if stage == 0:
-            return first_halo[nested, side, part, :, plain] * kept
-        return halo_rows[stage - 1, nested, side, part, :, plain] * kept
+            return jnp.where(kept, first_halo[nested, side, part, :, plain], 0.0)
+        return jnp.where(kept, halo_rows[stage - 1, nested, side, part, :, plain], 0.0)
 
     def put_row(stage, nested, part, plain, value):
         send_rows[stage - 1, nested, 0, part, :, plain] = value[0:1]
         send_rows[stage - 1, nested, 1, part, :, plain] = value[C_ROWS - 1 :]
 
     def halo_start(stage, nested):
-        for copy in halo_copies(stage, nested):
-            copy.start()
+        start_both(halo_copies(stage, nested))
 
     def halo_wait(stage, nested):
-        for copy in halo_copies(stage, nested):
-            copy.wait_recv()
-
-    mine = pl.ds(EDGE + me * P_ROWS, P_ROWS)
-    frames[mine] = frame[...]
+        wait_both(halo_copies(stage, nested))
+
     def deal(count, first, source, target, send, recv):
         own = (me >= first) & (me < first + count)
         place = lax.rem(me + (n // count + 1) * count - first, count)
@@ -390,103 +334,40 @@
             first = jnp.where(grid_index == nested, rows_smem[nested], first)
         return first
 
+    every(lambda other: frame, frames.at[mine], ag_send.at[0], ag_recv.at[0])
+    for index in (5, 6):
+        loads[index].wait()
+    for nested in range(NCHILD):
+        for side, row in ((0, 0), (1, C_ROWS - 1)):
+            for part in range(3):
+                first_send[nested, side, part] = now[nested, part, row : row + 1, centre]
+            first_send[nested, side, 3] = depth[nested, row : row + 1, centre]
+        halo_start(0, nested)
+
+    loads[10].wait()
     deal(ROW_UNITS, 0, lambda unit: win.at[unit], gathered.at[mine], t_send.at[0], t_recv.at[0])
-    every(lambda other: frame, frames.at[mine], ag_send.at[0], ag_recv.at[0])
+    loads[1].wait()
+    loads[2].wait()
+    for side, row in ((0, 0), (1, P_ROWS - 1)):
+        for part in range(3):
+            ocean_send[side, part] = p_now[part, row : row + 1, :]
+        ocean_send[side, 3] = p_depth[row : row + 1, :]
     ocean_start(0)
-    for nested in range(NCHILD):
-        halo_start(0, nested)
-
-    @pl.when(me < ROW_UNITS)
-    def _():
-        whole = gathered.at[pl.ds(EDGE, ocean_rows)]
-        pltpu.make_async_copy(whole, whole, t_recv.at[0]).wait()
-        first = grid_first(lax.rem(me // PARTS, NCHILD))
-        picked[...] = gathered[pl.ds(EDGE + first, FOOT_ROWS)]
-        every(lambda other: picked.at[other], rowbuf.at[me], t_send.at[2], t_recv.at[2])
-        pltpu.make_async_copy(picked.at[me], rowbuf.at[me], t_recv.at[2]).start()
-
-        @pl.when(me < ROW_UNITS // 2)
-        def _():
-            beside[0:1] = gathered[pl.ds(EDGE + first - 1, 1)]
-            beside[1:2] = gathered[pl.ds(EDGE + first + FOOT_ROWS, 1)]
-            for side, target in ((0, 0), (1, n - 1)):
-
-                @pl.when(me != target)
-                def _():
-                    remote(beside.at[side], besides.at[me], t_send.at[1], t_recv.at[1], target).start()
-
-                @pl.when(me == target)
-                def _():
-                    pltpu.make_async_copy(beside.at[side], besides.at[me], t_recv.at[1]).start()
-
-    def ocean_lanes(j):
-        here = pl.multiple_of(j * CHUNK, CHUNK)
-        return pl.ds(here, CHUNK), pl.ds(here + TILE, CHUNK), pl.ds(here, CHUNK + 2 * TILE)
-
-    def ocean_edge(side, field, plain):
-        return ocean_halo[side, field, :, plain] * (has_before if side == 0 else has_after)
-
-    def put8(array, part, inner, own, field, plain):
-        array[part, 1:5, inner] = own
-        if field is not None:
-            array[part, 0:1, inner] = ocean_edge(0, field, plain)
-            array[part, 5:6, inner] = ocean_edge(1, field, plain)
-
-    chunks = P_COLS // CHUNK
-    ocean_wait(0)
-
-    def assemble(j, carry):
-        plain, inner, wide = ocean_lanes(j)
-        for part in range(3):
-            put8(now8, part, inner, p_now[part, :, plain], part, plain)
-        depth8[1:5, inner] = p_depth[:, plain]
-        depth8[0:1, inner] = ocean_edge(0, 3, plain)
-        depth8[5:6, inner] = ocean_edge(1, 3, plain)
-        return carry
-
-    lax.fori_loop(0, chunks, assemble, 0)
-
-    def turn(field):
-        return pltpu.roll(field, 7, 0), pltpu.roll(field, 1, 0)
-
-    def ocean_rates(state, j):
-        plain, inner, wide = ocean_lanes(j)
-        shifted = []
-        for part in range(3):
-            block = state[part, :, wide]
-            middle = block[:, TILE : TILE + CHUNK]
-            shifted.append((middle,) + column_shifts(block, CHUNK) + turn(middle))
-        return rates(shifted, depth8[:, inner])
-
-    def ocean_first(j, carry):
-        plain, inner, wide = ocean_lanes(j)
-        changes, found = ocean_rates(now8, j)
-        for index, slope in enumerate(found):
-            pslopes[index, :, plain] = slope
-        for part in range(3):
-            second8[part, 1:5, inner] = p_old[part, :, plain] - changes[part][1:5]
-        return carry
-
-    lax.fori_loop(0, chunks, ocean_first, 0)
-
-    for nested in range(NCHILD):
-        def first_product(q):
-            tile = slice(TILE * q, TILE * (q + 1))
-            return second8[2, 1:5, TILE * (q + 1) : TILE * (q + 2)] * p_end[1, :, tile]
-
-        def second_product(q):
-            tile = slice(TILE * q, TILE * (q + 1))
-            v_2 = second8[2, 1:5, TILE * (q + 1) : TILE * (q + 2)]
-            return p_depth[:, tile] * p_end[0, :, tile] + v_2 * p_end[2, :, tile]
-
-        value = band_tiles(nested, (first_product, second_product))
-        for which in range(2):
-            for piece in range(PARTS):
-                unit = (which * NCHILD + nested) * PARTS + piece
-                for row in range(P_ROWS):
-                    at = which * P_ROWS + row
-                    side_win[unit, row] = value[at : at + 1, (piece + 1) * TILE : (piece + 2) * TILE]
-    deal(SIDE_UNITS, SIDE_FIRST, lambda unit: side_win.at[unit], side_gathered.at[mine], t_send.at[5], t_recv.at[5])
+
+    for array in (a2, a1):
+        array[:, :, :, 0:TILE] = jnp.zeros((NCHILD, 3, C_ROWS, TILE), jnp.float32)
+        array[:, :, :, TILE + C_COLS :] = jnp.zeros((NCHILD, 3, C_ROWS, TILE), jnp.float32)
+    depth[:, :, 0:TILE] = jnp.zeros((NCHILD, C_ROWS, TILE), jnp.float32)
+    depth[:, :, TILE + C_COLS :] = jnp.zeros((NCHILD, C_ROWS, TILE), jnp.float32)
+    for array in (now8, second8, a28, a18):
+        for lanes in (slice(0, TILE), slice(TILE + P_COLS, P_COLS + 2 * TILE)):
+            array[:, :, lanes] = jnp.zeros((3, 8, TILE), jnp.float32)
+        array[:, 6:8, :] = jnp.zeros((3, 2, P_COLS + 2 * TILE), jnp.float32)
+    depth8[:, 0:TILE] = jnp.zeros((8, TILE), jnp.float32)
+    depth8[:, TILE + P_COLS :] = jnp.zeros((8, TILE), jnp.float32)
+    depth8[6:8, :] = jnp.zeros((2, P_COLS + 2 * TILE), jnp.float32)
+    qrow[...] = jnp.zeros_like(qrow)
+    packet[...] = jnp.zeros_like(packet)
 
     all_but = frames.at[pl.ds(0, (n - 1) * P_ROWS)]
     pltpu.make_async_copy(all_but, all_but, ag_recv.at[0]).wait()
@@ -549,7 +430,7 @@
                 target(part, inner, plain, news[part], j)
             return carry
 
-        lax.fori_loop(0, C_COLS // CHUNK, chunk, 0)
+        lax.fori_loop(0, C_COLS // CHUNK, chunk, 0, unroll=COAST_UNROLL)
 
     def add_sums(which, nested, part, value, j):
         row = (nested * 3 + part) * 4 + j // 2
@@ -569,9 +450,29 @@
         halo_start(1, nested)
         return carry
 
-    for index in (7, 8, 9):
-        loads[index].wait()
+    loads[7].wait()
     lax.fori_loop(0, NCHILD, stage_a, 0)
+
+    @pl.when(me < ROW_UNITS)
+    def _():
+        whole = gathered.at[pl.ds(EDGE, ocean_rows)]
+        pltpu.make_async_copy(whole, whole, t_recv.at[0]).wait()
+        first = grid_first(lax.rem(me // PARTS, NCHILD))
+        picked[...] = gathered[pl.ds(EDGE + first, FOOT_ROWS)]
+        every(lambda other: picked.at[other], rowbuf.at[me], t_send.at[2], t_recv.at[2])
+        pltpu.make_async_copy(picked.at[me], rowbuf.at[me], t_recv.at[2]).start()
+
+        beside[0:1] = gathered[pl.ds(EDGE + first - 1, 1)]
+        beside[1:2] = gathered[pl.ds(EDGE + first + FOOT_ROWS, 1)]
+        for side, target in ((0, 0), (1, n - 1)):
+
+            @pl.when(me != target)
+            def _():
+                remote(beside.at[side], besides.at[me], t_send.at[1], t_recv.at[1], target).start()
+
+            @pl.when(me == target)
+            def _():
+                pltpu.make_async_copy(beside.at[side], besides.at[me], t_recv.at[1]).start()
 
     def stage_b(nested, carry):
         halo_wait(1, nested)
@@ -601,6 +502,77 @@
 
     deal(BACK, BACK_FIRST, lambda unit: pairs.at[unit], returned.at[pad + me], t_send.at[3], t_recv.at[3])
 
+    loads[0].wait()
+    loads[4].wait()
+    def ocean_lanes(j):
+        here = pl.multiple_of(j * CHUNK, CHUNK)
+        return pl.ds(here, CHUNK), pl.ds(here + TILE, CHUNK), pl.ds(here, CHUNK + 2 * TILE)
+
+    def ocean_edge(side, field, plain):
+        return jnp.where(has_before if side == 0 else has_after, ocean_halo[side, field, :, plain], 0.0)
+
+    def put8(array, part, inner, own, field, plain):
+        array[part, 1:5, inner] = own
+        if field is not None:
+            array[part, 0:1, inner] = ocean_edge(0, field, plain)
+            array[part, 5:6, inner] = ocean_edge(1, field, plain)
+
+    chunks = P_COLS // CHUNK
+    ocean_wait(0)
+
+    def assemble(j, carry):
+        plain, inner, wide = ocean_lanes(j)
+        for part in range(3):
+            put8(now8, part, inner, p_now[part, :, plain], part, plain)
+        depth8[1:5, inner] = p_depth[:, plain]
+        depth8[0:1, inner] = ocean_edge(0, 3, plain)
+        depth8[5:6, inner] = ocean_edge(1, 3, plain)
+        return carry
+
+    lax.fori_loop(0, chunks, assemble, 0, unroll=OCEAN_UNROLL)
+
+    def turn(field):
+        return pltpu.roll(field, 7, 0), pltpu.roll(field, 1, 0)
+
+    def ocean_rates(state, j):
+        plain, inner, wide = ocean_lanes(j)
+        shifted = []
+        for part in range(3):
+            block = state[part, :, wide]
+            middle = block[:, TILE : TILE + CHUNK]
+            shifted.append((middle,) + column_shifts(block, CHUNK) + turn(middle))
+        return rates(shifted, depth8[:, inner])
+
+    def ocean_first(j, carry):
+        plain, inner, wide = ocean_lanes(j)
+        changes, found = ocean_rates(now8, j)
+        for index, slope in enumerate(found):
+            pslopes[index, :, plain] = slope
+        for part in range(3):
+            second8[part, 1:5, inner] = p_old[part, :, plain] - changes[part][1:5]
+        return carry
+
+    lax.fori_loop(0, chunks, ocean_first, 0, unroll=OCEAN_UNROLL)
+
+    for nested in range(NCHILD):
+        def first_product(q):
+            tile = slice(TILE * q, TILE * (q + 1))
+            return second8[2, 1:5, TILE * (q + 1) : TILE * (q + 2)] * p_end[1, :, tile]
+
+        def second_product(q):
+            tile = slice(TILE * q, TILE * (q + 1))
+            v_2 = second8[2, 1:5, TILE * (q + 1) : TILE * (q + 2)]
+            return p_depth[:, tile] * p_end[0, :, tile] + v_2 * p_end[2, :, tile]
+
+        value = band_tiles(nested, (first_product, second_product))
+        for which in range(2):
+            for piece in range(PARTS):
+                unit = (which * NCHILD + nested) * PARTS + piece
+                for row in range(P_ROWS):
+                    at = which * P_ROWS + row
+                    side_win[unit, row] = value[at : at + 1, (piece + 1) * TILE : (piece + 2) * TILE]
+    deal(SIDE_UNITS, SIDE_FIRST, lambda unit: side_win.at[unit], side_gathered.at[mine], t_send.at[5], t_recv.at[5])
+
     @pl.when(me >= SIDE_FIRST)
     def _():
         whole = side_gathered.at[pl.ds(EDGE, ocean_rows)]
@@ -624,9 +596,9 @@
         for nested in range(NCHILD):
             for part in range(3):
                 for piece in range(PARTS):
-                    unit = ((3 * which + part) * NCHILD + nested) * PARTS + piece
+                    unit = (part * NCHILD + nested) * PARTS + piece
                     row = (nested * 3 + part) * PARTS + piece
-                    lhs[which, row : row + 1, :] = rowbuf[unit]
+                    lhs[which, row : row + 1, :] = rowbuf[unit, which : which + 1, :]
     spread[0] = exact_dot(lhs[0], spread_matrix)
 
     def spread_at(which, nested, part, j):
@@ -647,10 +619,11 @@
                 put_row(2, nested, part, plain, scaled[-1])
             return inner_carry
 
-        lax.fori_loop(0, C_COLS // CHUNK, chunk, 0)
+        lax.fori_loop(0, C_COLS // CHUNK, chunk, 0, unroll=COAST_UNROLL)
         halo_start(2, nested)
         return carry
 
+    loads[8].wait()
     lax.fori_loop(0, NCHILD, stage_c, 0)
 
     @pl.when((me == 0) | (me == n - 1))
@@ -662,7 +635,7 @@
 
             def line(array, field):
                 unit = (field * NCHILD + nested) * PARTS
-                return HALF * jnp.concatenate([array[unit + piece] for piece in range(PARTS)], axis=1)
+                return HALF * jnp.concatenate([array[unit + piece, 0:1, :] for piece in range(PARTS)], axis=1)
 
             ce, cv = line(besides, 0), line(besides, 2)
             e_q, v_q = [
@@ -701,9 +674,8 @@
                 lhs[1, row : row + 1, :] += qrow[nested, part : part + 1, TILE * q : TILE * (q + 1)]
     spread[1] = exact_dot(lhs[1], spread_matrix)
 
-    def adjoint(stage, nested, state, cots, slopes, target, beside_it):
+    def adjoint(stage, nested, state, cots, slopes, target):
         def chunk(j, carry):
-            beside_it(nested * (C_COLS // CHUNK) + j)
             here = pl.multiple_of(j * CHUNK, CHUNK)
             wide = pl.ds(here, CHUNK + 2 * TILE)
             plain = pl.ds(here, CHUNK)
@@ -727,7 +699,7 @@
             target(inner, plain, j, grads)
             return carry
 
-        lax.fori_loop(0, C_COLS // CHUNK, chunk, 0)
+        lax.fori_loop(0, C_COLS // CHUNK, chunk, 0, unroll=COAST_UNROLL)
 
     def frame_cots(nested, state, cots, first):
         for side in range(2):
@@ -745,44 +717,18 @@
                     lane == nested * 16 + side * 8 + first + part, column, packet[...]
                 )
 
-    steps = NCHILD * (C_COLS // CHUNK)
-    each = -(-n // steps)
-
-    @pl.when(me >= BACK_FIRST)
+    @pl.when((me >= BACK_FIRST) & (me < BACK_FIRST + BACK))
     def _():
         all_back = returned.at[pl.ds(pad, span)]
         pltpu.make_async_copy(all_back, all_back, t_recv.at[3]).wait()
         first = grid_first((me - BACK_FIRST) // (3 * PARTS))
         placed[...] = returned[pl.ds(pad - first, ocean_rows)]
-        pltpu.make_async_copy(
-            placed.at[pl.ds(me * P_ROWS, P_ROWS)], back.at[me - BACK_FIRST], t_recv.at[4]
-        ).start()
-
-    def some_placed(it):
-        @pl.when(me >= BACK_FIRST)
-        def _():
-            for index in range(each):
-                j = it * each + index
-
-                @pl.when((j > 0) & (j < n))
-                def _():
-                    target = lax.rem(me + j, n)
-                    remote(
-                        placed.at[pl.ds(target * P_ROWS, P_ROWS)],
-                        back.at[me - BACK_FIRST],
-                        t_send.at[4],
-                        t_recv.at[4],
-                        target,
-                    ).start()
-
-    def some_edges(it):
-        for index in range(each):
-            j = it * each + index
-
-            @pl.when((j > 0) & (j < n))
-            def _():
-                target = lax.rem(me + j, n)
-                remote(packet, edges.at[me], ag_send.at[1], ag_recv.at[1], target).start()
+
+        def rows_for(other):
+            return placed.at[pl.ds(other * P_ROWS, P_ROWS)]
+
+        every(rows_for, back.at[me - BACK_FIRST], t_send.at[4], t_recv.at[4])
+        pltpu.make_async_copy(rows_for(me), back.at[me - BACK_FIRST], t_recv.at[4]).start()
 
     def stage_d(nested, carry):
         halo_wait(2, nested)
@@ -796,17 +742,19 @@
                 a1[nested, part, :, inner] = scaled[-1]
                 put_row(3, nested, part, plain, scaled[-1])
 
-        adjoint(2, nested, nxt, a2, slopes2, target, some_placed)
+        adjoint(2, nested, nxt, a2, slopes2, target)
         halo_start(3, nested)
         frame_cots(nested, nxt, a2, 0)
         frame_cots(nested, now, a1, 3)
         return carry
 
+    loads[9].wait()
     lax.fori_loop(0, NCHILD, stage_d, 0)
     store_gold = pltpu.make_async_copy(mid, gold_out, store_sem.at[1])
     store_gold.start()
 
     edges[me] = packet[...]
+    every(lambda other: packet, edges.at[me], ag_send.at[1], ag_recv.at[1])
 
     def stage_e(nested, carry):
         halo_wait(3, nested)
@@ -815,10 +763,8 @@
             for part in range(3):
                 end[nested, part, :, plain] = end[nested, part, :, plain] + grads[part]
 
-        adjoint(3, nested, now, a1, slopes1, target, some_edges)
-        return carry
-
-    lax.fori_loop(0, NCHILD // 2, stage_e, 0)
+        adjoint(3, nested, now, a1, slopes1, target)
+        return carry
 
     row4 = me * P_ROWS + lax.broadcasted_iota(jnp.int32, (P_ROWS, CHUNK), 0)
     column4 = lax.broadcasted_iota(jnp.int32, (P_ROWS, CHUNK), 1)
@@ -873,13 +819,12 @@
                 ocean_send[side, 7 + part, :, plain] = cot[row : row + 1]
         return carry
 
-    lax.fori_loop(0, chunks, ocean_second, 0)
+    lax.fori_loop(0, chunks, ocean_second, 0, unroll=OCEAN_UNROLL)
     ocean_start(1)
 
-    lax.fori_loop(NCHILD // 2, NCHILD, stage_e, 0)
-    store_gnow = pltpu.make_async_copy(end, gnow_out, store_sem.at[2])
-    store_gnow.start()
-
+    lax.fori_loop(0, NCHILD // 2, stage_e, 0)
+
+    loads[3].wait()
     ocean_wait(1)
 
     def ocean_edges(j, carry):
@@ -890,7 +835,7 @@
                 array[part, 5:6, inner] = ocean_edge(1, first + part, plain)
         return carry
 
-    lax.fori_loop(0, chunks, ocean_edges, 0)
+    lax.fori_loop(0, chunks, ocean_edges, 0, unroll=OCEAN_UNROLL)
 
     def ocean_dy(field, index):
         ahead, behind = turn(field)
@@ -916,10 +861,14 @@
                 ocean_send[side, 10 + part, :, plain] = cot[row : row + 1]
         return carry
 
-    lax.fori_loop(0, chunks, ocean_third, 0)
+    lax.fori_loop(0, chunks, ocean_third, 0, unroll=OCEAN_UNROLL)
     ocean_start(2)
     store_pend = pltpu.make_async_copy(pend, pend_out, store_sem.at[3])
     store_pend.start()
+
+    lax.fori_loop(NCHILD // 2, NCHILD, stage_e, 0)
+    store_gnow = pltpu.make_async_copy(end, gnow_out, store_sem.at[2])
+    store_gnow.start()
 
     all_edges = edges.at[pl.ds(0, n - 1)]
     pltpu.make_async_copy(all_edges, all_edges, ag_recv.at[1]).wait()
@@ -961,7 +910,7 @@
             a18[part, 5:6, inner] = HALF * (ocean_edge(1, 10 + part, plain) + extra[5:6])
         return carry
 
-    lax.fori_loop(0, chunks, ocean_fourth, 0)
+    lax.fori_loop(0, chunks, ocean_fourth, 0, unroll=OCEAN_UNROLL)
     store_pgold = pltpu.make_async_copy(pgold, pgold_out, store_sem.at[4])
     store_pgold.start()
 
@@ -974,7 +923,7 @@
             pgnow[part, :, plain] = kept + (grads[part] + beside_at(j, 1, part))[1:5]
         return carry
 
-    lax.fori_loop(0, chunks, ocean_last, 0)
+    lax.fori_loop(0, chunks, ocean_last, 0, unroll=OCEAN_UNROLL)
     store_pgnow = pltpu.make_async_copy(pgnow, pgnow_out, store_sem.at[5])
     store_pgnow.start()
     for store in (store_next, store_gold, store_gnow, store_pend, store_pgold, store_pgnow):
@@ -985,14 +934,12 @@
 
     def drain_halo(nested, carry):
         for stage in range(4):
-            for copy in halo_copies(stage, nested):
-                copy.wait_send()
+            drain_both(halo_copies(stage, nested))
         return carry
 
     lax.fori_loop(0, NCHILD, drain_halo, 0)
     for stage in range(3):
-        for copy in ocean_copies(*ocean_stages[stage]):
-            copy.wait_send()
+        drain_both(ocean_copies(*ocean_stages[stage]))
 
     def drain(count, first, like, send):
         own = (me >= first) & (me < first + count)
@@ -1017,7 +964,7 @@
 
     for target in (0, n - 1):
 
-        @pl.when((me != target) & (me < ROW_UNITS // 2))
+        @pl.when((me != target) & (me < ROW_UNITS))
         def _():
             one = beside.at[0]
             pltpu.make_async_copy(one, one, t_send.at[1]).wait()
@@ -1027,13 +974,13 @@
             one = side_picked.at[0]
             pltpu.make_async_copy(one, one, t_send.at[6]).wait()
 
-    @pl.when(me >= BACK_FIRST)
+    @pl.when((me >= BACK_FIRST) & (me < BACK_FIRST + BACK))
     def _():
         gone = placed.at[pl.ds(0, (n - 1) * P_ROWS)]
         pltpu.make_async_copy(gone, gone, t_send.at[4]).wait()
 
 
-def everything(n, child_rows, child_cols, strips, coast):
+def everything(n, child_rows, child_cols, win, frame, strips, coast):
     f32 = jnp.float32
     anywhere = pl.BlockSpec(memory_space=pl.ANY)
     smem = pl.BlockSpec(memory_space=pltpu.SMEM)
@@ -1058,18 +1005,18 @@
         (NCHILD, 2, 4, 1, C_COLS),
         (3, NCHILD, 2, 3, 1, C_COLS),
         (3, NCHILD, 2, 3, 1, C_COLS),
-        (ROW_UNITS, P_ROWS, 1, TILE),
+        (ROW_UNITS, P_ROWS, 2, TILE),
         (SIDE_UNITS, P_ROWS, 1, TILE),
         (P_ROWS, 1, TILE),
         (ocean_rows + 2 * EDGE, 1, TILE),
         (16, TILE),
+        (ocean_rows + 2 * EDGE, 2, TILE),
         (ocean_rows + 2 * EDGE, 1, TILE),
-        (ocean_rows + 2 * EDGE, 1, TILE),
-        (FOOT_ROWS, 1, TILE),
+        (FOOT_ROWS, 2, TILE),
+        (2, 2, TILE),
         (2, 1, TILE),
-        (2, 1, TILE),
-        (ROW_UNITS, 1, TILE),
-        (ROW_UNITS // 2, 1, TILE),
+        (ROW_UNITS, 2, TILE),
+        (ROW_UNITS, 2, TILE),
         (SIDE_UNITS, 1, TILE),
         (2, BACK, TILE),
         (2, BACK, RATIO * TILE),
@@ -1104,11 +1051,11 @@
     return pl.pallas_call(
         functools.partial(coastal_kernel, n),
         out_shape=[jax.ShapeDtypeStruct(grid_shape, f32)] * 3 + [jax.ShapeDtypeStruct(ocean_shape, f32)] * 3,
-        in_specs=[smem] * 2 + [anywhere] * 10,
+        in_specs=[smem] * 2 + [anywhere] * 12,
         out_specs=[anywhere] * 6,
         scratch_shapes=[pltpu.VMEM(shape, f32) for shape in shapes]
         + [
-            dma((10,)),
+            dma((12,)),
             dma((6,)),
             dma((4, NCHILD, 2)),
             dma((4, NCHILD, 2)),
@@ -1122,7 +1069,77 @@
         compiler_params=pltpu.CompilerParams(
             collective_id=0, has_side_effects=True, vmem_limit_bytes=56 * 1024 * 1024
         ),
-    )(child_rows, child_cols, *strips, *coast)
+    )(child_rows, child_cols, win, frame, *strips, *coast)
+
+
+def window_kernel(cols, *refs):
+    sources, (win, frame), held, sem = refs[:5], refs[5:7], refs[7:12], refs[12]
+    reach = FOOT_COLS + 2 * TILE
+    shifts, copies = [], []
+    for nested in range(NCHILD):
+        left = cols[nested]
+        start = pl.multiple_of(jnp.clip((left - 2) // TILE * TILE, 0, P_COLS - reach), TILE)
+        shifts.append(reach - (left - start))
+        for index, (source, target) in enumerate(zip(sources, held)):
+            lanes = pl.ds(start, reach)
+            part = source.at[:, lanes] if index == 2 else source.at[:, :, lanes]
+            copies.append(pltpu.make_async_copy(part, target.at[nested], sem.at[index, nested]))
+    for copy in copies:
+        copy.start()
+    for copy in copies:
+        copy.wait()
+    old, now, depth, mid, end = held
+    lane = lax.broadcasted_iota(jnp.int32, (P_ROWS, TILE), 1)
+    packet = jnp.zeros((P_ROWS, TILE), jnp.float32)
+    for nested in range(NCHILD):
+        fields = [end[nested, i] for i in range(3)] + [mid[nested, i] for i in range(3)]
+        fields += [now[nested, i] for i in range(3)] + [old[nested, i] for i in range(3)] + [depth[nested]]
+        blocks = []
+        for first in range(0, len(fields), 2):
+            pair = fields[first : first + 2]
+            both = pltpu.roll(jnp.concatenate(pair, axis=0), shifts[nested], 1)
+            blocks += [both[P_ROWS * i : P_ROWS * (i + 1)] for i in range(len(pair))]
+        for which in range(2):
+            for part in range(3):
+                for piece in range(PARTS):
+                    unit = (part * NCHILD + nested) * PARTS + piece
+                    lanes = slice(piece * TILE, (piece + 1) * TILE)
+                    for row in range(P_ROWS):
+                        win[unit, row, which : which + 1, :] = blocks[3 * which + part][row : row + 1, lanes]
+        first_ok = jnp.where(cols[nested] >= 2, 1.0, 0.0)
+        last_ok = jnp.where(cols[nested] + FOOT_COLS + 1 < P_COLS, 1.0, 0.0)
+        for side, lanes in enumerate(((reach - 2, reach - 1, 0), (FOOT_COLS - 1, FOOT_COLS, FOOT_COLS + 1))):
+            found = []
+            for part in range(3):
+                for which, at in enumerate(lanes):
+                    cell = blocks[6 + part][:, at : at + 1]
+                    if side == 0 and which == 0:
+                        cell = cell * first_ok
+                    if side == 1 and which == 2:
+                        cell = cell * last_ok
+                    found.append(cell)
+            found += [blocks[index][:, lanes[1] : lanes[1] + 1] for index in (9, 10, 11, 12, 0, 1, 2)]
+            for index, cell in enumerate(found):
+                packet = jnp.where(lane == 32 * nested + 16 * side + index, cell, packet)
+    for row in range(P_ROWS):
+        frame[row] = packet[row : row + 1]
+
+
+def windows(strips, child_cols):
+    f32 = jnp.float32
+    reach = FOOT_COLS + 2 * TILE
+    return pl.pallas_call(
+        window_kernel,
+        out_shape=[
+            jax.ShapeDtypeStruct((ROW_UNITS, P_ROWS, 2, TILE), f32),
+            jax.ShapeDtypeStruct((P_ROWS, 1, TILE), f32),
+        ],
+        in_specs=[pl.BlockSpec(memory_space=pltpu.SMEM)] + [pl.BlockSpec(memory_space=pl.ANY)] * 5,
+        out_specs=[pl.BlockSpec(memory_space=pltpu.VMEM)] * 2,
+        scratch_shapes=[pltpu.VMEM((NCHILD,) + strip.shape[:-1] + (reach,), f32) for strip in strips]
+        + [pltpu.SemaphoreType.DMA((5, NCHILD))],
+        compiler_params=pltpu.CompilerParams(vmem_limit_bytes=60 * 1024 * 1024),
+    )(child_cols, *strips)
 
 
 def bounce_kernel(*refs):
@@ -1179,7 +1196,8 @@
 ):
     strips = (parent_old, parent_now, parent_depth, parent_cot_mid, parent_cot_end)
     coast = (child_old, child_now, child_depth, child_cot_mid, child_cot_end)
-    results = bounce(everything(n, child_rows, child_cols, strips, coast))
+    win, frame = windows(strips, child_cols)
+    results = bounce(everything(n, child_rows, child_cols, win, frame, strips, coast))
     child_end, child_gold, child_gnow, parent_end, parent_gold, parent_gnow = results
     return (parent_end, child_end, parent_gold, parent_gnow, child_gold, child_gnow)
 

time: 87.1 us -> 74.4 us (0.85)
  the two profiles are of different devices: /device:TPU:0 before, /device:TPU:8 now
where the time goes in v4:
time: 74.4 us; the launch traced here: 74.2 us
  Pallas kernels  73.5 us (99%)
    pallas_call x1, Pallas kernels, everything(): pl.pallas_call(functools.partial(coastal_kernel, n), out_shape=[jax.Shape...  65 us
    pallas_call x1, Pallas kernels, bounce(): pl.pallas_call(bounce_kernel, out_shape=[jax.ShapeDtypeStruct(array.shape...  5.28 us
    pallas_call x1, Pallas kernels, windows(): pl.pallas_call(window_kernel, out_shape=[jax.ShapeDtypeStruct((ROW_UNITS,...  3.21 us

profile of v4, /device:TPU:8, one launch (start us, length us, event | category | flops | bytes accessed | tf_op | source)
XLA Modules:
  0.0 74.2 jit_solution(14523913033436709364)
XLA Ops:
  0.6 3.2 %shard_map.163 = (f32[48,4,2,128]{3,2,1,0:T(2,128)}, f32[4,1,128]{2,1,0:T(1,128)}) custom-call(s32[4]{0:T(128)} %cols_smem.1, f32[3,4,8192]{2,1,0:T(4,128)} %refs_0_.3, f32[3,4,8192]{2,1,0:T(4,128)} %refs_1_.3, f32[4,8192]{1,0:T(4,128)} %refs_2_.3, f32[3,4,8192]{2,1,0:T(4,128)} %refs_3_.3, f32[3,4,8192]{2,1,0:T(4,128)} %refs_4_.3), custom_call_target="tpu_custom_call" | custom-call | tf_op jit(solution)/shard_map/pallas_call | solution.py:1131
  3.8 65.0 %shard_map.164 = (f32[4,3,8,4096]{3,2,1,0:T(8,128)}, f32[4,3,8,4096]{3,2,1,0:T(8,128)}, f32[4,3,8,4096]{3,2,1,0:T(8,128)}, f32[3,4,8192]{2,1,0:T(4,128)}, f32[3,4,8192]{2,1,0:T(4,128)}, /*index=5*/f32[3,4,8192]{2,1,0:T(4,128)}) custom-call(s32[4]{0:T(128)} %rows_smem.1, s32[4]{0:T(128)} %cols_smem.1, f32[48,4,2,128]{3,2,1,0:T(2,128)} %get-tuple-element.20.win_hbm, ...), custom_call_target="tpu_custom_call" | custom-call | tf_op jit(solution)/shard_map/pallas_call | solution.py:1051
  68.9 5.3 %shard_map.165 = (f32[4,3,8,4096]{3,2,1,0:T(8,128)}, f32[4,3,8,4096]{3,2,1,0:T(8,128)}, f32[4,3,8,4096]{3,2,1,0:T(8,128)}, f32[3,4,8192]{2,1,0:T(4,128)}, f32[3,4,8192]{2,1,0:T(4,128)}, /*index=5*/f32[3,4,8192]{2,1,0:T(4,128)}) custom-call(f32[4,3,8,4096]{3,2,1,0:T(8,128)} %get-tuple-element.22.refs_0_, f32[4,3,8,4096]{3,2,1,0:T(8,128)} %get-tuple-element.23.refs_1_, ...), custom_call_target="tpu_custom_call" | custom-call | tf_op jit(solution)/shard_map/pallas_call | solution.py:1171

commit v5 on v4

--- a/solution.py
+++ b/solution.py
@@ -250,19 +250,19 @@
         pl.when(has_before)(pair[0].wait_send)
         pl.when(has_after)(pair[1].wait_send)
 
-    def ocean_copies(first, count, stage):
-        fields = pl.ds(first, count)
+    def ocean_copies(first, count, stage, lanes=pl.ds(0, P_COLS)):
+        fields, all_rows = pl.ds(first, count), pl.ds(0, 1)
         return (
             remote(
-                ocean_send.at[0, fields],
-                ocean_halo.at[1, fields],
+                ocean_send.at[0, fields, all_rows, lanes],
+                ocean_halo.at[1, fields, all_rows, lanes],
                 ocean_send_sem.at[stage, 0],
                 ocean_recv_sem.at[stage, 1],
                 down,
             ),
             remote(
-                ocean_send.at[1, fields],
-                ocean_halo.at[0, fields],
+                ocean_send.at[1, fields, all_rows, lanes],
+                ocean_halo.at[0, fields, all_rows, lanes],
                 ocean_send_sem.at[stage, 1],
                 ocean_recv_sem.at[stage, 0],
                 up,
@@ -271,8 +271,9 @@
 
     ocean_stages = ((0, 4, 0), (4, 6, 1), (10, 3, 2))
 
-    def ocean_start(stage):
-        start_both(ocean_copies(*ocean_stages[stage]))
+    def ocean_start(stage, band):
+        lanes = pl.ds(pl.multiple_of(band * BAND, BAND), BAND)
+        start_both(ocean_copies(*ocean_stages[stage], lanes))
 
     def ocean_wait(stage):
         wait_both(ocean_copies(*ocean_stages[stage]))
@@ -326,7 +327,7 @@
             remote(source(other), target, send, recv, other).start()
             return carry
 
-        lax.fori_loop(1, n, one, 0)
+        lax.fori_loop(1, n, one, 0, unroll=4)
 
     def grid_first(grid_index):
         first = rows_smem[0]
@@ -345,14 +346,12 @@
         halo_start(0, nested)
 
     loads[10].wait()
-    deal(ROW_UNITS, 0, lambda unit: win.at[unit], gathered.at[mine], t_send.at[0], t_recv.at[0])
     loads[1].wait()
     loads[2].wait()
     for side, row in ((0, 0), (1, P_ROWS - 1)):
         for part in range(3):
             ocean_send[side, part] = p_now[part, row : row + 1, :]
         ocean_send[side, 3] = p_depth[row : row + 1, :]
-    ocean_start(0)
 
     for array in (a2, a1):
         array[:, :, :, 0:TILE] = jnp.zeros((NCHILD, 3, C_ROWS, TILE), jnp.float32)
@@ -453,27 +452,9 @@
     loads[7].wait()
     lax.fori_loop(0, NCHILD, stage_a, 0)
 
-    @pl.when(me < ROW_UNITS)
-    def _():
-        whole = gathered.at[pl.ds(EDGE, ocean_rows)]
-        pltpu.make_async_copy(whole, whole, t_recv.at[0]).wait()
-        first = grid_first(lax.rem(me // PARTS, NCHILD))
-        picked[...] = gathered[pl.ds(EDGE + first, FOOT_ROWS)]
-        every(lambda other: picked.at[other], rowbuf.at[me], t_send.at[2], t_recv.at[2])
-        pltpu.make_async_copy(picked.at[me], rowbuf.at[me], t_recv.at[2]).start()
-
-        beside[0:1] = gathered[pl.ds(EDGE + first - 1, 1)]
-        beside[1:2] = gathered[pl.ds(EDGE + first + FOOT_ROWS, 1)]
-        for side, target in ((0, 0), (1, n - 1)):
-
-            @pl.when(me != target)
-            def _():
-                remote(beside.at[side], besides.at[me], t_send.at[1], t_recv.at[1], target).start()
-
-            @pl.when(me == target)
-            def _():
-                pltpu.make_async_copy(beside.at[side], besides.at[me], t_recv.at[1]).start()
-
+    deal(ROW_UNITS, 0, lambda unit: win.at[unit], gathered.at[mine], t_send.at[0], t_recv.at[0])
+    for band in range(P_COLS // BAND):
+        ocean_start(0, band)
     def stage_b(nested, carry):
         halo_wait(1, nested)
 
@@ -502,6 +483,27 @@
 
     deal(BACK, BACK_FIRST, lambda unit: pairs.at[unit], returned.at[pad + me], t_send.at[3], t_recv.at[3])
 
+    @pl.when(me < ROW_UNITS)
+    def _():
+        whole = gathered.at[pl.ds(EDGE, ocean_rows)]
+        pltpu.make_async_copy(whole, whole, t_recv.at[0]).wait()
+        first = grid_first(lax.rem(me // PARTS, NCHILD))
+        picked[...] = gathered[pl.ds(EDGE + first, FOOT_ROWS)]
+        every(lambda other: picked.at[other], rowbuf.at[me], t_send.at[2], t_recv.at[2])
+        pltpu.make_async_copy(picked.at[me], rowbuf.at[me], t_recv.at[2]).start()
+
+        beside[0:1] = gathered[pl.ds(EDGE + first - 1, 1)]
+        beside[1:2] = gathered[pl.ds(EDGE + first + FOOT_ROWS, 1)]
+        for side, target in ((0, 0), (1, n - 1)):
+
+            @pl.when(me != target)
+            def _():
+                remote(beside.at[side], besides.at[me], t_send.at[1], t_recv.at[1], target).start()
+
+            @pl.when(me == target)
+            def _():
+                pltpu.make_async_copy(beside.at[side], besides.at[me], t_recv.at[1]).start()
+
     loads[0].wait()
     loads[4].wait()
     def ocean_lanes(j):
@@ -590,6 +592,19 @@
             @pl.when(me == target)
             def _():
                 pltpu.make_async_copy(side_picked.at[side], place, t_recv.at[6]).start()
+
+    @pl.when((me >= BACK_FIRST) & (me < BACK_FIRST + BACK))
+    def _():
+        all_back = returned.at[pl.ds(pad, span)]
+        pltpu.make_async_copy(all_back, all_back, t_recv.at[3]).wait()
+        first = grid_first((me - BACK_FIRST) // (3 * PARTS))
+        placed[...] = returned[pl.ds(pad - first, ocean_rows)]
+
+        def rows_for(other):
+            return placed.at[pl.ds(other * P_ROWS, P_ROWS)]
+
+        every(rows_for, back.at[me - BACK_FIRST], t_send.at[4], t_recv.at[4])
+        pltpu.make_async_copy(rows_for(me), back.at[me - BACK_FIRST], t_recv.at[4]).start()
 
     pltpu.make_async_copy(rowbuf, rowbuf, t_recv.at[2]).wait()
     for which in range(2):
@@ -717,19 +732,6 @@
                     lane == nested * 16 + side * 8 + first + part, column, packet[...]
                 )
 
-    @pl.when((me >= BACK_FIRST) & (me < BACK_FIRST + BACK))
-    def _():
-        all_back = returned.at[pl.ds(pad, span)]
-        pltpu.make_async_copy(all_back, all_back, t_recv.at[3]).wait()
-        first = grid_first((me - BACK_FIRST) // (3 * PARTS))
-        placed[...] = returned[pl.ds(pad - first, ocean_rows)]
-
-        def rows_for(other):
-            return placed.at[pl.ds(other * P_ROWS, P_ROWS)]
-
-        every(rows_for, back.at[me - BACK_FIRST], t_send.at[4], t_recv.at[4])
-        pltpu.make_async_copy(rows_for(me), back.at[me - BACK_FIRST], t_recv.at[4]).start()
-
     def stage_d(nested, carry):
         halo_wait(2, nested)
 
@@ -754,7 +756,6 @@
     store_gold.start()
 
     edges[me] = packet[...]
-    every(lambda other: packet, edges.at[me], ag_send.at[1], ag_recv.at[1])
 
     def stage_e(nested, carry):
         halo_wait(3, nested)
@@ -819,10 +820,16 @@
                 ocean_send[side, 7 + part, :, plain] = cot[row : row + 1]
         return carry
 
-    lax.fori_loop(0, chunks, ocean_second, 0, unroll=OCEAN_UNROLL)
-    ocean_start(1)
+    def ocean_second_band(band, carry):
+        per = BAND // CHUNK
+        lax.fori_loop(0, per, lambda j, inner: ocean_second(band * per + j, inner), 0, unroll=OCEAN_UNROLL)
+        ocean_start(1, band)
+        return carry
+
+    lax.fori_loop(0, P_COLS // BAND, ocean_second_band, 0)
 
     lax.fori_loop(0, NCHILD // 2, stage_e, 0)
+    every(lambda other: packet, edges.at[me], ag_send.at[1], ag_recv.at[1])
 
     loads[3].wait()
     ocean_wait(1)
@@ -861,8 +868,13 @@
                 ocean_send[side, 10 + part, :, plain] = cot[row : row + 1]
         return carry
 
-    lax.fori_loop(0, chunks, ocean_third, 0, unroll=OCEAN_UNROLL)
-    ocean_start(2)
+    def ocean_third_band(band, carry):
+        per = BAND // CHUNK
+        lax.fori_loop(0, per, lambda j, inner: ocean_third(band * per + j, inner), 0, unroll=OCEAN_UNROLL)
+        ocean_start(2, band)
+        return carry
+
+    lax.fori_loop(0, P_COLS // BAND, ocean_third_band, 0)
     store_pend = pltpu.make_async_copy(pend, pend_out, store_sem.at[3])
     store_pend.start()
 

time: 74.4 us -> 72.2 us (0.970)
  the two profiles are of different devices: /device:TPU:8 before, /device:TPU:16 now
where the time goes in v5:
time: 72.2 us; the launch traced here: 72 us
  Pallas kernels  71.3 us (99%)
    pallas_call x1, Pallas kernels, everything(): pl.pallas_call(functools.partial(coastal_kernel, n), out_shape=[jax.Shape...  62.9 us
    pallas_call x1, Pallas kernels, bounce(): pl.pallas_call(bounce_kernel, out_shape=[jax.ShapeDtypeStruct(array.shape...  5.28 us
    pallas_call x1, Pallas kernels, windows(): pl.pallas_call(window_kernel, out_shape=[jax.ShapeDtypeStruct((ROW_UNITS,...  3.21 us

profile of v5, /device:TPU:16, one launch (start us, length us, event | category | flops | bytes accessed | tf_op | source)
XLA Modules:
  0.0 72.0 jit_solution(14252107890585019530)
XLA Ops:
  0.6 3.2 %shard_map.163 = (f32[48,4,2,128]{3,2,1,0:T(2,128)}, f32[4,1,128]{2,1,0:T(1,128)}) custom-call(s32[4]{0:T(128)} %cols_smem.1, f32[3,4,8192]{2,1,0:T(4,128)} %refs_0_.3, f32[3,4,8192]{2,1,0:T(4,128)} %refs_1_.3, f32[4,8192]{1,0:T(4,128)} %refs_2_.3, f32[3,4,8192]{2,1,0:T(4,128)} %refs_3_.3, f32[3,4,8192]{2,1,0:T(4,128)} %refs_4_.3), custom_call_target="tpu_custom_call" | custom-call | tf_op jit(solution)/shard_map/pallas_call | solution.py:1143
  3.8 62.9 %shard_map.164 = (f32[4,3,8,4096]{3,2,1,0:T(8,128)}, f32[4,3,8,4096]{3,2,1,0:T(8,128)}, f32[4,3,8,4096]{3,2,1,0:T(8,128)}, f32[3,4,8192]{2,1,0:T(4,128)}, f32[3,4,8192]{2,1,0:T(4,128)}, /*index=5*/f32[3,4,8192]{2,1,0:T(4,128)}) custom-call(s32[4]{0:T(128)} %rows_smem.1, s32[4]{0:T(128)} %cols_smem.1, f32[48,4,2,128]{3,2,1,0:T(2,128)} %get-tuple-element.20.win_hbm, ...), custom_call_target="tpu_custom_call" | custom-call | tf_op jit(solution)/shard_map/pallas_call | solution.py:1063
  66.7 5.3 %shard_map.165 = (f32[4,3,8,4096]{3,2,1,0:T(8,128)}, f32[4,3,8,4096]{3,2,1,0:T(8,128)}, f32[4,3,8,4096]{3,2,1,0:T(8,128)}, f32[3,4,8192]{2,1,0:T(4,128)}, f32[3,4,8192]{2,1,0:T(4,128)}, /*index=5*/f32[3,4,8192]{2,1,0:T(4,128)}) custom-call(f32[4,3,8,4096]{3,2,1,0:T(8,128)} %get-tuple-element.22.refs_0_, f32[4,3,8,4096]{3,2,1,0:T(8,128)} %get-tuple-element.23.refs_1_, ...), custom_call_target="tpu_custom_call" | custom-call | tf_op jit(solution)/shard_map/pallas_call | solution.py:1183

commit v6 on v5

--- a/solution.py
+++ b/solution.py
@@ -1158,14 +1158,17 @@
     sources, targets, held, sems = refs[:6], refs[6:12], refs[12:18], refs[18]
     pieces = []
     for index in range(6):
-        for part in range(sources[index].shape[0]):
+        size = sources[index].shape[0]
+        count = 1
+        for place in range(count):
+            part = pl.ds(place * (size // count), size // count)
             pieces.append(
                 (
                     pltpu.make_async_copy(
-                        sources[index].at[part], held[index].at[part], sems.at[0, index, part]
+                        sources[index].at[part], held[index].at[part], sems.at[0, index, place]
                     ),
                     pltpu.make_async_copy(
-                        held[index].at[part], targets[index].at[part], sems.at[1, index, part]
+                        held[index].at[part], targets[index].at[part], sems.at[1, index, place]
                     ),
                 )
             )

time: 72.2 us -> 71.6 us (level)
  no operation moved by 1% of the time
where the time goes in v6:
time: 71.6 us; the launch traced here: 71.4 us
  Pallas kernels  70.7 us (99%)
    pallas_call x1, Pallas kernels, everything(): pl.pallas_call(functools.partial(coastal_kernel, n), out_shape=[jax.Shape...  62.9 us
    pallas_call x1, Pallas kernels, bounce(): pl.pallas_call(bounce_kernel, out_shape=[jax.ShapeDtypeStruct(array.shape...  4.68 us
    pallas_call x1, Pallas kernels, windows(): pl.pallas_call(window_kernel, out_shape=[jax.ShapeDtypeStruct((ROW_UNITS,...  3.21 us

profile of v6, /device:TPU:16, one launch (start us, length us, event | category | flops | bytes accessed | tf_op | source)
XLA Modules:
  0.0 71.4 jit_solution(15055843660704607539)
XLA Ops:
  0.6 3.2 %shard_map.163 = (f32[48,4,2,128]{3,2,1,0:T(2,128)}, f32[4,1,128]{2,1,0:T(1,128)}) custom-call(s32[4]{0:T(128)} %cols_smem.1, f32[3,4,8192]{2,1,0:T(4,128)} %refs_0_.3, f32[3,4,8192]{2,1,0:T(4,128)} %refs_1_.3, f32[4,8192]{1,0:T(4,128)} %refs_2_.3, f32[3,4,8192]{2,1,0:T(4,128)} %refs_3_.3, f32[3,4,8192]{2,1,0:T(4,128)} %refs_4_.3), custom_call_target="tpu_custom_call" | custom-call | tf_op jit(solution)/shard_map/pallas_call | solution.py:1143
  3.8 62.9 %shard_map.164 = (f32[4,3,8,4096]{3,2,1,0:T(8,128)}, f32[4,3,8,4096]{3,2,1,0:T(8,128)}, f32[4,3,8,4096]{3,2,1,0:T(8,128)}, f32[3,4,8192]{2,1,0:T(4,128)}, f32[3,4,8192]{2,1,0:T(4,128)}, /*index=5*/f32[3,4,8192]{2,1,0:T(4,128)}) custom-call(s32[4]{0:T(128)} %rows_smem.1, s32[4]{0:T(128)} %cols_smem.1, f32[48,4,2,128]{3,2,1,0:T(2,128)} %get-tuple-element.20.win_hbm, ...), custom_call_target="tpu_custom_call" | custom-call | tf_op jit(solution)/shard_map/pallas_call | solution.py:1063
  66.7 4.7 %shard_map.165 = (f32[4,3,8,4096]{3,2,1,0:T(8,128)}, f32[4,3,8,4096]{3,2,1,0:T(8,128)}, f32[4,3,8,4096]{3,2,1,0:T(8,128)}, f32[3,4,8192]{2,1,0:T(4,128)}, f32[3,4,8192]{2,1,0:T(4,128)}, /*index=5*/f32[3,4,8192]{2,1,0:T(4,128)}) custom-call(f32[4,3,8,4096]{3,2,1,0:T(8,128)} %get-tuple-element.22.refs_0_, f32[4,3,8,4096]{3,2,1,0:T(8,128)} %get-tuple-element.23.refs_1_, ...), custom_call_target="tpu_custom_call" | custom-call | tf_op jit(solution)/shard_map/pallas_call | solution.py:1186
